TPU v7x, 32 devices: a whole 2x2x4 slice. The times are simulated.
32 devices in a mesh: mesh: 8 (over z, x), vec: 4 (over y, core).
Axes of the slice: x: 2, y: 2, z: 4, core: 2. Of those that a mesh axis runs over, the one named last changes fastest.
Arguments:
- panel: float32 [65536, 128], P('mesh', 'vec'), may hold values from -6 to 6
- orient: int32 [65536], P('mesh'), may hold values from -1 to 1, as said below
- mass: float32 [65536], P('mesh'), may hold values from 0.5 to 2
- stiff_diag: bfloat16 [512, 128, 128], P('mesh'), may hold values from -0.05 to 4, as said below
- near_coupling: bfloat16 [512, 128, 128], P('mesh'), may hold values from -0.1796875 to 0.1796875
- far_coupling: bfloat16 [512, 128, 128], P('mesh'), may hold values from -0.1796875 to 0.1796875
Outputs:
- filtered: float32 [65536, 128], P('mesh', 'vec')
- ritz_stiff: float32 [128, 128], P('vec', 'mesh')
- ritz_mass: float32 [128, 128], P('vec', 'mesh')
Inputs may be any that keep to these rules, and one draw needn't show every extreme that they name: `orient`: every entry is +1 or -1. `stiff_diag`: each block is symmetric; its diagonal entries lie from 2 to 4 and its off-diagonal entries have magnitude at most 0.05.
All inputs are finite; a program needn't handle non-finite values.
Results may differ from a plain program's by a relative error of at most 0.0035.
Values may be sent and summed in bfloat16 or wider, within the bound.
No kernel may reach another device: no remote copies, remote signals or barrier semaphores. Data moves between devices by JAX's collectives and lax.ppermute only.
A program may use at most 64 MiB of HBM per device.

v0:
```python
import jax
import jax.numpy as jnp
from jax import lax
from jax.sharding import PartitionSpec as P

SPAN = 32
DEGREE = 4
APPS = 2


filter_center = 6.0
filter_radius = 8.0


def passed_along(x, axis, by):
    size = lax.axis_size(axis)
    pairs = [(i, i + by) for i in range(size) if 0 <= i + by < size]
    return lax.ppermute(x, axis, pairs)


def extended_2(x, sides, width):
    for axis, dim in sides:
        size, length = (lax.axis_size(axis), x.shape[dim])
        up = [(i, (i + 1) % size) for i in range(size - 1)]
        down = [(j, i) for i, j in up]
        last = lax.slice_in_dim(x, length - width, length, axis=dim)
        initial = lax.slice_in_dim(x, 0, width, axis=dim)
        before = lax.ppermute(last, axis, up)
        after = lax.ppermute(initial, axis, down)
        x = jnp.concatenate([before, x, after], axis=dim)
    return x


def blockmul(matrix, values):
    return lax.dot_general(
        matrix, values, (((2,), (1,)), ((0,), (0,))), preferred_element_type=jnp.float32
    )


def blockmul_turned(matrix, values):
    return lax.dot_general(
        matrix, values, (((1,), (1,)), ((0,), (0,))), preferred_element_type=jnp.float32
    )


def contract_rows(left, right):
    return lax.dot_general(
        left, right, (((0,), (0,)), ((), ())), preferred_element_type=jnp.float32
    )


def shards(panel, orient, mass, stiff_diag, near_coupling, far_coupling):
    rows, columns = panel.shape
    blocks = stiff_diag.shape[0]
    width = stiff_diag.shape[1]
    span = SPAN
    scale = orient.astype(jnp.float32) * lax.rsqrt(mass)
    leading = jnp.concatenate([near_coupling[0:1], far_coupling[0:span]], axis=0)
    following = passed_along(leading, "mesh", -1)
    near_after = jnp.concatenate([near_coupling[1:], following[0:1]], axis=0)
    far_after = jnp.concatenate([far_coupling[span:], following[1:]], axis=0)

    def operate(field):
        scaled = (scale[:, None] * field).astype(jnp.bfloat16).reshape(blocks, width, columns)
        total = blockmul(stiff_diag, scaled)
        extended = extended_2(scaled, (("mesh", 0),), span)
        total = total + blockmul(near_coupling, extended[span - 1 : span - 1 + blocks])
        total = total + blockmul(far_coupling, extended[0:blocks])
        total = total + blockmul_turned(near_after, extended[span + 1 : span + 1 + blocks])
        total = total + blockmul_turned(far_after, extended[2 * span : 2 * span + blocks])
        return scale[:, None] * total.reshape(rows, columns)

    filtered = panel
    for application in range(APPS):
        before = filtered
        current = (operate(filtered) - filter_center * filtered) / filter_radius
        for step in range(DEGREE - 1):
            nextval = 2.0 * (operate(current) - filter_center * current) / filter_radius - before
            before, current = (current, nextval)
        filtered = current
    image = operate(filtered)
    filtered_b = filtered.astype(jnp.bfloat16)
    image_b = image.astype(jnp.bfloat16)
    gathered = (
        lax.all_gather(filtered_b, "vec", axis=1, tiled=True),
        lax.all_gather(image_b, "vec", axis=1, tiled=True),
    )
    partial_stiff = contract_rows(filtered_b, gathered[1])
    partial_mass = contract_rows(filtered_b, gathered[0])
    summed = (
        lax.psum_scatter(partial_stiff, "mesh", scatter_dimension=1, tiled=True),
        lax.psum_scatter(partial_mass, "mesh", scatter_dimension=1, tiled=True),
    )
    return (filtered, summed[0], summed[1])


def solution(mesh):
    placed = (
        P("mesh", "vec"),
        P("mesh"),
        P("mesh"),
        P("mesh", None, None),
        P("mesh", None, None),
        P("mesh", None, None),
    )
    return jax.shard_map(
        shards,
        mesh=mesh,
        in_specs=placed,
        out_specs=(P("mesh", "vec"), P("vec", "mesh"), P("vec", "mesh")),
        check_vma=False,
    )
```

profile of v0, /device:TPU:0, one launch (start us, length us, event | category | flops | bytes accessed | tf_op | source)
XLA Modules:
  0.0 389.5 jit_solution(11056659859652742226)
XLA Ops:
  11.0 5.5 %collective-permute-start = (bf16[32,128,32]{1,2,0:T(8,128)(2,1)S(1)}, bf16[32,128,32]{1,2,0:T(8,128)(2,1)S(1)}, u32[]{:S(2)}, u32[]{:S(2)}) collective-permute-start(bf16[32,128,32]{1,2,0:T(8,128)(2,1)S(1)} %bitcast.440), channel_id=1, source_target_pairs={{0,4},{4,8},{8,12},{12,16},{16,20},{20,24},{24,28},{1,5},{5,9},{9,... | collective-permute-start | bytes 786440 | tf_op jit(solution)/shard_map/ppermute | solution.py:28
  20.3 29.4 %collective-permute-done = bf16[32,128,32]{1,2,0:T(8,128)(2,1)S(1)} collective-permute-done((bf16[32,128,32]{1,2,0:T(8,128)(2,1)S(1)}, bf16[32,128,32]{1,2,0:T(8,128)(2,1)S(1)}, u32[]{:S(2)}, u32[]{:S(2)}) %collective-permute-start) | collective-permute-done | bytes 262176 | tf_op jit(solution)/shard_map/ppermute | solution.py:28
  55.5 5.0 %collective-permute-start.3 = (bf16[32,128,32]{1,2,0:T(8,128)(2,1)S(1)}, bf16[32,128,32]{1,2,0:T(8,128)(2,1)S(1)}, u32[]{:S(2)}, u32[]{:S(2)}) collective-permute-start(bf16[32,128,32]{1,2,0:T(8,128)(2,1)S(1)} %bitcast.441), channel_id=1, source_target_pairs={{0,4},{4,8},{8,12},{12,16},{16,20},{20,24},{24,28},{1,5},{5,9},{9,... | collective-permute-start | bytes 786440 | tf_op jit(solution)/shard_map/ppermute | solution.py:28
  61.8 9.1 %collective-permute-done.3 = bf16[32,128,32]{1,2,0:T(8,128)(2,1)S(1)} collective-permute-done((bf16[32,128,32]{1,2,0:T(8,128)(2,1)S(1)}, bf16[32,128,32]{1,2,0:T(8,128)(2,1)S(1)}, u32[]{:S(2)}, u32[]{:S(2)}) %collective-permute-start.3) | collective-permute-done | bytes 262176 | tf_op jit(solution)/shard_map/ppermute | solution.py:28
  76.7 5.2 %collective-permute-start.5 = (bf16[32,128,32]{1,2,0:T(8,128)(2,1)S(1)}, bf16[32,128,32]{1,2,0:T(8,128)(2,1)S(1)}, u32[]{:S(2)}, u32[]{:S(2)}) collective-permute-start(bf16[32,128,32]{1,2,0:T(8,128)(2,1)S(1)} %bitcast.442), channel_id=1, source_target_pairs={{0,4},{4,8},{8,12},{12,16},{16,20},{20,24},{24,28},{1,5},{5,9},{9,... | collective-permute-start | bytes 786440 | tf_op jit(solution)/shard_map/ppermute | solution.py:28
  83.1 8.9 %collective-permute-done.5 = bf16[32,128,32]{1,2,0:T(8,128)(2,1)S(1)} collective-permute-done((bf16[32,128,32]{1,2,0:T(8,128)(2,1)S(1)}, bf16[32,128,32]{1,2,0:T(8,128)(2,1)S(1)}, u32[]{:S(2)}, u32[]{:S(2)}) %collective-permute-start.5) | collective-permute-done | bytes 262176 | tf_op jit(solution)/shard_map/ppermute | solution.py:28
  98.1 5.0 %collective-permute-start.7 = (bf16[32,128,32]{1,2,0:T(8,128)(2,1)S(1)}, bf16[32,128,32]{1,2,0:T(8,128)(2,1)S(1)}, u32[]{:S(2)}, u32[]{:S(2)}) collective-permute-start(bf16[32,128,32]{1,2,0:T(8,128)(2,1)S(1)} %bitcast.443), channel_id=1, source_target_pairs={{0,4},{4,8},{8,12},{12,16},{16,20},{20,24},{24,28},{1,5},{5,9},{9,... | collective-permute-start | bytes 786440 | tf_op jit(solution)/shard_map/ppermute | solution.py:28
  104.3 9.1 %collective-permute-done.7 = bf16[32,128,32]{1,2,0:T(8,128)(2,1)S(1)} collective-permute-done((bf16[32,128,32]{1,2,0:T(8,128)(2,1)S(1)}, bf16[32,128,32]{1,2,0:T(8,128)(2,1)S(1)}, u32[]{:S(2)}, u32[]{:S(2)}) %collective-permute-start.7) | collective-permute-done | bytes 262176 | tf_op jit(solution)/shard_map/ppermute | solution.py:28
  119.6 5.0 %collective-permute-start.9 = (bf16[32,128,32]{1,2,0:T(8,128)(2,1)S(1)}, bf16[32,128,32]{1,2,0:T(8,128)(2,1)S(1)}, u32[]{:S(2)}, u32[]{:S(2)}) collective-permute-start(bf16[32,128,32]{1,2,0:T(8,128)(2,1)S(1)} %bitcast.444), channel_id=1, source_target_pairs={{0,4},{4,8},{8,12},{12,16},{16,20},{20,24},{24,28},{1,5},{5,9},{9,... | collective-permute-start | bytes 786440 | tf_op jit(solution)/shard_map/ppermute | solution.py:28
  125.8 9.1 %collective-permute-done.9 = bf16[32,128,32]{1,2,0:T(8,128)(2,1)S(1)} collective-permute-done((bf16[32,128,32]{1,2,0:T(8,128)(2,1)S(1)}, bf16[32,128,32]{1,2,0:T(8,128)(2,1)S(1)}, u32[]{:S(2)}, u32[]{:S(2)}) %collective-permute-start.9) | collective-permute-done | bytes 262176 | tf_op jit(solution)/shard_map/ppermute | solution.py:28
  139.3 1.5 collective-permute-start.12
  140.8 5.0 %collective-permute-start.11 = (bf16[32,128,32]{1,2,0:T(8,128)(2,1)S(1)}, bf16[32,128,32]{1,2,0:T(8,128)(2,1)S(1)}, u32[]{:S(2)}, u32[]{:S(2)}) collective-permute-start(bf16[32,128,32]{1,2,0:T(8,128)(2,1)S(1)} %bitcast.445), channel_id=1, source_target_pairs={{0,4},{4,8},{8,12},{12,16},{16,20},{20,24},{24,28},{1,5},{5,9},{9,... | collective-permute-start | bytes 786440 | tf_op jit(solution)/shard_map/ppermute | solution.py:28
  147.0 8.9 %collective-permute-done.11 = bf16[32,128,32]{1,2,0:T(8,128)(2,1)S(1)} collective-permute-done((bf16[32,128,32]{1,2,0:T(8,128)(2,1)S(1)}, bf16[32,128,32]{1,2,0:T(8,128)(2,1)S(1)}, u32[]{:S(2)}, u32[]{:S(2)}) %collective-permute-start.11) | collective-permute-done | bytes 262176 | tf_op jit(solution)/shard_map/ppermute | solution.py:28
  161.7 5.0 %collective-permute-start.13 = (bf16[32,128,32]{1,2,0:T(8,128)(2,1)S(1)}, bf16[32,128,32]{1,2,0:T(8,128)(2,1)S(1)}, u32[]{:S(2)}, u32[]{:S(2)}) collective-permute-start(bf16[32,128,32]{1,2,0:T(8,128)(2,1)S(1)} %bitcast.446), channel_id=1, source_target_pairs={{0,4},{4,8},{8,12},{12,16},{16,20},{20,24},{24,28},{1,5},{5,9},{9,... | collective-permute-start | bytes 786440 | tf_op jit(solution)/shard_map/ppermute | solution.py:28
  168.0 9.1 %collective-permute-done.13 = bf16[32,128,32]{1,2,0:T(8,128)(2,1)S(1)} collective-permute-done((bf16[32,128,32]{1,2,0:T(8,128)(2,1)S(1)}, bf16[32,128,32]{1,2,0:T(8,128)(2,1)S(1)}, u32[]{:S(2)}, u32[]{:S(2)}) %collective-permute-start.13) | collective-permute-done | bytes 262176 | tf_op jit(solution)/shard_map/ppermute | solution.py:28
  183.1 5.3 %collective-permute-start.15 = (bf16[32,128,32]{1,2,0:T(8,128)(2,1)S(1)}, bf16[32,128,32]{1,2,0:T(8,128)(2,1)S(1)}, u32[]{:S(2)}, u32[]{:S(2)}) collective-permute-start(bf16[32,128,32]{1,2,0:T(8,128)(2,1)S(1)} %bitcast.447), channel_id=1, source_target_pairs={{0,4},{4,8},{8,12},{12,16},{16,20},{20,24},{24,28},{1,5},{5,9},{9,... | collective-permute-start | bytes 786440 | tf_op jit(solution)/shard_map/ppermute | solution.py:28
  189.6 8.9 %collective-permute-done.15 = bf16[32,128,32]{1,2,0:T(8,128)(2,1)S(1)} collective-permute-done((bf16[32,128,32]{1,2,0:T(8,128)(2,1)S(1)}, bf16[32,128,32]{1,2,0:T(8,128)(2,1)S(1)}, u32[]{:S(2)}, u32[]{:S(2)}) %collective-permute-start.15) | collective-permute-done | bytes 262176 | tf_op jit(solution)/shard_map/ppermute | solution.py:28
  206.5 5.0 %collective-permute-start.17 = (bf16[32,128,32]{1,2,0:T(8,128)(2,1)S(1)}, bf16[32,128,32]{1,2,0:T(8,128)(2,1)S(1)}, u32[]{:S(2)}, u32[]{:S(2)}) collective-permute-start(bf16[32,128,32]{1,2,0:T(8,128)(2,1)S(1)} %bitcast.448), channel_id=1, source_target_pairs={{0,4},{4,8},{8,12},{12,16},{16,20},{20,24},{24,28},{1,5},{5,9},{9,... | collective-permute-start | bytes 786440 | tf_op jit(solution)/shard_map/ppermute | solution.py:28
  212.8 9.1 %collective-permute-done.17 = bf16[32,128,32]{1,2,0:T(8,128)(2,1)S(1)} collective-permute-done((bf16[32,128,32]{1,2,0:T(8,128)(2,1)S(1)}, bf16[32,128,32]{1,2,0:T(8,128)(2,1)S(1)}, u32[]{:S(2)}, u32[]{:S(2)}) %collective-permute-start.17) | collective-permute-done | bytes 262176 | tf_op jit(solution)/shard_map/ppermute | solution.py:28
  229.3 2.9 fusion.124
  232.3 20.9 %all-gather.3.cloned.1.call-done = bf16[8192,128]{0,1:T(8,128)(2,1)} async-done(((bf16[8192,32]{0,1:T(8,128)(2,1)}), bf16[8192,128]{0,1:T(8,128)(2,1)}) %all-gather.3.cloned.1.call-update) | async-done | bytes 2097168 | tf_op jit(solution)/shard_map/all_gather | solution.py:86
  253.2 2.9 fusion.123
  256.1 62.3 %reduce-scatter.5.cloned.1.call-done = f32[32,16]{0,1:T(8,128)} async-done(((f32[32,128]{0,1:T(8,128)}), f32[32,16]{0,1:T(8,128)}) %reduce-scatter.5.cloned.1.call-update) | async-done | bytes 2064 | tf_op jit(solution)/shard_map/reduce_scatter | solution.py:92
  318.4 64.1 %reduce-scatter.3.cloned.1.call-done = f32[32,16]{0,1:T(8,128)} async-done(((f32[32,128]{0,1:T(8,128)}), f32[32,16]{0,1:T(8,128)}) %reduce-scatter.3.cloned.1.call-update) | async-done | bytes 2064 | tf_op jit(solution)/shard_map/reduce_scatter | solution.py:91
  (174 shorter events, 71.9 us)
Async XLA Ops:
  7.2 221.9 %all-gather.5.cloned.1.call-start = ((), (), s32[]{:S(2)}) async-start(), calls=%async_computation.4 | async-start | bytes 2621440 | tf_op jit(solution)/shard_map/all_gather | solution.py:85
  9.7 40.3 %collective-permute-start.2 = (bf16[32,128,32]{1,2,0:T(8,128)(2,1)S(1)}, bf16[32,128,32]{1,2,0:T(8,128)(2,1)S(1)}, u32[]{:S(2)}, u32[]{:S(2)}) collective-permute-start(bf16[32,128,32]{1,2,0:T(8,128)(2,1)S(1)} %bitcast.431), channel_id=1, source_target_pairs={{4,0},{8,4},{12,8},{16,12},{20,16},{24,20},{28,24},{5,1},{9,5},{13... | collective-permute-start | bytes 786440 | tf_op jit(solution)/shard_map/ppermute | solution.py:29
  11.0 38.7 %collective-permute-start = (bf16[32,128,32]{1,2,0:T(8,128)(2,1)S(1)}, bf16[32,128,32]{1,2,0:T(8,128)(2,1)S(1)}, u32[]{:S(2)}, u32[]{:S(2)}) collective-permute-start(bf16[32,128,32]{1,2,0:T(8,128)(2,1)S(1)} %bitcast.440), channel_id=1, source_target_pairs={{0,4},{4,8},{8,12},{12,16},{16,20},{20,24},{24,28},{1,5},{5,9},{9,... | collective-permute-start | bytes 786440 | tf_op jit(solution)/shard_map/ppermute | solution.py:28
  16.8 181.9 %copy-start.12 = (bf16[32,128,128]{2,1,0:T(8,128)(2,1)}, bf16[32,128,128]{2,1,0:T(8,128)(2,1)S(1)}, u32[]{:S(2)}) copy-start(bf16[32,128,128]{2,1,0:T(8,128)(2,1)S(1)} %get-tuple-element.9) | copy-start | bytes 3145732
  17.4 33.8 %collective-permute-start.1 = (bf16[33,128,128]{2,1,0:T(8,128)(2,1)S(1)}, bf16[33,128,128]{2,1,0:T(8,128)(2,1)S(1)}, u32[]{:S(2)}, u32[]{:S(2)}) collective-permute-start(bf16[33,128,128]{2,1,0:T(8,128)(2,1)S(1)} %pad_maximum_fusion.2), channel_id=1, source_target_pairs={{4,0},{8,4},{12,8},{16,12},{20,16},{24,20},{28,24},{5,1},{9,5},{13... | collective-permute-start | bytes 3244040 | tf_op jit(solution)/shard_map/ppermute | solution.py:18
  54.2 16.8 %collective-permute-start.4 = (bf16[32,128,32]{1,2,0:T(8,128)(2,1)S(1)}, bf16[32,128,32]{1,2,0:T(8,128)(2,1)S(1)}, u32[]{:S(2)}, u32[]{:S(2)}) collective-permute-start(bf16[32,128,32]{1,2,0:T(8,128)(2,1)S(1)} %bitcast.432), channel_id=1, source_target_pairs={{4,0},{8,4},{12,8},{16,12},{20,16},{24,20},{28,24},{5,1},{9,5},{13... | collective-permute-start | bytes 786440 | tf_op jit(solution)/shard_map/ppermute | solution.py:29
  55.5 15.3 %collective-permute-start.3 = (bf16[32,128,32]{1,2,0:T(8,128)(2,1)S(1)}, bf16[32,128,32]{1,2,0:T(8,128)(2,1)S(1)}, u32[]{:S(2)}, u32[]{:S(2)}) collective-permute-start(bf16[32,128,32]{1,2,0:T(8,128)(2,1)S(1)} %bitcast.441), channel_id=1, source_target_pairs={{0,4},{4,8},{8,12},{12,16},{16,20},{20,24},{24,28},{1,5},{5,9},{9,... | collective-permute-start | bytes 786440 | tf_op jit(solution)/shard_map/ppermute | solution.py:28
  75.4 16.8 %collective-permute-start.6 = (bf16[32,128,32]{1,2,0:T(8,128)(2,1)S(1)}, bf16[32,128,32]{1,2,0:T(8,128)(2,1)S(1)}, u32[]{:S(2)}, u32[]{:S(2)}) collective-permute-start(bf16[32,128,32]{1,2,0:T(8,128)(2,1)S(1)} %bitcast.433), channel_id=1, source_target_pairs={{4,0},{8,4},{12,8},{16,12},{20,16},{24,20},{28,24},{5,1},{9,5},{13... | collective-permute-start | bytes 786440 | tf_op jit(solution)/shard_map/ppermute | solution.py:29
  76.7 15.3 %collective-permute-start.5 = (bf16[32,128,32]{1,2,0:T(8,128)(2,1)S(1)}, bf16[32,128,32]{1,2,0:T(8,128)(2,1)S(1)}, u32[]{:S(2)}, u32[]{:S(2)}) collective-permute-start(bf16[32,128,32]{1,2,0:T(8,128)(2,1)S(1)} %bitcast.442), channel_id=1, source_target_pairs={{0,4},{4,8},{8,12},{12,16},{16,20},{20,24},{24,28},{1,5},{5,9},{9,... | collective-permute-start | bytes 786440 | tf_op jit(solution)/shard_map/ppermute | solution.py:28
  96.8 16.8 %collective-permute-start.8 = (bf16[32,128,32]{1,2,0:T(8,128)(2,1)S(1)}, bf16[32,128,32]{1,2,0:T(8,128)(2,1)S(1)}, u32[]{:S(2)}, u32[]{:S(2)}) collective-permute-start(bf16[32,128,32]{1,2,0:T(8,128)(2,1)S(1)} %bitcast.434), channel_id=1, source_target_pairs={{4,0},{8,4},{12,8},{16,12},{20,16},{24,20},{28,24},{5,1},{9,5},{13... | collective-permute-start | bytes 786440 | tf_op jit(solution)/shard_map/ppermute | solution.py:29
  98.1 15.3 %collective-permute-start.7 = (bf16[32,128,32]{1,2,0:T(8,128)(2,1)S(1)}, bf16[32,128,32]{1,2,0:T(8,128)(2,1)S(1)}, u32[]{:S(2)}, u32[]{:S(2)}) collective-permute-start(bf16[32,128,32]{1,2,0:T(8,128)(2,1)S(1)} %bitcast.443), channel_id=1, source_target_pairs={{0,4},{4,8},{8,12},{12,16},{16,20},{20,24},{24,28},{1,5},{5,9},{9,... | collective-permute-start | bytes 786440 | tf_op jit(solution)/shard_map/ppermute | solution.py:28
  118.3 16.8 %collective-permute-start.10 = (bf16[32,128,32]{1,2,0:T(8,128)(2,1)S(1)}, bf16[32,128,32]{1,2,0:T(8,128)(2,1)S(1)}, u32[]{:S(2)}, u32[]{:S(2)}) collective-permute-start(bf16[32,128,32]{1,2,0:T(8,128)(2,1)S(1)} %bitcast.435), channel_id=1, source_target_pairs={{4,0},{8,4},{12,8},{16,12},{20,16},{24,20},{28,24},{5,1},{9,5},{13... | collective-permute-start | bytes 786440 | tf_op jit(solution)/shard_map/ppermute | solution.py:29
  119.6 15.3 %collective-permute-start.9 = (bf16[32,128,32]{1,2,0:T(8,128)(2,1)S(1)}, bf16[32,128,32]{1,2,0:T(8,128)(2,1)S(1)}, u32[]{:S(2)}, u32[]{:S(2)}) collective-permute-start(bf16[32,128,32]{1,2,0:T(8,128)(2,1)S(1)} %bitcast.444), channel_id=1, source_target_pairs={{0,4},{4,8},{8,12},{12,16},{16,20},{20,24},{24,28},{1,5},{5,9},{9,... | collective-permute-start | bytes 786440 | tf_op jit(solution)/shard_map/ppermute | solution.py:28
  139.3 16.8 %collective-permute-start.12 = (bf16[32,128,32]{1,2,0:T(8,128)(2,1)S(1)}, bf16[32,128,32]{1,2,0:T(8,128)(2,1)S(1)}, u32[]{:S(2)}, u32[]{:S(2)}) collective-permute-start(bf16[32,128,32]{1,2,0:T(8,128)(2,1)S(1)} %bitcast.436), channel_id=1, source_target_pairs={{4,0},{8,4},{12,8},{16,12},{20,16},{24,20},{28,24},{5,1},{9,5},{13... | collective-permute-start | bytes 786440 | tf_op jit(solution)/shard_map/ppermute | solution.py:29
  140.8 15.1 %collective-permute-start.11 = (bf16[32,128,32]{1,2,0:T(8,128)(2,1)S(1)}, bf16[32,128,32]{1,2,0:T(8,128)(2,1)S(1)}, u32[]{:S(2)}, u32[]{:S(2)}) collective-permute-start(bf16[32,128,32]{1,2,0:T(8,128)(2,1)S(1)} %bitcast.445), channel_id=1, source_target_pairs={{0,4},{4,8},{8,12},{12,16},{16,20},{20,24},{24,28},{1,5},{5,9},{9,... | collective-permute-start | bytes 786440 | tf_op jit(solution)/shard_map/ppermute | solution.py:28
  160.4 16.8 %collective-permute-start.14 = (bf16[32,128,32]{1,2,0:T(8,128)(2,1)S(1)}, bf16[32,128,32]{1,2,0:T(8,128)(2,1)S(1)}, u32[]{:S(2)}, u32[]{:S(2)}) collective-permute-start(bf16[32,128,32]{1,2,0:T(8,128)(2,1)S(1)} %bitcast.437), channel_id=1, source_target_pairs={{4,0},{8,4},{12,8},{16,12},{20,16},{24,20},{28,24},{5,1},{9,5},{13... | collective-permute-start | bytes 786440 | tf_op jit(solution)/shard_map/ppermute | solution.py:29
  161.7 15.3 %collective-permute-start.13 = (bf16[32,128,32]{1,2,0:T(8,128)(2,1)S(1)}, bf16[32,128,32]{1,2,0:T(8,128)(2,1)S(1)}, u32[]{:S(2)}, u32[]{:S(2)}) collective-permute-start(bf16[32,128,32]{1,2,0:T(8,128)(2,1)S(1)} %bitcast.446), channel_id=1, source_target_pairs={{0,4},{4,8},{8,12},{12,16},{16,20},{20,24},{24,28},{1,5},{5,9},{9,... | collective-permute-start | bytes 786440 | tf_op jit(solution)/shard_map/ppermute | solution.py:28
  181.8 16.8 %collective-permute-start.16 = (bf16[32,128,32]{1,2,0:T(8,128)(2,1)S(1)}, bf16[32,128,32]{1,2,0:T(8,128)(2,1)S(1)}, u32[]{:S(2)}, u32[]{:S(2)}) collective-permute-start(bf16[32,128,32]{1,2,0:T(8,128)(2,1)S(1)} %bitcast.438), channel_id=1, source_target_pairs={{4,0},{8,4},{12,8},{16,12},{20,16},{24,20},{28,24},{5,1},{9,5},{13... | collective-permute-start | bytes 786440 | tf_op jit(solution)/shard_map/ppermute | solution.py:29
  183.1 15.3 %collective-permute-start.15 = (bf16[32,128,32]{1,2,0:T(8,128)(2,1)S(1)}, bf16[32,128,32]{1,2,0:T(8,128)(2,1)S(1)}, u32[]{:S(2)}, u32[]{:S(2)}) collective-permute-start(bf16[32,128,32]{1,2,0:T(8,128)(2,1)S(1)} %bitcast.447), channel_id=1, source_target_pairs={{0,4},{4,8},{8,12},{12,16},{16,20},{20,24},{24,28},{1,5},{5,9},{9,... | collective-permute-start | bytes 786440 | tf_op jit(solution)/shard_map/ppermute | solution.py:28
  205.0 48.2 %all-gather.3.cloned.1.call-start = ((), (), s32[]{:S(2)}) async-start(), calls=%async_computation.2 | async-start | bytes 2621440 | tf_op jit(solution)/shard_map/all_gather | solution.py:86
  205.2 16.8 %collective-permute-start.18 = (bf16[32,128,32]{1,2,0:T(8,128)(2,1)S(1)}, bf16[32,128,32]{1,2,0:T(8,128)(2,1)S(1)}, u32[]{:S(2)}, u32[]{:S(2)}) collective-permute-start(bf16[32,128,32]{1,2,0:T(8,128)(2,1)S(1)} %bitcast.439), channel_id=1, source_target_pairs={{4,0},{8,4},{12,8},{16,12},{20,16},{24,20},{28,24},{5,1},{9,5},{13... | collective-permute-start | bytes 786440 | tf_op jit(solution)/shard_map/ppermute | solution.py:29
  206.5 15.3 %collective-permute-start.17 = (bf16[32,128,32]{1,2,0:T(8,128)(2,1)S(1)}, bf16[32,128,32]{1,2,0:T(8,128)(2,1)S(1)}, u32[]{:S(2)}, u32[]{:S(2)}) collective-permute-start(bf16[32,128,32]{1,2,0:T(8,128)(2,1)S(1)} %bitcast.448), channel_id=1, source_target_pairs={{0,4},{4,8},{8,12},{12,16},{16,20},{20,24},{24,28},{1,5},{5,9},{9,... | collective-permute-start | bytes 786440 | tf_op jit(solution)/shard_map/ppermute | solution.py:28
  229.0 89.4 %reduce-scatter.5.cloned.1.call-start = ((), (), s32[]{:S(2)}) async-start(), calls=%async_computation.5 | async-start | bytes 73728 | tf_op jit(solution)/shard_map/reduce_scatter | solution.py:92
  232.2 150.3 %reduce-scatter.3.cloned.1.call-start = ((), (), s32[]{:S(2)}) async-start(), calls=%async_computation.3 | async-start | bytes 73728 | tf_op jit(solution)/shard_map/reduce_scatter | solution.py:91
  (14 other events, 379.1 us)
Sparse Core Ops, SparseCore 0:
  205.1 23.8 all-gather.4
  230.6 22.5 all-gather.2
  257.1 61.2 reduce-scatter.4
  322.3 60.2 reduce-scatter.2
where the time goes:
time: 397 us; the launch traced here: 390 us
  waiting for transfers between devices  249 us (63%)
  starting transfers between devices  59.6 us (15%)
  matrix products  50.2 us (13%)
  between operations  15.1 us (4%)
  other arithmetic  7.93 us (2%)
  local copies, waits for them, and re-layouts  7.53 us (2%)
    ppermute x9, waiting for transfers between devices, extended_2(): before = lax.ppermute(last, axis, up)  102 us
    reduce_scatter x1, waiting for transfers between devices, shards(): lax.psum_scatter(partial_stiff, 'mesh', scatter_dimension=1, tiled=True)  64.1 us
    reduce_scatter x1, waiting for transfers between devices, shards(): lax.psum_scatter(partial_mass, 'mesh', scatter_dimension=1, tiled=True)  62.3 us
    ppermute x9, starting transfers between devices, extended_2(): before = lax.ppermute(last, axis, up)  46.2 us
    dot_general x27, matrix products, blockmul(): lax.dot_general(matrix, values, (((2,), (1,)), ((0,), (0,))), preferred_e...  32.5 us
    all_gather x1, waiting for transfers between devices, shards(): lax.all_gather(image_b, 'vec', axis=1, tiled=True)  20.9 us
    dot_general x18, matrix products, blockmul_turned(): lax.dot_general(matrix, values, (((1,), (1,)), ((0,), (0,))), preferred_e...  11.9 us
    ppermute x9, starting transfers between devices, extended_2(): after = lax.ppermute(initial, axis, down)  11.8 us
  transfers between devices with their start and end apart: 23, of which 12 were waited for; matrix products, arithmetic and copies ran while one was open for 6% of the time, Pallas kernels for 0%

commit v1 on v0

v1 whole, which is shorter than its diff:
```python
import functools

import jax
import jax.numpy as jnp
from jax import lax
from jax.experimental import pallas as pl
from jax.experimental.pallas import tpu as pltpu
from jax.sharding import PartitionSpec as P

SPAN = 32
DEGREE = 4
APPS = 2
CENTER = 6.0
RADIUS = 8.0

BOTH = ("mesh", "vec")
F32 = jnp.float32
BF16 = jnp.bfloat16
VMEM_LIMIT = 24 * 1024 * 1024


def gray(t):
    return t ^ (t >> 1)


class Plan:
    def __init__(self, meshes, vecs, blocks, width, columns):
        self.meshes, self.vecs, self.blocks, self.width, self.columns = meshes, vecs, blocks, width, columns
        self.ring = [(0, gray(t)) for t in range(vecs)] + [(1, gray(t)) for t in reversed(range(vecs))]
        self.segments = 2 * vecs
        self.seg = {place: s for s, place in enumerate(self.ring)}
        self.layers = meshes // 2
        self.own = blocks // SPAN
        self.rows = 2 * self.own
        self.run = SPAN // self.segments
        self.half = self.run // 2
        self.lanes = self.run * width
        self.vectors = vecs * columns
        self.inner, self.outer = {}, {}
        for i in range(self.rows):
            for p in range(self.run):
                self.inner["D", i, p] = len(self.inner)
        for i in range(self.rows):
            for p in range(1, self.run):
                self.inner["N", i, p] = len(self.inner)
        for i in range(1, self.rows):
            for p in range(self.run):
                self.inner["F", i, p] = len(self.inner)
        for p in range(self.run):
            self.outer["F", 0, p] = len(self.outer)
        for p in range(self.run):
            self.outer["F", self.rows, p] = len(self.outer)
        for i in range(self.rows):
            self.outer["N", i, 0] = len(self.outer)
            self.outer["N", i, self.run] = len(self.outer)
        for i in (0, self.rows - 1, self.rows):
            self.outer["N", i, self.half] = len(self.outer)
        self.n_first = self.run + 2
        self.n_rest = self.own * self.run + self.own * (self.run + 1) + (self.own - 1) * self.run

    def received(self, kind, r, p):
        if kind == "D":
            return 1, r * self.run + p
        if kind == "N":
            return 1, self.own * self.run + r * (self.run + 1) + p
        if r == 0:
            return 0, p
        return 1, self.own * self.run + self.own * (self.run + 1) + (r - 1) * self.run + p

    def swap(self, x, partner):
        pairs = []
        for m in range(self.meshes):
            for v in range(self.vecs):
                to, at = partner(m, v)
                pairs.append((m * self.vecs + v, to * self.vecs + at))
        return lax.ppermute(x, BOTH, pairs)

    def layer_a(self, m, v):
        to = m ^ 2
        return (to, v) if to < self.meshes else (m, v ^ 1)

    def layer_b(self, m, v):
        z = m // 2
        to = m + 2 if z % 2 else m - 2
        return (to, v) if 0 <= to < self.meshes else (m, v ^ 1)

    def ring_swap(self, m, v):
        s = self.seg[m % 2, v]
        x, at = self.ring[(s + 1) % self.segments if s % 2 else (s - 1) % self.segments]
        return m - m % 2 + x, at

    def core_swap(self, m, v):
        return m, v ^ 1


def place(plan):
    m, v = lax.axis_index("mesh"), lax.axis_index("vec")
    x, z = lax.rem(m, 2), lax.div(m, 2)
    s = jnp.int32(0)
    for k, (a, b) in enumerate(plan.ring):
        s = s + jnp.where((x == a) & (v == b), k, 0)
    return x, z, v, s


def column(plan, s, p):
    return lax.rem(plan.run * s + (p - plan.half + SPAN), SPAN)


def pieces(plan, s):
    found = []
    for p in range(plan.run):
        j = (plan.run * s + p - plan.half) % SPAN
        if found and found[-1][1] + found[-1][2] == j:
            found[-1][2] += 1
        else:
            found.append([p, j, 1])
    return found


def dot(u, w):
    return lax.dot_general(u, w, (((1,), (0,)), ((), ())), preferred_element_type=F32)


def dot_turned(u, w):
    return lax.dot_general(u, w, (((1,), (1,)), ((), ())), preferred_element_type=F32)


def call(kernel, outs, ins, args, scratch=(), flops=0, moved=0, aliases=None):
    return pl.pallas_call(
        kernel,
        out_shape=outs,
        in_specs=ins,
        out_specs=jax.tree.map(lambda _: pl.BlockSpec(memory_space=pltpu.VMEM), outs),
        scratch_shapes=list(scratch),
        compiler_params=pltpu.CompilerParams(vmem_limit_bytes=VMEM_LIMIT),
        cost_estimate=pl.CostEstimate(flops=flops, bytes_accessed=moved, transcendentals=0),
    )(*args)


def vm(n):
    return [pl.BlockSpec(memory_space=pltpu.VMEM)] * n


def anywhere(n):
    return [pl.BlockSpec(memory_space=pl.ANY)] * n


def shape(*dims, dtype=F32):
    return jax.ShapeDtypeStruct(dims, dtype)


def prepare_kernel(plan, panel, orient, mass, diag, near, far, scale, chunks, own, first, rest, parts, sems):
    x, z, v, s = place(plan)
    other = plan.segments - 1 - s
    copies = []

    def fetch(src, r, seg, p, dst):
        at = r * SPAN + column(plan, seg, p)
        copy = pltpu.make_async_copy(src.at[at], dst, sems.at[len(copies)])
        copy.start()
        copies.append(copy)

    for p in range(plan.run):
        fetch(far, 0, other, p, first.at[p])
    fetch(near, 0, other, plan.half, first.at[plan.run])
    for r in range(plan.own):
        for p in range(plan.run):
            fetch(diag, r, other, p, rest.at[plan.received("D", r, p)[1]])
        for p in range(plan.run + 1):
            fetch(near, r, other, p, rest.at[plan.received("N", r, p)[1]])
        if r > 0:
            for p in range(plan.run):
                fetch(far, r, other, p, rest.at[plan.received("F", r, p)[1]])
    for p in range(plan.run):
        fetch(far, 0, s, p, own.at[p])
    fetch(near, 0, s, plan.half, own.at[plan.run])

    scale[...] = orient[...].astype(F32) * lax.rsqrt(mass[...])
    parts[...] = jnp.zeros_like(parts)
    count = plan.own * plan.run
    for r in range(plan.own):
        for p in range(plan.run):
            value = scale[pl.ds(r * SPAN + column(plan, other, p), 1), :]
            for part in range(3):
                rounded = value.astype(BF16).astype(F32)
                parts[pl.ds(part * count + r * plan.run + p, 1), :] = rounded
                value = value - rounded
    first[plan.run + 1] = parts[...].astype(BF16)

    for d in range(plan.segments):
        seg = plan.seg[d // plan.vecs, d % plan.vecs]
        for r in range(plan.own):
            for p, j, n in pieces(plan, seg):
                lo = (r * SPAN + j) * plan.width
                chunks[d, r, :, p * plan.width : (p + n) * plan.width] = panel[:, lo : lo + n * plan.width]
    for copy in copies:
        copy.wait()


def prepare(plan, panel, orient, mass, diag, near, far):
    w = plan.width
    n_copies = plan.n_first - 1 + plan.n_rest + plan.run + 1
    return call(
        functools.partial(prepare_kernel, plan),
        (
            shape(plan.blocks, w),
            shape(plan.segments, plan.own, plan.columns, plan.lanes),
            shape(plan.run + 1, w, w, dtype=BF16),
            shape(plan.n_first, w, w, dtype=BF16),
            shape(plan.n_rest, w, w, dtype=BF16),
        ),
        vm(3) + anywhere(3),
        (panel, orient, mass, diag, near, far),
        [pltpu.VMEM((w, w), F32), pltpu.SemaphoreType.DMA((n_copies,))],
        moved=4 << 20,
    )


def emit(plan, i, u, even_layer, even_seg, u_out, send_a, send_b, send_core, send_ring):
    u_out[i] = u
    if i in (0, plan.rows - 1):
        at_even, at_odd = (send_b, send_a) if i == 0 else (send_a, send_b)

        @pl.when(even_layer)
        def _():
            at_even[...] = u

        @pl.when(jnp.logical_not(even_layer))
        def _():
            at_odd[...] = u

    left, right = u[:, : plan.width], u[:, plan.lanes - plan.width :]

    @pl.when(even_seg)
    def _():
        send_core[i] = right
        send_ring[i] = left

    @pl.when(jnp.logical_not(even_seg))
    def _():
        send_core[i] = left
        send_ring[i] = right


def sends(plan):
    w = plan.width
    edge = shape(plan.vectors, plan.lanes, dtype=BF16)
    side = shape(plan.rows, plan.vectors, w, dtype=BF16)
    return (shape(plan.rows, plan.vectors, plan.lanes, dtype=BF16), edge, edge, side, side)


def begin_kernel(plan, got, scale_own, first, y_out, scale_out, u_out, send_a, send_b, send_core, send_ring):
    x, z, v, s = place(plan)
    even_layer, even_seg = lax.rem(z, 2) == 0, lax.rem(s, 2) == 0
    count = plan.own * plan.run
    parts = first[plan.run + 1].astype(F32)
    theirs = (parts[:count] + parts[count : 2 * count]) + parts[2 * count : 3 * count]
    for i in range(plan.rows):
        half, r = divmod(i, plan.own)
        for p in range(plan.run):
            mine = scale_own[pl.ds(r * SPAN + column(plan, s, p), 1), :]
            scale_out[pl.ds(i * plan.run + p, 1), :] = jnp.where(
                x == half, mine, theirs[r * plan.run + p : r * plan.run + p + 1]
            )
    for i in range(plan.rows):
        half, r = divmod(i, plan.own)
        for v in range(plan.vecs):
            y_out[i, v * plan.columns : (v + 1) * plan.columns, :] = got[half * plan.vecs + v, r]
        u = []
        for p in range(plan.run):
            row = scale_out[pl.ds(i * plan.run + p, 1), :]
            u.append((row * y_out[i, :, p * plan.width : (p + 1) * plan.width]).astype(BF16))
        emit(plan, i, jnp.concatenate(u, axis=1), even_layer, even_seg, u_out, send_a, send_b, send_core, send_ring)


def begin(plan, got, scale_own, first):
    return call(
        functools.partial(begin_kernel, plan),
        (shape(plan.rows, plan.vectors, plan.lanes), shape(plan.rows * plan.run, plan.width)) + sends(plan),
        vm(3),
        (got, scale_own, first),
        moved=4 << 20,
    )


def weights_kernel(plan, diag, near, far, first, rest, below, inner, outer, sems):
    x, z, v, s = place(plan)
    local = {"D": diag, "N": near, "F": far}
    waits = []
    for table, out in ((plan.inner, inner), (plan.outer, outer)):
        for (kind, i, p), k in table.items():
            dst, sem = out.at[k], sems.at[len(waits)]
            if i == plan.rows:
                pltpu.make_async_copy(below.at[p if kind == "F" else plan.run], dst, sem).start()
            else:
                half, r = divmod(i, plan.own)
                which, index = plan.received(kind, r, p)
                there = (first, rest)[which].at[index]
                here = local[kind].at[r * SPAN + column(plan, s, p)]

                @pl.when(x == half)
                def _():
                    pltpu.make_async_copy(here, dst, sem).start()

                @pl.when(x != half)
                def _():
                    pltpu.make_async_copy(there, dst, sem).start()

            waits.append(pltpu.make_async_copy(first.at[0], dst, sem))
    for copy in waits:
        copy.wait()


def weights(plan, diag, near, far, first, rest, below):
    w = plan.width
    return call(
        functools.partial(weights_kernel, plan),
        (shape(len(plan.inner), w, w, dtype=BF16), shape(len(plan.outer), w, w, dtype=BF16)),
        anywhere(6),
        (diag, near, far, first, rest, below),
        [pltpu.SemaphoreType.DMA((len(plan.inner) + len(plan.outer),))],
        moved=4 << 20,
    )


def inner_kernel(plan, factors, has_before, gram, *refs):
    a, b, c = factors
    refs = list(refs)
    u, y = refs[:2]
    before = refs[2] if has_before else None
    w_in, scale, part = refs[2 + has_before : 5 + has_before]
    x, z, v, s = place(plan)
    wrap = (s == 0).astype(jnp.int32)
    width, half, last = plan.width, plan.half, plan.rows - 1
    at = plan.inner
    for i in range(plan.rows):
        for p in range(plan.run):
            lanes = slice(p * width, (p + 1) * width)
            total = dot(u[i, :, lanes], w_in[at["D", i, p]])
            if p == half:
                if i > 0:
                    total += dot_turned(u[i - wrap, :, (p - 1) * width : p * width], w_in[at["N", i, p]])
            elif p > 0:
                total += dot_turned(u[i, :, (p - 1) * width : p * width], w_in[at["N", i, p]])
            if p + 1 == half:
                if i < last:
                    near = at["N", i, half] + wrap * (plan.run - 1)
                    total += dot(u[i + wrap, :, (p + 1) * width : (p + 2) * width], w_in[near])
            elif p + 1 < plan.run:
                total += dot(u[i, :, (p + 1) * width : (p + 2) * width], w_in[at["N", i, p + 1]])
            if i > 0:
                total += dot_turned(u[i - 1, :, lanes], w_in[at["F", i, p]])
            if i < last:
                total += dot(u[i + 1, :, lanes], w_in[at["F", i + 1, p]])
            result = (a * scale[pl.ds(i * plan.run + p, 1), :]) * total
            if b:
                result += b * y[i, :, lanes]
            if has_before:
                result += c * before[i, :, lanes]
            part[i, :, lanes] = result
    if gram:
        mass = refs[5 + has_before]
        total = jnp.zeros(mass.shape, F32)
        for i in range(plan.rows):
            rounded = y[i].astype(BF16)
            total += dot_turned(rounded, rounded)
        mass[...] = total


def inner(plan, factors, u, y, before, w_in, scale, gram=False):
    has_before = before is not None
    args = (u, y) + ((before,) if has_before else ()) + (w_in, scale)
    outs = (shape(plan.rows, plan.vectors, plan.lanes),)
    if gram:
        outs += (shape(plan.vectors, plan.vectors),)
    return call(
        functools.partial(inner_kernel, plan, factors, has_before, gram),
        outs,
        vm(len(args)),
        args,
        flops=130 << 20,
        moved=5 << 20,
    )


def halo_terms(plan, u, w_out, got_a, got_b, got_core, got_ring, top, bottom, left, right):
    x, z, v, s = place(plan)
    even_layer, even_seg, wrap = lax.rem(z, 2) == 0, lax.rem(s, 2) == 0, s == 0
    width, half, last, at = plan.width, plan.half, plan.rows - 1, plan.outer

    @pl.when(even_layer)
    def _():
        top[...] = got_b[...]
        bottom[...] = got_a[...]

    @pl.when(jnp.logical_not(even_layer))
    def _():
        top[...] = got_a[...]
        bottom[...] = got_b[...]

    @pl.when(z == 0)
    def _():
        top[...] = jnp.zeros_like(top)

    @pl.when(z == plan.layers - 1)
    def _():
        bottom[...] = jnp.zeros_like(bottom)

    @pl.when(even_seg)
    def _():
        left[...] = got_ring[...]
        right[...] = got_core[...]

    @pl.when(jnp.logical_not(even_seg))
    def _():
        left[...] = got_core[...]
        right[...] = got_ring[...]

    def row(i):
        found = {0: dot_turned(left[i], w_out[at["N", i, 0]])}
        found[plan.run - 1] = dot(right[i], w_out[at["N", i, plan.run]])

        def add(p, term):
            found[p] = found[p] + term if p in found else term

        if i == 0:
            for p in range(plan.run):
                add(p, dot_turned(top[:, p * width : (p + 1) * width], w_out[at["F", 0, p]]))
            lanes = slice((half - 1) * width, half * width)
            before = jnp.where(wrap, top[:, lanes].astype(F32), u[0, :, lanes].astype(F32)).astype(BF16)
            add(half, dot_turned(before, w_out[at["N", 0, half]]))
        if i == last:
            for p in range(plan.run):
                add(p, dot(bottom[:, p * width : (p + 1) * width], w_out[at["F", plan.rows, p]]))
            lanes = slice(half * width, (half + 1) * width)
            after = jnp.where(wrap, bottom[:, lanes].astype(F32), u[last, :, lanes].astype(F32)).astype(BF16)
            here, there = at["N", last, half], at["N", plan.rows, half]
            add(half - 1, dot(after, w_out[here + wrap.astype(jnp.int32) * (there - here)]))
        return found

    return row, even_layer, even_seg


def halo_scratch(plan):
    edge = pltpu.VMEM((plan.vectors, plan.lanes), BF16)
    side = pltpu.VMEM((plan.rows, plan.vectors, plan.width), BF16)
    return [edge, edge, side, side]


def finished_row(plan, i, part, scale, factor, terms):
    out = []
    for p in range(plan.run):
        value = part[i, :, p * plan.width : (p + 1) * plan.width]
        if p in terms:
            value += (factor * scale[pl.ds(i * plan.run + p, 1), :]) * terms[p]
        out.append(value)
    return out


def outer_kernel(plan, factor, leaving, part, u, w_out, scale, got_a, got_b, got_core, got_ring, *refs):
    refs = list(refs)
    y_out, u_out, send_a, send_b, send_core, send_ring = refs[:6]
    halos = refs[-4:]
    row, even_layer, even_seg = halo_terms(plan, u, w_out, got_a, got_b, got_core, got_ring, *halos)
    width = plan.width
    for i in range(plan.rows):
        values = finished_row(plan, i, part, scale, factor, row(i))
        rounded = []
        for p, value in enumerate(values):
            y_out[i, :, p * width : (p + 1) * width] = value
            rounded.append((scale[pl.ds(i * plan.run + p, 1), :] * value).astype(BF16))
        emit(plan, i, jnp.concatenate(rounded, axis=1), even_layer, even_seg, u_out, send_a, send_b, send_core, send_ring)
    if leaving:
        exit_core = refs[6]
        core = lax.rem(lax.axis_index("vec"), 2)
        for k in range(plan.segments // 2):
            half, chip = divmod(k, plan.vecs // 2)
            first = pl.multiple_of((2 * chip + 1 - core) * plan.columns, plan.columns)
            for r in range(plan.own):
                exit_core[k, r] = y_out[half * plan.own + r, pl.ds(first, plan.columns), :]


def exit_shape(plan, n):
    return shape(n, plan.own, plan.columns, plan.lanes)


def outer(plan, factor, part, u, w_out, scale, got, leaving=False):
    outs = (shape(plan.rows, plan.vectors, plan.lanes),) + sends(plan)
    if leaving:
        outs += (exit_shape(plan, plan.segments // 2),)
    args = (part, u, w_out, scale) + tuple(got)
    return call(
        functools.partial(outer_kernel, plan, factor, leaving),
        outs,
        vm(len(args)),
        args,
        halo_scratch(plan),
        flops=40 << 20,
        moved=5 << 20,
    )


def chip_order(plan):
    return [(dx, dy) for dx in range(2) for dy in range(plan.vecs // 2)]


def leave_kernel(plan, y, got_core, *outs):
    x, z, v, s = place(plan)
    core, chip = lax.rem(v, 2), lax.div(v, 2)
    for (dx, dy), out in zip(chip_order(plan), outs, strict=True):
        to_x = jnp.where(x == 1, 1 - dx, dx)
        to_chip = chip
        if dy:
            to_chip = jnp.int32(0)
            for k in range(plan.vecs // 2):
                to_chip = to_chip + jnp.where(chip == k, k ^ dy, 0)
        first = pl.multiple_of((2 * to_chip + core) * plan.columns, plan.columns)
        for r in range(plan.own):
            out[0, r] = y[to_x * plan.own + r, pl.ds(first, plan.columns), :]
            out[1, r] = got_core[to_x * (plan.vecs // 2) + to_chip, r]


def leave(plan, y, got_core):
    n = len(chip_order(plan))
    return call(
        functools.partial(leave_kernel, plan), (exit_shape(plan, 2),) * n, vm(2), (y, got_core), moved=4 << 20
    )


def arrive_kernel(plan, *refs):
    *gots, out = refs
    x, z, v, s = place(plan)
    core, chip = lax.rem(v, 2), lax.div(v, 2)
    for (dx, dy), got in zip(chip_order(plan), gots, strict=True):
        for other in range(2):
            seg = jnp.int32(0)
            for m in range(2):
                for at in range(plan.vecs):
                    source = plan.seg[m ^ dx, (at ^ other) ^ (2 * dy)]
                    seg = seg + jnp.where((x == m) & (v == at), source, 0)
            for r in range(plan.own):
                for p in range(plan.run):
                    to = pl.multiple_of((r * SPAN + column(plan, seg, p)) * plan.width, plan.width)
                    out[:, pl.ds(to, plan.width)] = got[other, r, :, p * plan.width : (p + 1) * plan.width]


def arrive(plan, gots):
    return call(
        functools.partial(arrive_kernel, plan),
        shape(plan.columns, plan.blocks * plan.width),
        vm(len(gots)),
        tuple(gots),
        moved=2 << 20,
    )


def gram_pieces(plan):
    rows = plan.vectors // plan.meshes
    height = 8 if rows % 8 == 0 else rows
    return rows, height, rows // height


def image_kernel(plan, part, u, w_out, scale, got_a, got_b, got_core, got_ring, y, mass, out, *halos):
    row, _, _ = halo_terms(plan, u, w_out, got_a, got_b, got_core, got_ring, *halos)
    stiff = jnp.zeros((plan.vectors, plan.vectors), F32)
    for i in range(plan.rows):
        values = finished_row(plan, i, part, scale, 1.0, row(i))
        image = jnp.concatenate([value.astype(BF16) for value in values], axis=1)
        stiff += dot_turned(image, y[i].astype(BF16))
    rows, height, count = gram_pieces(plan)
    both = (stiff, mass[...])
    for m in range(plan.meshes):
        for v in range(plan.vecs):
            lanes = slice(v * plan.columns, (v + 1) * plan.columns)
            out[m * plan.vecs + v] = jnp.concatenate(
                [g[m * rows + h * height : m * rows + (h + 1) * height, lanes] for g in both for h in range(count)],
                axis=1,
            )


def image(plan, part, u, w_out, scale, got, y, mass):
    rows, height, count = gram_pieces(plan)
    args = (part, u, w_out, scale) + tuple(got) + (y, mass)
    return call(
        functools.partial(image_kernel, plan),
        shape(plan.meshes * plan.vecs, height, 2 * count * plan.columns),
        vm(len(args)),
        args,
        halo_scratch(plan),
        flops=50 << 20,
        moved=5 << 20,
    )


def sum_kernel(plan, got, stiff, mass):
    rows, height, count = gram_pieces(plan)
    total = jnp.sum(got[...], axis=0)
    for k, out in enumerate((stiff, mass)):
        for h in range(count):
            lo = (k * count + h) * plan.columns
            out[h * height : (h + 1) * height, :] = total[:, lo : lo + plan.columns]


def shards(plan, panel, orient, mass, diag, near, far):
    w = plan.width
    panel = panel.T
    orient, mass = orient.reshape(plan.blocks, w), mass.reshape(plan.blocks, w)
    scale_own, chunks, own, first, rest = prepare(plan, panel, orient, mass, diag, near, far)

    def half(m, v):
        return m ^ 1, v

    first = plan.swap(first, half)
    rest = plan.swap(rest, half)
    groups = [
        [(2 * z + d // plan.vecs) * plan.vecs + d % plan.vecs for d in range(plan.segments)] for z in range(plan.layers)
    ]
    got = lax.all_to_all(chunks, BOTH, 0, 0, tiled=True, axis_index_groups=groups)
    above = jnp.where(lax.axis_index("mesh") % 2 == 0, own, first[: plan.run + 1])
    pairs = [(m * plan.vecs + v, (m - 2) * plan.vecs + v) for m in range(2, plan.meshes) for v in range(plan.vecs)]
    below = lax.ppermute(above, BOTH, pairs)

    y, scale, *field = begin(plan, got, scale_own, first)
    w_in, w_out = weights(plan, diag, near, far, first, rest, below)

    def exchange(field):
        u, a, b, core, ring = field
        return u, (
            plan.swap(a, plan.layer_a),
            plan.swap(b, plan.layer_b),
            plan.swap(core, plan.core_swap),
            plan.swap(ring, plan.ring_swap),
        )

    for application in range(APPS):
        before = None
        for step in range(DEGREE):
            factors = (2.0 / RADIUS, -2.0 * CENTER / RADIUS, -1.0) if step else (1.0 / RADIUS, -CENTER / RADIUS, 0.0)
            u, halos = exchange(field)
            (part,) = inner(plan, factors, u, y, before, w_in, scale)
            leaving = application == APPS - 1 and step == DEGREE - 1
            new, *field = outer(plan, factors[0], part, u, w_out, scale, halos, leaving)
            before, y = y, new
    *field, exit_core = field
    u, halos = exchange(field)
    part, mass_gram = inner(plan, (1.0, 0.0, 0.0), u, y, None, w_in, scale, gram=True)
    got_core = plan.swap(exit_core, plan.core_swap)
    parts = leave(plan, y, got_core)
    kept = []
    for (dx, dy), sent in zip(chip_order(plan), parts, strict=True):
        if dx or dy:
            sent = plan.swap(sent, lambda m, v, dx=dx, dy=dy: (m ^ dx, v ^ (2 * dy)))
        kept.append(sent)
    grams = image(plan, part, u, w_out, scale, halos, y, mass_gram)
    grams = lax.all_to_all(grams, BOTH, 0, 0, tiled=True)
    rows = gram_pieces(plan)[0]
    stiff_gram, mass_gram = call(
        functools.partial(sum_kernel, plan), (shape(rows, plan.columns),) * 2, vm(1), (grams,), moved=1 << 17
    )
    filtered = arrive(plan, kept)
    return filtered.T, stiff_gram.T, mass_gram.T


def solution(mesh):
    placed = (P("mesh", "vec"), P("mesh"), P("mesh"), P("mesh"), P("mesh"), P("mesh"))

    def run(panel, orient, mass, diag, near, far):
        meshes, vecs = mesh.shape["mesh"], mesh.shape["vec"]
        plan = Plan(meshes, vecs, diag.shape[0] // meshes, diag.shape[1], panel.shape[1] // vecs)
        return jax.shard_map(
            functools.partial(shards, plan),
            mesh=mesh,
            in_specs=placed,
            out_specs=(P("mesh", "vec"), P("vec", "mesh"), P("vec", "mesh")),
            check_vma=False,
        )(panel, orient, mass, diag, near, far)

    return run
```

time: 397 us -> 150 us (0.38); the launches traced: 390 us -> 150 us
  waiting for transfers between devices: 249 us -> 54.7 us
  matrix products: 50.2 us -> 0 us
  Pallas kernels: 0 us -> 24.8 us
  starting transfers between devices: 59.6 us -> 44.6 us
  between operations: 15.1 us -> 0.92 us
  blocking collectives: 0 us -> 10.8 us
  other arithmetic: 7.93 us -> 0.67 us
  local copies, waits for them, and re-layouts: 7.53 us -> 13.2 us
    reduce_scatter x2 -> x0, waiting for transfers between devices: 126 us -> none  [the longest x1 64.1 us: shards(): lax.psum_scatter(partial_stiff, 'mesh', scatter_dimension=1, tiled=True)]
    dot_general x47 -> x0, matrix products: 50.2 us -> none  [the longest x27 32.5 us: blockmul(): lax.dot_general(matrix, values, (((2,), (1,)), ((0,), (0,))), preferred_e...]
    ppermute x19 -> x43, waiting for transfers between devices: 102 us -> 54.7 us  [the longest x42 50.2 us: swap(): return lax.ppermute(x, BOTH, pairs)]
    pallas_call x0 -> x24, Pallas kernels: none -> 24.8 us  [call(): pl.pallas_call(kernel, out_shape=outs, in_specs=ins, out_specs=jax.tree.m...]
    all_gather x2 -> x0, waiting for transfers between devices: 20.9 us -> none  [the longest x1 20.9 us: shards(): lax.all_gather(image_b, 'vec', axis=1, tiled=True)]
    ppermute x19 -> x43, starting transfers between devices: 59.4 us -> 39.3 us  [the longest x42 38.1 us: swap(): return lax.ppermute(x, BOTH, pairs)]
    all_to_all x0 -> x1, blocking collectives: none -> 10.8 us  [shards(): grams = lax.all_to_all(grams, BOTH, 0, 0, tiled=True)]
    unnamed x46 -> x24, local copies, waits for them, and re-layouts: 3.95 us -> 13.2 us
  transfers between devices with their start and end apart: 23 -> 44, of which waited for: 12 -> 17; matrix products, arithmetic and copies ran while one was open for 6% -> 0% of each run, Pallas kernels for 0% -> 9%
where the time goes in v1:
time: 150 us
  waiting for transfers between devices  54.7 us (36%)
  starting transfers between devices  44.6 us (30%)
  Pallas kernels  24.8 us (17%)
  local copies, waits for them, and re-layouts  13.2 us (9%)
  blocking collectives  10.8 us (7%)
    ppermute x42, waiting for transfers between devices, swap(): return lax.ppermute(x, BOTH, pairs)  50.2 us
    ppermute x42, starting transfers between devices, swap(): return lax.ppermute(x, BOTH, pairs)  38.1 us
    pallas_call x24, Pallas kernels, call(): pl.pallas_call(kernel, out_shape=outs, in_specs=ins, out_specs=jax.tree.m...  24.8 us
    unnamed x24, local copies, waits for them, and re-layouts  13.2 us
    all_to_all x1, blocking collectives, shards(): grams = lax.all_to_all(grams, BOTH, 0, 0, tiled=True)  10.8 us
    all_to_all x1, starting transfers between devices, shards(): lax.all_to_all(chunks, BOTH, 0, 0, tiled=True, axis_index_groups=groups)  5.3 us
    ppermute x1, waiting for transfers between devices, shards(): below = lax.ppermute(above, BOTH, pairs)  4.46 us
  transfers between devices with their start and end apart: 44, of which 17 were waited for; matrix products, arithmetic and copies ran while one was open for 0% of the time, Pallas kernels for 9%

profile of v1, /device:TPU:0, one launch (start us, length us, event | category | flops | bytes accessed | tf_op | source)
XLA Modules:
  0.0 149.8 jit_solution(4071425467726106930)
XLA Ops:
  8.2 1.8 %shard_map.85 = (f32[64,128]{1,0:T(8,128)S(1)}, f32[8,2,32,512]{3,2,1,0:T(8,128)S(1)}, bf16[5,128,128]{2,1,0:T(8,128)(2,1)S(1)}, bf16[6,128,128]{2,1,0:T(8,128)(2,1)S(1)}, bf16[22,128,128]{2,1,0:T(8,128)(2,1)S(1)}) custom-call(f32[32,8192]{1,0:T(8,128)S(1)} %bitcast.6, s32[64,128]{1,0:T(8,128)S(1)} %bitcast.7, f32[64,128]{1,0:T(8,128)S(1)} %bitcast.8, ...), custom_call_target="tpu_custom_call" | custom-call | bytes 4194304 | tf_op jit(solution)/shard_map/pallas_call | solution.py:129
  12.5 5.3 %all-to-all-start = ((f32[8,2,32,512]{3,2,1,0:T(8,128)}), f32[8,2,32,512]{3,2,1,0:T(8,128)S(1)}, u32[]{:S(2)}, u32[]{:S(2)}) async-start(f32[8,2,32,512]{3,2,1,0:T(8,128)} %copy-done.7), calls=%async_computation | async-start | bytes 2097152 | tf_op jit(solution)/shard_map/all_to_all | solution.py:618
  17.8 2.0 %collective-permute-start.1 = (bf16[22,128,128]{2,1,0:T(8,128)(2,1)}, bf16[22,128,128]{2,1,0:T(8,128)(2,1)}, u32[]{:S(2)}, u32[]{:S(2)}) collective-permute-start(bf16[22,128,128]{2,1,0:T(8,128)(2,1)} %copy-done.10), channel_id=1, source_target_pairs={{0,4},{1,5},{2,6},{3,7},{4,0},{5,1},{6,2},{7,3},{8,12},{9,13},{10,... | collective-permute-start | bytes 2162696 | tf_op jit(solution)/shard_map/ppermute | solution.py:76
  19.9 32.1 %collective-permute-done.first = bf16[6,128,128]{2,1,0:T(8,128)(2,1)S(1)} collective-permute-done((bf16[6,128,128]{2,1,0:T(8,128)(2,1)}, bf16[6,128,128]{2,1,0:T(8,128)(2,1)S(1)}, u32[]{:S(2)}, u32[]{:S(2)}) %collective-permute-start) | collective-permute-done | bytes 196640 | tf_op jit(solution)/shard_map/ppermute | solution.py:76
  54.2 2.7 %collective-permute-start.3 = (bf16[128,512]{1,0:T(8,128)(2,1)S(1)}, bf16[128,512]{1,0:T(8,128)(2,1)S(1)}, u32[]{:S(2)}, u32[]{:S(2)}) collective-permute-start(bf16[128,512]{1,0:T(8,128)(2,1)S(1)} %get-tuple-element.84), channel_id=1, source_target_pairs={{0,8},{1,9},{2,10},{3,11},{4,12},{5,13},{6,14},{7,15},{8,0},{9,1},... | collective-permute-start | bytes 393224 | tf_op jit(solution)/shard_map/ppermute | solution.py:76
  57.4 4.5 %collective-permute-done.2.below = bf16[5,128,128]{2,1,0:T(8,128)(2,1)S(1)} collective-permute-done((bf16[5,128,128]{2,1,0:T(8,128)(2,1)}, bf16[5,128,128]{2,1,0:T(8,128)(2,1)S(1)}, u32[]{:S(2)}, u32[]{:S(2)}) %collective-permute-start.2) | collective-permute-done | bytes 163872 | tf_op jit(solution)/shard_map/ppermute | solution.py:621
  65.4 3.0 %shard_map.87 = (bf16[40,128,128]{2,1,0:T(8,128)(2,1)S(1)}, bf16[19,128,128]{2,1,0:T(8,128)(2,1)S(1)}) custom-call(bf16[64,128,128]{2,1,0:T(8,128)(2,1)S(1)} %copy-done.1, bf16[64,128,128]{2,1,0:T(8,128)(2,1)S(1)} %copy-done.3, bf16[64,128,128]{2,1,0:T(8,128)(2,1)S(1)} %copy-done.5, bf16[6,128,128]{2,1,0:T(8,128)(2,1)S(1)} %collective-permute-done.first, ...), custom_call_target="tpu_custom_call" | custom-call | bytes 4194304 | tf_op jit(solution)/shard_map/pallas_call | solution.py:129
  70.4 1.6 %collective-permute-start.7 = (bf16[128,512]{1,0:T(8,128)(2,1)S(1)}, bf16[128,512]{1,0:T(8,128)(2,1)S(1)}, u32[]{:S(2)}, u32[]{:S(2)}) collective-permute-start(bf16[128,512]{1,0:T(8,128)(2,1)S(1)} %get-tuple-element.90), channel_id=1, source_target_pairs={{0,8},{1,9},{2,10},{3,11},{4,12},{5,13},{6,14},{7,15},{8,0},{9,1},... | collective-permute-start | bytes 393224 | tf_op jit(solution)/shard_map/ppermute | solution.py:76
  75.4 2.1 %collective-permute-done.10.got_ring = bf16[4,128,128]{2,1,0:T(8,128)(2,1)S(1)} collective-permute-done((bf16[4,128,128]{2,1,0:T(8,128)(2,1)S(1)}, bf16[4,128,128]{2,1,0:T(8,128)(2,1)S(1)}, u32[]{:S(2)}, u32[]{:S(2)}) %collective-permute-start.10) | collective-permute-done | bytes 131104 | tf_op jit(solution)/shard_map/ppermute | solution.py:76
  83.5 1.6 %collective-permute-done.14.got_ring = bf16[4,128,128]{2,1,0:T(8,128)(2,1)S(1)} collective-permute-done((bf16[4,128,128]{2,1,0:T(8,128)(2,1)S(1)}, bf16[4,128,128]{2,1,0:T(8,128)(2,1)S(1)}, u32[]{:S(2)}, u32[]{:S(2)}) %collective-permute-start.14) | collective-permute-done | bytes 131104 | tf_op jit(solution)/shard_map/ppermute | solution.py:76
  86.1 2.0 %collective-permute-start.15 = (bf16[128,512]{1,0:T(8,128)(2,1)S(1)}, bf16[128,512]{1,0:T(8,128)(2,1)S(1)}, u32[]{:S(2)}, u32[]{:S(2)}) collective-permute-start(bf16[128,512]{1,0:T(8,128)(2,1)S(1)} %get-tuple-element.102), channel_id=1, source_target_pairs={{0,8},{1,9},{2,10},{3,11},{4,12},{5,13},{6,14},{7,15},{8,0},{9,1},... | collective-permute-start | bytes 393224 | tf_op jit(solution)/shard_map/ppermute | solution.py:76
  91.5 2.2 %collective-permute-done.18.got_ring = bf16[4,128,128]{2,1,0:T(8,128)(2,1)S(1)} collective-permute-done((bf16[4,128,128]{2,1,0:T(8,128)(2,1)S(1)}, bf16[4,128,128]{2,1,0:T(8,128)(2,1)S(1)}, u32[]{:S(2)}, u32[]{:S(2)}) %collective-permute-start.18) | collective-permute-done | bytes 131104 | tf_op jit(solution)/shard_map/ppermute | solution.py:76
  101.5 1.6 %collective-permute-start.23 = (bf16[128,512]{1,0:T(8,128)(2,1)S(1)}, bf16[128,512]{1,0:T(8,128)(2,1)S(1)}, u32[]{:S(2)}, u32[]{:S(2)}) collective-permute-start(bf16[128,512]{1,0:T(8,128)(2,1)S(1)} %get-tuple-element.114), channel_id=1, source_target_pairs={{0,8},{1,9},{2,10},{3,11},{4,12},{5,13},{6,14},{7,15},{8,0},{9,1},... | collective-permute-start | bytes 393224 | tf_op jit(solution)/shard_map/ppermute | solution.py:76
  103.6 1.6 %collective-permute-start.26 = (bf16[4,128,128]{2,1,0:T(8,128)(2,1)S(1)}, bf16[4,128,128]{2,1,0:T(8,128)(2,1)S(1)}, u32[]{:S(2)}, u32[]{:S(2)}) collective-permute-start(bf16[4,128,128]{2,1,0:T(8,128)(2,1)S(1)} %get-tuple-element.117), channel_id=1, source_target_pairs={{0,4},{1,3},{2,6},{3,1},{4,0},{5,7},{6,2},{7,5},{8,12},{9,11},{10,... | collective-permute-start | bytes 393224 | tf_op jit(solution)/shard_map/ppermute | solution.py:76
  106.5 2.1 %collective-permute-done.26.got_ring = bf16[4,128,128]{2,1,0:T(8,128)(2,1)S(1)} collective-permute-done((bf16[4,128,128]{2,1,0:T(8,128)(2,1)S(1)}, bf16[4,128,128]{2,1,0:T(8,128)(2,1)S(1)}, u32[]{:S(2)}, u32[]{:S(2)}) %collective-permute-start.26) | collective-permute-done | bytes 131104 | tf_op jit(solution)/shard_map/ppermute | solution.py:76
  111.5 1.6 %collective-permute-start.30 = (bf16[4,128,128]{2,1,0:T(8,128)(2,1)S(1)}, bf16[4,128,128]{2,1,0:T(8,128)(2,1)S(1)}, u32[]{:S(2)}, u32[]{:S(2)}) collective-permute-start(bf16[4,128,128]{2,1,0:T(8,128)(2,1)S(1)} %get-tuple-element.123), channel_id=1, source_target_pairs={{0,4},{1,3},{2,6},{3,1},{4,0},{5,7},{6,2},{7,5},{8,12},{9,11},{10,... | collective-permute-start | bytes 393224 | tf_op jit(solution)/shard_map/ppermute | solution.py:76
  114.8 1.7 %collective-permute-done.30.got_ring = bf16[4,128,128]{2,1,0:T(8,128)(2,1)S(1)} collective-permute-done((bf16[4,128,128]{2,1,0:T(8,128)(2,1)S(1)}, bf16[4,128,128]{2,1,0:T(8,128)(2,1)S(1)}, u32[]{:S(2)}, u32[]{:S(2)}) %collective-permute-start.30) | collective-permute-done | bytes 131104 | tf_op jit(solution)/shard_map/ppermute | solution.py:76
  117.4 2.0 %collective-permute-start.31 = (bf16[128,512]{1,0:T(8,128)(2,1)S(1)}, bf16[128,512]{1,0:T(8,128)(2,1)S(1)}, u32[]{:S(2)}, u32[]{:S(2)}) collective-permute-start(bf16[128,512]{1,0:T(8,128)(2,1)S(1)} %get-tuple-element.126), channel_id=1, source_target_pairs={{0,8},{1,9},{2,10},{3,11},{4,12},{5,13},{6,14},{7,15},{8,0},{9,1},... | collective-permute-start | bytes 393224 | tf_op jit(solution)/shard_map/ppermute | solution.py:76
  119.9 1.6 %collective-permute-start.34 = (bf16[4,128,128]{2,1,0:T(8,128)(2,1)S(1)}, bf16[4,128,128]{2,1,0:T(8,128)(2,1)S(1)}, u32[]{:S(2)}, u32[]{:S(2)}) collective-permute-start(bf16[4,128,128]{2,1,0:T(8,128)(2,1)S(1)} %get-tuple-element.129), channel_id=1, source_target_pairs={{0,4},{1,3},{2,6},{3,1},{4,0},{5,7},{6,2},{7,5},{8,12},{9,11},{10,... | collective-permute-start | bytes 393224 | tf_op jit(solution)/shard_map/ppermute | solution.py:76
  122.7 2.2 %collective-permute-done.34.got_ring = bf16[4,128,128]{2,1,0:T(8,128)(2,1)S(1)} collective-permute-done((bf16[4,128,128]{2,1,0:T(8,128)(2,1)S(1)}, bf16[4,128,128]{2,1,0:T(8,128)(2,1)S(1)}, u32[]{:S(2)}, u32[]{:S(2)}) %collective-permute-start.34) | collective-permute-done | bytes 131104 | tf_op jit(solution)/shard_map/ppermute | solution.py:76
  126.9 1.6 %collective-permute-start.42 = (bf16[4,128,128]{2,1,0:T(8,128)(2,1)S(1)}, bf16[4,128,128]{2,1,0:T(8,128)(2,1)S(1)}, u32[]{:S(2)}, u32[]{:S(2)}) collective-permute-start(bf16[4,128,128]{2,1,0:T(8,128)(2,1)S(1)} %get-tuple-element.141), channel_id=1, source_target_pairs={{0,4},{1,3},{2,6},{3,1},{4,0},{5,7},{6,2},{7,5},{8,12},{9,11},{10,... | collective-permute-start | bytes 393224 | tf_op jit(solution)/shard_map/ppermute | solution.py:76
  130.1 1.7 %collective-permute-done.39.got_a = bf16[128,512]{1,0:T(8,128)(2,1)S(1)} collective-permute-done((bf16[128,512]{1,0:T(8,128)(2,1)S(1)}, bf16[128,512]{1,0:T(8,128)(2,1)S(1)}, u32[]{:S(2)}, u32[]{:S(2)}) %collective-permute-start.39) | collective-permute-done | bytes 131104 | tf_op jit(solution)/shard_map/ppermute | solution.py:76
  131.9 1.6 %collective-permute-start.37 = (f32[2,2,32,512]{3,2,1,0:T(8,128)S(1)}, f32[2,2,32,512]{3,2,1,0:T(8,128)S(1)}, u32[]{:S(2)}, u32[]{:S(2)}) collective-permute-start(f32[2,2,32,512]{3,2,1,0:T(8,128)S(1)} %get-tuple-element.134), channel_id=1, source_target_pairs={{0,4},{1,5},{2,6},{3,7},{4,0},{5,1},{6,2},{7,3},{8,12},{9,13},{10,... | collective-permute-start | bytes 786440 | tf_op jit(solution)/shard_map/ppermute | solution.py:76
  137.1 10.8 %all_to_all.10.got = f32[32,8,128]{2,1,0:T(8,128)S(1)} all-to-all(f32[32,8,128]{2,1,0:T(8,128)S(1)} %shard_map.107), channel_id=1, replica_groups=mesh['mesh'=8,'vec'=4] {'mesh','vec'}, dimensions={0} | all-to-all | bytes 262144 | tf_op jit(solution)/shard_map/all_to_all | solution.py:655
  (114 shorter events, 57.7 us)
Async XLA Ops:
  12.5 41.4 %all-to-all-start = ((f32[8,2,32,512]{3,2,1,0:T(8,128)}), f32[8,2,32,512]{3,2,1,0:T(8,128)S(1)}, u32[]{:S(2)}, u32[]{:S(2)}) async-start(f32[8,2,32,512]{3,2,1,0:T(8,128)} %copy-done.7), calls=%async_computation | async-start | bytes 2097152 | tf_op jit(solution)/shard_map/all_to_all | solution.py:618
  17.8 44.4 %collective-permute-start.1 = (bf16[22,128,128]{2,1,0:T(8,128)(2,1)}, bf16[22,128,128]{2,1,0:T(8,128)(2,1)}, u32[]{:S(2)}, u32[]{:S(2)}) collective-permute-start(bf16[22,128,128]{2,1,0:T(8,128)(2,1)} %copy-done.10), channel_id=1, source_target_pairs={{0,4},{1,5},{2,6},{3,7},{4,0},{5,1},{6,2},{7,3},{8,12},{9,13},{10,... | collective-permute-start | bytes 2162696 | tf_op jit(solution)/shard_map/ppermute | solution.py:76
  19.8 32.1 %collective-permute-start = (bf16[6,128,128]{2,1,0:T(8,128)(2,1)}, bf16[6,128,128]{2,1,0:T(8,128)(2,1)S(1)}, u32[]{:S(2)}, u32[]{:S(2)}) collective-permute-start(bf16[6,128,128]{2,1,0:T(8,128)(2,1)} %copy-done.11), channel_id=1, source_target_pairs={{0,4},{1,5},{2,6},{3,7},{4,0},{5,1},{6,2},{7,3},{8,12},{9,13},{10,... | collective-permute-start | bytes 589832 | tf_op jit(solution)/shard_map/ppermute | solution.py:76
  52.6 9.2 %collective-permute-start.2 = (bf16[5,128,128]{2,1,0:T(8,128)(2,1)}, bf16[5,128,128]{2,1,0:T(8,128)(2,1)S(1)}, u32[]{:S(2)}, u32[]{:S(2)}) collective-permute-start(bf16[5,128,128]{2,1,0:T(8,128)(2,1)} %slice_select_fusion), channel_id=1, source_target_pairs={{8,0},{9,1},{10,2},{11,3},{12,4},{13,5},{14,6},{15,7},{16,8},{17,9... | collective-permute-start | bytes 491528 | tf_op jit(solution)/shard_map/ppermute | solution.py:621
  54.2 15.2 %collective-permute-start.3 = (bf16[128,512]{1,0:T(8,128)(2,1)S(1)}, bf16[128,512]{1,0:T(8,128)(2,1)S(1)}, u32[]{:S(2)}, u32[]{:S(2)}) collective-permute-start(bf16[128,512]{1,0:T(8,128)(2,1)S(1)} %get-tuple-element.84), channel_id=1, source_target_pairs={{0,8},{1,9},{2,10},{3,11},{4,12},{5,13},{6,14},{7,15},{8,0},{9,1},... | collective-permute-start | bytes 393224 | tf_op jit(solution)/shard_map/ppermute | solution.py:76
  56.9 12.5 %collective-permute-start.4 = (bf16[128,512]{1,0:T(8,128)(2,1)S(1)}, bf16[128,512]{1,0:T(8,128)(2,1)S(1)}, u32[]{:S(2)}, u32[]{:S(2)}) collective-permute-start(bf16[128,512]{1,0:T(8,128)(2,1)S(1)} %get-tuple-element.85), channel_id=1, source_target_pairs={{0,1},{1,0},{2,3},{3,2},{4,5},{5,4},{6,7},{7,6},{8,16},{9,17},{10,... | collective-permute-start | bytes 393224 | tf_op jit(solution)/shard_map/ppermute | solution.py:76
  56.9 12.5 %collective-permute-start.5 = (bf16[4,128,128]{2,1,0:T(8,128)(2,1)S(1)}, bf16[4,128,128]{2,1,0:T(8,128)(2,1)S(1)}, u32[]{:S(2)}, u32[]{:S(2)}) collective-permute-start(bf16[4,128,128]{2,1,0:T(8,128)(2,1)S(1)} %get-tuple-element.86), channel_id=1, source_target_pairs={{0,1},{1,0},{2,3},{3,2},{4,5},{5,4},{6,7},{7,6},{8,9},{9,8},{10,11... | collective-permute-start | bytes 393224 | tf_op jit(solution)/shard_map/ppermute | solution.py:76
  61.8 7.6 %collective-permute-start.6 = (bf16[4,128,128]{2,1,0:T(8,128)(2,1)S(1)}, bf16[4,128,128]{2,1,0:T(8,128)(2,1)S(1)}, u32[]{:S(2)}, u32[]{:S(2)}) collective-permute-start(bf16[4,128,128]{2,1,0:T(8,128)(2,1)S(1)} %get-tuple-element.87), channel_id=1, source_target_pairs={{0,4},{1,3},{2,6},{3,1},{4,0},{5,7},{6,2},{7,5},{8,12},{9,11},{10,... | collective-permute-start | bytes 393224 | tf_op jit(solution)/shard_map/ppermute | solution.py:76
  70.4 5.0 %collective-permute-start.7 = (bf16[128,512]{1,0:T(8,128)(2,1)S(1)}, bf16[128,512]{1,0:T(8,128)(2,1)S(1)}, u32[]{:S(2)}, u32[]{:S(2)}) collective-permute-start(bf16[128,512]{1,0:T(8,128)(2,1)S(1)} %get-tuple-element.90), channel_id=1, source_target_pairs={{0,8},{1,9},{2,10},{3,11},{4,12},{5,13},{6,14},{7,15},{8,0},{9,1},... | collective-permute-start | bytes 393224 | tf_op jit(solution)/shard_map/ppermute | solution.py:76
  72.5 5.0 %collective-permute-start.10 = (bf16[4,128,128]{2,1,0:T(8,128)(2,1)S(1)}, bf16[4,128,128]{2,1,0:T(8,128)(2,1)S(1)}, u32[]{:S(2)}, u32[]{:S(2)}) collective-permute-start(bf16[4,128,128]{2,1,0:T(8,128)(2,1)S(1)} %get-tuple-element.93), channel_id=1, source_target_pairs={{0,4},{1,3},{2,6},{3,1},{4,0},{5,7},{6,2},{7,5},{8,12},{9,11},{10,... | collective-permute-start | bytes 393224 | tf_op jit(solution)/shard_map/ppermute | solution.py:76
  78.5 5.0 %collective-permute-start.11 = (bf16[128,512]{1,0:T(8,128)(2,1)S(1)}, bf16[128,512]{1,0:T(8,128)(2,1)S(1)}, u32[]{:S(2)}, u32[]{:S(2)}) collective-permute-start(bf16[128,512]{1,0:T(8,128)(2,1)S(1)} %get-tuple-element.96), channel_id=1, source_target_pairs={{0,8},{1,9},{2,10},{3,11},{4,12},{5,13},{6,14},{7,15},{8,0},{9,1},... | collective-permute-start | bytes 393224 | tf_op jit(solution)/shard_map/ppermute | solution.py:76
  80.2 5.0 %collective-permute-start.14 = (bf16[4,128,128]{2,1,0:T(8,128)(2,1)S(1)}, bf16[4,128,128]{2,1,0:T(8,128)(2,1)S(1)}, u32[]{:S(2)}, u32[]{:S(2)}) collective-permute-start(bf16[4,128,128]{2,1,0:T(8,128)(2,1)S(1)} %get-tuple-element.99), channel_id=1, source_target_pairs={{0,4},{1,3},{2,6},{3,1},{4,0},{5,7},{6,2},{7,5},{8,12},{9,11},{10,... | collective-permute-start | bytes 393224 | tf_op jit(solution)/shard_map/ppermute | solution.py:76
  86.1 5.3 %collective-permute-start.15 = (bf16[128,512]{1,0:T(8,128)(2,1)S(1)}, bf16[128,512]{1,0:T(8,128)(2,1)S(1)}, u32[]{:S(2)}, u32[]{:S(2)}) collective-permute-start(bf16[128,512]{1,0:T(8,128)(2,1)S(1)} %get-tuple-element.102), channel_id=1, source_target_pairs={{0,8},{1,9},{2,10},{3,11},{4,12},{5,13},{6,14},{7,15},{8,0},{9,1},... | collective-permute-start | bytes 393224 | tf_op jit(solution)/shard_map/ppermute | solution.py:76
  94.6 5.0 %collective-permute-start.19 = (bf16[128,512]{1,0:T(8,128)(2,1)S(1)}, bf16[128,512]{1,0:T(8,128)(2,1)S(1)}, u32[]{:S(2)}, u32[]{:S(2)}) collective-permute-start(bf16[128,512]{1,0:T(8,128)(2,1)S(1)} %get-tuple-element.108), channel_id=1, source_target_pairs={{0,8},{1,9},{2,10},{3,11},{4,12},{5,13},{6,14},{7,15},{8,0},{9,1},... | collective-permute-start | bytes 393224 | tf_op jit(solution)/shard_map/ppermute | solution.py:76
  101.5 5.0 %collective-permute-start.23 = (bf16[128,512]{1,0:T(8,128)(2,1)S(1)}, bf16[128,512]{1,0:T(8,128)(2,1)S(1)}, u32[]{:S(2)}, u32[]{:S(2)}) collective-permute-start(bf16[128,512]{1,0:T(8,128)(2,1)S(1)} %get-tuple-element.114), channel_id=1, source_target_pairs={{0,8},{1,9},{2,10},{3,11},{4,12},{5,13},{6,14},{7,15},{8,0},{9,1},... | collective-permute-start | bytes 393224 | tf_op jit(solution)/shard_map/ppermute | solution.py:76
  109.7 5.0 %collective-permute-start.27 = (bf16[128,512]{1,0:T(8,128)(2,1)S(1)}, bf16[128,512]{1,0:T(8,128)(2,1)S(1)}, u32[]{:S(2)}, u32[]{:S(2)}) collective-permute-start(bf16[128,512]{1,0:T(8,128)(2,1)S(1)} %get-tuple-element.120), channel_id=1, source_target_pairs={{0,8},{1,9},{2,10},{3,11},{4,12},{5,13},{6,14},{7,15},{8,0},{9,1},... | collective-permute-start | bytes 393224 | tf_op jit(solution)/shard_map/ppermute | solution.py:76
  117.4 5.3 %collective-permute-start.31 = (bf16[128,512]{1,0:T(8,128)(2,1)S(1)}, bf16[128,512]{1,0:T(8,128)(2,1)S(1)}, u32[]{:S(2)}, u32[]{:S(2)}) collective-permute-start(bf16[128,512]{1,0:T(8,128)(2,1)S(1)} %get-tuple-element.126), channel_id=1, source_target_pairs={{0,8},{1,9},{2,10},{3,11},{4,12},{5,13},{6,14},{7,15},{8,0},{9,1},... | collective-permute-start | bytes 393224 | tf_op jit(solution)/shard_map/ppermute | solution.py:76
  126.0 5.9 %collective-permute-start.39 = (bf16[128,512]{1,0:T(8,128)(2,1)S(1)}, bf16[128,512]{1,0:T(8,128)(2,1)S(1)}, u32[]{:S(2)}, u32[]{:S(2)}) collective-permute-start(bf16[128,512]{1,0:T(8,128)(2,1)S(1)} %get-tuple-element.138), channel_id=1, source_target_pairs={{0,8},{1,9},{2,10},{3,11},{4,12},{5,13},{6,14},{7,15},{8,0},{9,1},... | collective-permute-start | bytes 393224 | tf_op jit(solution)/shard_map/ppermute | solution.py:76
  126.4 7.1 %collective-permute-start.40 = (bf16[128,512]{1,0:T(8,128)(2,1)S(1)}, bf16[128,512]{1,0:T(8,128)(2,1)S(1)}, u32[]{:S(2)}, u32[]{:S(2)}) collective-permute-start(bf16[128,512]{1,0:T(8,128)(2,1)S(1)} %get-tuple-element.139), channel_id=1, source_target_pairs={{0,1},{1,0},{2,3},{3,2},{4,5},{5,4},{6,7},{7,6},{8,16},{9,17},{10,... | collective-permute-start | bytes 393224 | tf_op jit(solution)/shard_map/ppermute | solution.py:76
  126.6 9.6 %collective-permute-start.41 = (bf16[4,128,128]{2,1,0:T(8,128)(2,1)S(1)}, bf16[4,128,128]{2,1,0:T(8,128)(2,1)S(1)}, u32[]{:S(2)}, u32[]{:S(2)}) collective-permute-start(bf16[4,128,128]{2,1,0:T(8,128)(2,1)S(1)} %get-tuple-element.140), channel_id=1, source_target_pairs={{0,1},{1,0},{2,3},{3,2},{4,5},{5,4},{6,7},{7,6},{8,9},{9,8},{10,11... | collective-permute-start | bytes 393224 | tf_op jit(solution)/shard_map/ppermute | solution.py:76
  126.9 9.3 %collective-permute-start.42 = (bf16[4,128,128]{2,1,0:T(8,128)(2,1)S(1)}, bf16[4,128,128]{2,1,0:T(8,128)(2,1)S(1)}, u32[]{:S(2)}, u32[]{:S(2)}) collective-permute-start(bf16[4,128,128]{2,1,0:T(8,128)(2,1)S(1)} %get-tuple-element.141), channel_id=1, source_target_pairs={{0,4},{1,3},{2,6},{3,1},{4,0},{5,7},{6,2},{7,5},{8,12},{9,11},{10,... | collective-permute-start | bytes 393224 | tf_op jit(solution)/shard_map/ppermute | solution.py:76
  128.6 20.0 %collective-permute-start.36 = (f32[2,2,32,512]{3,2,1,0:T(8,128)S(1)}, f32[2,2,32,512]{3,2,1,0:T(8,128)S(1)}, u32[]{:S(2)}, u32[]{:S(2)}) collective-permute-start(f32[2,2,32,512]{3,2,1,0:T(8,128)S(1)} %get-tuple-element.133), channel_id=1, source_target_pairs={{0,2},{1,3},{2,0},{3,1},{4,6},{5,7},{6,4},{7,5},{8,10},{9,11},{10,... | collective-permute-start | bytes 786440 | tf_op jit(solution)/shard_map/ppermute | solution.py:76
  131.9 16.7 %collective-permute-start.37 = (f32[2,2,32,512]{3,2,1,0:T(8,128)S(1)}, f32[2,2,32,512]{3,2,1,0:T(8,128)S(1)}, u32[]{:S(2)}, u32[]{:S(2)}) collective-permute-start(f32[2,2,32,512]{3,2,1,0:T(8,128)S(1)} %get-tuple-element.134), channel_id=1, source_target_pairs={{0,4},{1,5},{2,6},{3,7},{4,0},{5,1},{6,2},{7,3},{8,12},{9,13},{10,... | collective-permute-start | bytes 786440 | tf_op jit(solution)/shard_map/ppermute | solution.py:76
  133.5 15.1 %collective-permute-start.38 = (f32[2,2,32,512]{3,2,1,0:T(8,128)S(1)}, f32[2,2,32,512]{3,2,1,0:T(8,128)S(1)}, u32[]{:S(2)}, u32[]{:S(2)}) collective-permute-start(f32[2,2,32,512]{3,2,1,0:T(8,128)S(1)} %get-tuple-element.135), channel_id=1, source_target_pairs={{0,6},{1,7},{2,4},{3,5},{4,2},{5,3},{6,0},{7,1},{8,14},{9,15},{10,... | collective-permute-start | bytes 786440 | tf_op jit(solution)/shard_map/ppermute | solution.py:76
  (32 other events, 141.8 us)

commit v2 on v1

v2 whole, which is shorter than its diff:
```python
import functools

import jax
import jax.numpy as jnp
from jax import lax
from jax.experimental import pallas as pl
from jax.experimental.pallas import tpu as pltpu
from jax.sharding import PartitionSpec as P

SPAN = 32
DEGREE = 4
APPS = 2
CENTER = 6.0
RADIUS = 8.0

BOTH = ("mesh", "vec")
ORDER = ("ring", "a", "b", "core")
F32 = jnp.float32
BF16 = jnp.bfloat16
VMEM_LIMIT = 24 * 1024 * 1024


def gray(t):
    return t ^ (t >> 1)


class Plan:
    def __init__(self, meshes, vecs, blocks, width, columns):
        self.meshes, self.vecs, self.blocks, self.width, self.columns = meshes, vecs, blocks, width, columns
        self.ring = [(0, gray(t)) for t in range(vecs)] + [(1, gray(t)) for t in reversed(range(vecs))]
        self.segments = 2 * vecs
        self.seg = {place: s for s, place in enumerate(self.ring)}
        self.layers = meshes // 2
        self.own = blocks // SPAN
        self.rows = 2 * self.own
        self.run = SPAN // self.segments
        self.half = self.run // 2
        self.lanes = self.run * width
        self.vectors = vecs * columns
        self.inner, self.outer = {}, {}
        for i in range(self.rows):
            for p in range(self.run):
                self.inner["D", i, p] = len(self.inner)
        for i in range(self.rows):
            for p in range(1, self.run):
                self.inner["N", i, p] = len(self.inner)
        for i in range(1, self.rows):
            for p in range(self.run):
                self.inner["F", i, p] = len(self.inner)
        for p in range(self.run):
            self.outer["F", 0, p] = len(self.outer)
        for p in range(self.run):
            self.outer["F", self.rows, p] = len(self.outer)
        for i in range(self.rows):
            self.outer["N", i, 0] = len(self.outer)
            self.outer["N", i, self.run] = len(self.outer)
        for i in (0, self.rows - 1, self.rows):
            self.outer["N", i, self.half] = len(self.outer)
        self.count = self.own * self.run
        self.aux = self.run + 1
        self.n_first = self.aux + 1 + self.count // 2
        self.n_rest = self.own * (self.run + 1) - 1 + (self.own - 1) * self.run

    def received(self, kind, r, p):
        if kind == "N":
            if r == 0 and p == self.half:
                return 0, self.run
            return 1, r * (self.run + 1) + p - (r > 0 or p > self.half)
        if r == 0:
            return 0, p
        return 1, self.own * (self.run + 1) - 1 + (r - 1) * self.run + p

    def swap(self, x, partner):
        pairs = []
        for m in range(self.meshes):
            for v in range(self.vecs):
                to, at = partner(m, v)
                pairs.append((m * self.vecs + v, to * self.vecs + at))
        return lax.ppermute(x, BOTH, pairs)

    def layer_a(self, m, v):
        to = m ^ 2
        return (to, v) if to < self.meshes else (m, v ^ 1)

    def layer_b(self, m, v):
        z = m // 2
        to = m + 2 if z % 2 else m - 2
        return (to, v) if 0 <= to < self.meshes else (m, v ^ 1)

    def ring_swap(self, m, v):
        s = self.seg[m % 2, v]
        x, at = self.ring[(s + 1) % self.segments if s % 2 else (s - 1) % self.segments]
        return m - m % 2 + x, at

    def core_swap(self, m, v):
        return m, v ^ 1


def place(plan):
    m, v = lax.axis_index("mesh"), lax.axis_index("vec")
    x, z = lax.rem(m, 2), lax.div(m, 2)
    s = jnp.int32(0)
    for k, (a, b) in enumerate(plan.ring):
        s = s + jnp.where((x == a) & (v == b), k, 0)
    return x, z, v, s


def column(plan, s, p):
    return lax.rem(plan.run * s + (p - plan.half + SPAN), SPAN)


def pieces(plan, s):
    found = []
    for p in range(plan.run):
        j = (plan.run * s + p - plan.half) % SPAN
        if found and found[-1][1] + found[-1][2] == j:
            found[-1][2] += 1
        else:
            found.append([p, j, 1])
    return found


def dot(u, w):
    return lax.dot_general(u, w, (((1,), (0,)), ((), ())), preferred_element_type=F32)


def dot_turned(u, w):
    return lax.dot_general(u, w, (((1,), (1,)), ((), ())), preferred_element_type=F32)


def call(name, kernel, outs, ins, args, scratch=(), flops=0, moved=0):
    return pl.pallas_call(
        kernel,
        name=name,
        out_shape=outs,
        in_specs=ins,
        out_specs=jax.tree.map(lambda _: pl.BlockSpec(memory_space=pltpu.VMEM), outs),
        scratch_shapes=list(scratch),
        compiler_params=pltpu.CompilerParams(vmem_limit_bytes=VMEM_LIMIT),
        cost_estimate=pl.CostEstimate(flops=flops, bytes_accessed=moved, transcendentals=0),
    )(*args)


def vm(n):
    return [pl.BlockSpec(memory_space=pltpu.VMEM)] * n


def in_hbm(n):
    return [pl.BlockSpec(memory_space=pltpu.HBM)] * n


def shape(*dims, dtype=F32):
    return jax.ShapeDtypeStruct(dims, dtype)


class Copies:
    def __init__(self, sems):
        self.sems, self.started = sems, []

    def start(self, src, dst):
        copy = pltpu.make_async_copy(src, dst, self.sems.at[len(self.started)])
        copy.start()
        self.started.append(copy)

    def start_one(self, first, src, dst, otherwise):
        sem = self.sems.at[len(self.started)]

        @pl.when(first)
        def _():
            pltpu.make_async_copy(src, dst, sem).start()

        @pl.when(jnp.logical_not(first))
        def _():
            pltpu.make_async_copy(src, otherwise, sem).start()

        self.started.append(pltpu.make_async_copy(src, dst, sem))

    def wait(self, lo=0, hi=None):
        for copy in self.started[lo:hi]:
            copy.wait()


def block_of(plan, src, seg, r, p):
    return src.at[r * SPAN + column(plan, seg, p)]


def upper(w):
    return lax.broadcasted_iota(jnp.int32, (w, w), 0) <= lax.broadcasted_iota(jnp.int32, (w, w), 1)


def on_diagonal(w):
    return lax.broadcasted_iota(jnp.int32, (w, w), 0) == lax.broadcasted_iota(jnp.int32, (w, w), 1)


def prepare_kernel(plan, panel, orient, mass, diag, near, far, scale, enter, own_enter, first, *scratch):
    signs, masses, blocks, parts, sems = scratch
    x, z, v, s = place(plan)
    other = plan.segments - 1 - s
    core = lax.rem(v, 2)
    copies = Copies(sems)
    copies.start(orient, signs)
    copies.start(mass, masses)
    for r in range(plan.own):
        for p in range(plan.run):
            copies.start(block_of(plan, diag, other, r, p), blocks.at[r * plan.run + p])
    for d in range(plan.segments):
        chip, at_core = divmod(d, 2)
        seg = plan.seg[d // plan.vecs, d % plan.vecs]
        for r in range(plan.own):
            for p, j, n in pieces(plan, seg):
                src = panel.at[:, pl.ds((r * SPAN + j) * plan.width, n * plan.width)]
                lanes = pl.ds(p * plan.width, n * plan.width)
                copies.start_one(core == at_core, src, own_enter.at[chip, r, :, lanes], enter.at[chip, r, :, lanes])
    for p in range(plan.run):
        copies.start(block_of(plan, far, other, 0, p), first.at[p])
    copies.start(block_of(plan, near, other, 0, plan.half), first.at[plan.run])
    copies.wait(0, 2)
    scale[...] = signs[...].astype(F32) * lax.rsqrt(masses[...])
    parts[...] = jnp.zeros_like(parts)
    for r in range(plan.own):
        for p in range(plan.run):
            value = scale[pl.ds(r * SPAN + column(plan, other, p), 1), :]
            for part in range(3):
                rounded = value.astype(BF16).astype(F32)
                at = part * plan.count + r * plan.run + p
                parts[at : at + 1, :] = rounded
                value = value - rounded
    copies.wait(2, 2 + plan.count)
    keep, line = upper(plan.width), on_diagonal(plan.width)
    for k in range(plan.count // 2):
        one, two = blocks[2 * k].astype(F32), blocks[2 * k + 1].astype(F32)
        first[plan.aux + 1 + k] = jnp.where(keep, one, two).astype(BF16)
        at = 3 * plan.count + k
        parts[at : at + 1, :] = jnp.sum(jnp.where(line, two, 0.0), axis=0, keepdims=True)
    first[plan.aux] = parts[...].astype(BF16)
    copies.wait(2 + plan.count)


def prepare(plan, panel, orient, mass, diag, near, far):
    w = plan.width
    n_copies = 2 + plan.count + plan.run + 1
    n_copies += plan.own * sum(len(pieces(plan, seg)) for seg in range(plan.segments))
    args = [pltpu.with_memory_space_constraint(a, pltpu.HBM) for a in (panel, orient, mass, diag, near, far)]
    entering = shape(plan.segments // 2, plan.own, plan.columns, plan.lanes)
    return call(
        "prepare",
        functools.partial(prepare_kernel, plan),
        (shape(plan.blocks, w), entering, entering, shape(plan.n_first, w, w, dtype=BF16)),
        in_hbm(6),
        args,
        [
            pltpu.VMEM((plan.blocks, w), orient.dtype),
            pltpu.VMEM((plan.blocks, w), F32),
            pltpu.VMEM((plan.count, w, w), BF16),
            pltpu.VMEM((w, w), F32),
            pltpu.SemaphoreType.DMA((n_copies,)),
        ],
        moved=4 << 20,
    )


def fetch_kernel(plan, diag, near, far, own_diag, own_first, own_rest, rest, sems):
    x, z, v, s = place(plan)
    copies = Copies(sems)
    for seg, heads, tail in ((plan.segments - 1 - s, None, rest), (s, own_first, own_rest)):
        for kind, src in (("N", near), ("F", far)):
            for r in range(plan.own):
                for p in range(plan.run + (kind == "N")):
                    which, at = plan.received(kind, r, p)
                    if which == 1:
                        copies.start(block_of(plan, src, seg, r, p), tail.at[at])
                    elif heads is not None:
                        copies.start(block_of(plan, src, seg, r, p), heads.at[at])
    for r in range(plan.own):
        for p in range(plan.run):
            copies.start(block_of(plan, diag, s, r, p), own_diag.at[r * plan.run + p])
    copies.wait()


def fetch(plan, diag, near, far):
    w = plan.width
    args = [pltpu.with_memory_space_constraint(a, pltpu.HBM) for a in (diag, near, far)]
    return call(
        "fetch",
        functools.partial(fetch_kernel, plan),
        tuple(shape(n, w, w, dtype=BF16) for n in (plan.count, plan.run + 1, plan.n_rest, plan.n_rest)),
        in_hbm(3),
        args,
        [pltpu.SemaphoreType.DMA((2 * plan.n_rest + plan.run + 1 + plan.count,))],
        moved=3 << 20,
    )


def enter_kernel(plan, own_enter, got_core, *outs):
    x, z, v, s = place(plan)
    core, chip = lax.rem(v, 2), lax.div(v, 2)
    for (dx, dy), out in zip(chip_order(plan), outs, strict=True):
        at = chip_at(plan, x, chip, dx, dy)
        for r in range(plan.own):
            out[core, r] = own_enter[at, r]
            out[1 - core, r] = got_core[at, r]


def enter(plan, own_enter, got_core):
    n = len(chip_order(plan))
    return call(
        "enter",
        functools.partial(enter_kernel, plan),
        (exit_shape(plan, 2),) * n,
        vm(2),
        (own_enter, got_core),
        moved=4 << 20,
    )


def chip_order(plan):
    pairs = [(dx, dy) for dx in range(2) for dy in range(plan.vecs // 2)]
    return pairs[plan.vecs // 2 :] + pairs[: plan.vecs // 2]


def chip_at(plan, x, chip, dx, dy):
    to_x = 1 - x if dx else x
    to_chip = chip
    if dy:
        to_chip = jnp.int32(0)
        for k in range(plan.vecs // 2):
            to_chip = to_chip + jnp.where(chip == k, k ^ dy, 0)
    return to_x * (plan.vecs // 2) + to_chip


def emit(plan, u_out, send_a, send_b, send_core, send_ring):
    x, z, v, s = place(plan)
    last, width = plan.rows - 1, plan.width
    even_layer, even_seg = lax.rem(z, 2) == 0, lax.rem(s, 2) == 0
    send_a[...] = lax.select(even_layer, u_out[last], u_out[0])
    send_b[...] = lax.select(even_layer, u_out[0], u_out[last])
    for i in range(plan.rows):
        left, right = u_out[i, :, :width], u_out[i, :, plan.lanes - width :]
        send_core[i] = lax.select(even_seg, right, left)
        send_ring[i] = lax.select(even_seg, left, right)


def sends(plan):
    w = plan.width
    edge = shape(plan.vectors, plan.lanes, dtype=BF16)
    side = shape(plan.rows, plan.vectors, w, dtype=BF16)
    return (shape(plan.rows, plan.vectors, plan.lanes, dtype=BF16), edge, edge, side, side)


def begin_kernel(plan, scale_own, first, *refs):
    gots, refs = refs[: plan.vecs], refs[plan.vecs :]
    y_out, scale_out, u_out, send_a, send_b, send_core, send_ring = refs
    x, z, v, s = place(plan)
    count = plan.count
    parts = first[plan.aux].astype(F32)
    theirs = (parts[:count] + parts[count : 2 * count]) + parts[2 * count : 3 * count]
    chip = lax.div(v, 2)
    for (dx, dy), got in zip(chip_order(plan), gots, strict=True):
        from_x = 1 - x if dx else x
        from_chip = chip_at(plan, x, chip, dx, dy) - from_x * (plan.vecs // 2)
        for core in range(2):
            lo = pl.multiple_of((2 * from_chip + core) * plan.columns, plan.columns)
            for r in range(plan.own):
                y_out[from_x * plan.own + r, pl.ds(lo, plan.columns), :] = got[core, r]
    for i in range(plan.rows):
        half, r = divmod(i, plan.own)
        for p in range(plan.run):
            mine = scale_own[pl.ds(r * SPAN + column(plan, s, p), 1), :]
            scale_out[pl.ds(i * plan.run + p, 1), :] = jnp.where(
                x == half, mine, theirs[r * plan.run + p : r * plan.run + p + 1]
            )
    for i in range(plan.rows):
        for p in range(plan.run):
            row, lanes = scale_out[pl.ds(i * plan.run + p, 1), :], slice(p * plan.width, (p + 1) * plan.width)
            u_out[i, :, lanes] = (row * y_out[i, :, lanes]).astype(BF16)
    emit(plan, u_out, send_a, send_b, send_core, send_ring)


def begin(plan, gots, scale_own, first):
    return call(
        "begin", functools.partial(begin_kernel, plan),
        (shape(plan.rows, plan.vectors, plan.lanes), shape(plan.rows * plan.run, plan.width)) + sends(plan),
        vm(2 + len(gots)),
        (scale_own, first, *gots),
        moved=4 << 20,
    )


def weights_kernel(plan, own_diag, own_first, own_rest, first, rest, below, inner, outer):
    x, _, _, _ = place(plan)
    keep, line = upper(plan.width), on_diagonal(plan.width)
    lines = first[plan.aux].astype(F32)
    for k in range(plan.count // 2):
        both = first[plan.aux + 1 + k].astype(F32)
        turned = both.T
        at = 3 * plan.count + k
        found = jnp.where(keep, both, turned), jnp.where(line, lines[at : at + 1], jnp.where(keep, turned, both))
        for at, value in zip((2 * k, 2 * k + 1), found, strict=True):
            r, p = divmod(at, plan.run)
            value = value.astype(BF16)
            for half in range(2):
                mine, theirs = plan.inner["D", half * plan.own + r, p], plan.inner["D", (1 - half) * plan.own + r, p]

                @pl.when(x == half)
                def _():
                    inner[mine] = own_diag[at]
                    inner[theirs] = value

    for half in range(2):

        @pl.when(x == half)
        def _():
            for table, out in ((plan.inner, inner), (plan.outer, outer)):
                for (kind, i, p), k in table.items():
                    if i == plan.rows:
                        out[k] = below[p if kind == "F" else plan.run]
                    elif kind != "D":
                        group, r = divmod(i, plan.own)
                        which, index = plan.received(kind, r, p)
                        source = (own_first, own_rest) if group == half else (first, rest)
                        out[k] = source[which][index]


def weights(plan, own_diag, own_first, own_rest, first, rest, below):
    w = plan.width
    return call(
        "weights",
        functools.partial(weights_kernel, plan),
        (shape(len(plan.inner), w, w, dtype=BF16), shape(len(plan.outer), w, w, dtype=BF16)),
        vm(6),
        (own_diag, own_first, own_rest, first, rest, below),
        moved=4 << 20,
    )


def inner_kernel(plan, factors, has_before, gram, *refs):
    a, b, c = factors
    refs = list(refs)
    u, y = refs[:2]
    before = refs[2] if has_before else None
    w_in, scale, part = refs[2 + has_before : 5 + has_before]
    x, z, v, s = place(plan)
    wrap = (s == 0).astype(jnp.int32)
    width, half, last = plan.width, plan.half, plan.rows - 1
    at = plan.inner
    for i in range(plan.rows):
        for p in range(plan.run):
            lanes = slice(p * width, (p + 1) * width)
            total = dot(u[i, :, lanes], w_in[at["D", i, p]])
            if p == half:
                if i > 0:
                    total += dot_turned(u[i - wrap, :, (p - 1) * width : p * width], w_in[at["N", i, p]])
            elif p > 0:
                total += dot_turned(u[i, :, (p - 1) * width : p * width], w_in[at["N", i, p]])
            if p + 1 == half:
                if i < last:
                    near = at["N", i, half] + wrap * (plan.run - 1)
                    total += dot(u[i + wrap, :, (p + 1) * width : (p + 2) * width], w_in[near])
            elif p + 1 < plan.run:
                total += dot(u[i, :, (p + 1) * width : (p + 2) * width], w_in[at["N", i, p + 1]])
            if i > 0:
                total += dot_turned(u[i - 1, :, lanes], w_in[at["F", i, p]])
            if i < last:
                total += dot(u[i + 1, :, lanes], w_in[at["F", i + 1, p]])
            result = (a * scale[pl.ds(i * plan.run + p, 1), :]) * total
            if b:
                result += b * y[i, :, lanes]
            if has_before:
                result += c * before[i, :, lanes]
            part[i, :, lanes] = result
    if gram:
        mass = refs[5 + has_before]
        total = jnp.zeros(mass.shape, F32)
        for i in range(plan.rows):
            rounded = y[i].astype(BF16)
            total += dot_turned(rounded, rounded)
        mass[...] = total


def inner(plan, factors, u, y, before, w_in, scale, gram=False):
    has_before = before is not None
    args = (u, y) + ((before,) if has_before else ()) + (w_in, scale)
    outs = (shape(plan.rows, plan.vectors, plan.lanes),)
    if gram:
        outs += (shape(plan.vectors, plan.vectors),)
    return call(
        "inner", functools.partial(inner_kernel, plan, factors, has_before, gram),
        outs,
        vm(len(args)),
        args,
        flops=130 << 20,
        moved=5 << 20,
    )


def halo_terms(plan, u, w_out, *gots):
    x, z, v, s = place(plan)
    even_layer, even_seg, wrap = lax.rem(z, 2) == 0, lax.rem(s, 2) == 0, s == 0
    width, half, last, at = plan.width, plan.half, plan.rows - 1, plan.outer
    got = dict(zip(ORDER, gots, strict=True))
    got_a, got_b, got_ring, got_core = got["a"], got["b"], got["ring"], got["core"]
    none = jnp.zeros(got_a.shape, BF16)
    top = lax.select(z == 0, none, lax.select(even_layer, got_b[...], got_a[...]))
    bottom = lax.select(z == plan.layers - 1, none, lax.select(even_layer, got_a[...], got_b[...]))
    left = [lax.select(even_seg, got_ring[i], got_core[i]) for i in range(plan.rows)]
    right = [lax.select(even_seg, got_core[i], got_ring[i]) for i in range(plan.rows)]

    def row(i):
        found = {0: dot_turned(left[i], w_out[at["N", i, 0]])}
        found[plan.run - 1] = dot(right[i], w_out[at["N", i, plan.run]])

        def add(p, term):
            found[p] = found[p] + term if p in found else term

        if i == 0:
            for p in range(plan.run):
                add(p, dot_turned(top[:, p * width : (p + 1) * width], w_out[at["F", 0, p]]))
            lanes = slice((half - 1) * width, half * width)
            before = lax.select(wrap, top[:, lanes], u[0, :, lanes])
            add(half, dot_turned(before, w_out[at["N", 0, half]]))
        if i == last:
            for p in range(plan.run):
                add(p, dot(bottom[:, p * width : (p + 1) * width], w_out[at["F", plan.rows, p]]))
            lanes = slice(half * width, (half + 1) * width)
            after = lax.select(wrap, bottom[:, lanes], u[last, :, lanes])
            here, there = at["N", last, half], at["N", plan.rows, half]
            add(half - 1, dot(after, w_out[here + wrap.astype(jnp.int32) * (there - here)]))
        return found

    return row


def finished_row(plan, i, part, scale, factor, terms):
    out = []
    for p in range(plan.run):
        value = part[i, :, p * plan.width : (p + 1) * plan.width]
        if p in terms:
            value += (factor * scale[pl.ds(i * plan.run + p, 1), :]) * terms[p]
        out.append(value)
    return out


def outer_kernel(plan, factor, leaving, part, u, w_out, scale, got_0, got_1, got_2, got_3, *refs):
    refs = list(refs)
    y_out, u_out, send_a, send_b, send_core, send_ring = refs[:6]
    row = halo_terms(plan, u, w_out, got_0, got_1, got_2, got_3)
    width = plan.width
    for i in range(plan.rows):
        values = finished_row(plan, i, part, scale, factor, row(i))
        for p, value in enumerate(values):
            y_out[i, :, p * width : (p + 1) * width] = value
            u_out[i, :, p * width : (p + 1) * width] = (scale[pl.ds(i * plan.run + p, 1), :] * value).astype(BF16)
    emit(plan, u_out, send_a, send_b, send_core, send_ring)
    if leaving:
        exit_core = refs[6]
        core = lax.rem(lax.axis_index("vec"), 2)
        for k in range(plan.segments // 2):
            half, chip = divmod(k, plan.vecs // 2)
            first = pl.multiple_of((2 * chip + 1 - core) * plan.columns, plan.columns)
            for r in range(plan.own):
                exit_core[k, r] = y_out[half * plan.own + r, pl.ds(first, plan.columns), :]


def exit_shape(plan, n):
    return shape(n, plan.own, plan.columns, plan.lanes)


def outer(plan, factor, part, u, w_out, scale, got, leaving=False):
    outs = (shape(plan.rows, plan.vectors, plan.lanes),) + sends(plan)
    if leaving:
        outs += (exit_shape(plan, plan.segments // 2),)
    args = (part, u, w_out, scale) + tuple(got)
    return call(
        "outer", functools.partial(outer_kernel, plan, factor, leaving),
        outs,
        vm(len(args)),
        args,
        flops=40 << 20,
        moved=5 << 20,
    )


def leave_kernel(plan, y, got_core, *outs):
    x, z, v, s = place(plan)
    core, chip = lax.rem(v, 2), lax.div(v, 2)
    for (dx, dy), out in zip(chip_order(plan), outs, strict=True):
        at = chip_at(plan, x, chip, dx, dy)
        to_x = 1 - x if dx else x
        first = pl.multiple_of((2 * (at - to_x * (plan.vecs // 2)) + core) * plan.columns, plan.columns)
        for r in range(plan.own):
            out[0, r] = y[to_x * plan.own + r, pl.ds(first, plan.columns), :]
            out[1, r] = got_core[at, r]


def leave(plan, y, got_core):
    n = len(chip_order(plan))
    return call(
        "leave", functools.partial(leave_kernel, plan), (exit_shape(plan, 2),) * n, vm(2), (y, got_core), moved=4 << 20
    )


def arrive_kernel(plan, *refs):
    *gots, out = refs
    x, z, v, s = place(plan)
    core, chip = lax.rem(v, 2), lax.div(v, 2)
    for (dx, dy), got in zip(chip_order(plan), gots, strict=True):
        for other in range(2):
            seg = jnp.int32(0)
            for m in range(2):
                for at in range(plan.vecs):
                    source = plan.seg[m ^ dx, (at ^ other) ^ (2 * dy)]
                    seg = seg + jnp.where((x == m) & (v == at), source, 0)
            for r in range(plan.own):
                for p in range(plan.run):
                    to = pl.multiple_of((r * SPAN + column(plan, seg, p)) * plan.width, plan.width)
                    out[:, pl.ds(to, plan.width)] = got[other, r, :, p * plan.width : (p + 1) * plan.width]


def arrive(plan, gots):
    return call(
        "arrive", functools.partial(arrive_kernel, plan),
        shape(plan.columns, plan.blocks * plan.width),
        vm(len(gots)),
        tuple(gots),
        moved=2 << 20,
    )


def gram_pieces(plan):
    rows = plan.vectors // plan.meshes
    height = 8 if rows % 8 == 0 else rows
    return rows, height, rows // height


def image_kernel(plan, part, u, w_out, scale, got_0, got_1, got_2, got_3, y, mass, out):
    row = halo_terms(plan, u, w_out, got_0, got_1, got_2, got_3)
    stiff = jnp.zeros((plan.vectors, plan.vectors), F32)
    for i in range(plan.rows):
        values = finished_row(plan, i, part, scale, 1.0, row(i))
        image = jnp.concatenate([value.astype(BF16) for value in values], axis=1)
        stiff += dot_turned(image, y[i].astype(BF16))
    rows, height, count = gram_pieces(plan)
    both = (stiff, mass[...])
    for m in range(plan.meshes):
        for v in range(plan.vecs):
            lanes = slice(v * plan.columns, (v + 1) * plan.columns)
            out[m * plan.vecs + v] = jnp.concatenate(
                [g[m * rows + h * height : m * rows + (h + 1) * height, lanes] for g in both for h in range(count)],
                axis=1,
            )


def image(plan, part, u, w_out, scale, got, y, mass):
    rows, height, count = gram_pieces(plan)
    args = (part, u, w_out, scale) + tuple(got) + (y, mass)
    return call(
        "image", functools.partial(image_kernel, plan),
        shape(plan.meshes * plan.vecs, height, 2 * count * plan.columns),
        vm(len(args)),
        args,
        flops=50 << 20,
        moved=5 << 20,
    )


def sum_kernel(plan, got, stiff, mass):
    rows, height, count = gram_pieces(plan)
    total = jnp.sum(got[...], axis=0)
    for k, out in enumerate((stiff, mass)):
        for h in range(count):
            lo = (k * count + h) * plan.columns
            out[h * height : (h + 1) * height, :] = total[:, lo : lo + plan.columns]


def shards(plan, panel, orient, mass, diag, near, far):
    w = plan.width
    panel = panel.T
    orient, mass = orient.reshape(plan.blocks, w), mass.reshape(plan.blocks, w)
    scale_own, entering, own_entering, first = prepare(plan, panel, orient, mass, diag, near, far)
    own_diag, own_first, own_rest, rest = fetch(plan, diag, near, far)

    def half(m, v):
        return m ^ 1, v

    def spread(parts):
        found = []
        for (dx, dy), sent in zip(chip_order(plan), parts, strict=True):
            if dx or dy:
                sent = plan.swap(sent, lambda m, v, dx=dx, dy=dy: (m ^ dx, v ^ (2 * dy)))
            found.append(sent)
        return found

    first = plan.swap(first, half)
    parts = enter(plan, own_entering, plan.swap(entering, plan.core_swap))
    gots = spread(parts)
    first, rest, *gots = lax.optimization_barrier((first, rest, *gots))
    rest = plan.swap(rest, half)
    above = jnp.where(lax.axis_index("mesh") % 2 == 0, own_first, first[: plan.run + 1])
    pairs = [(m * plan.vecs + v, (m - 2) * plan.vecs + v) for m in range(2, plan.meshes) for v in range(plan.vecs)]
    below = lax.ppermute(above, BOTH, pairs)

    y, scale, *field = begin(plan, gots, scale_own, first)
    w_in, w_out = weights(plan, own_diag, own_first, own_rest, first, rest, below)

    def exchange(field):
        u, a, b, core, ring = field
        got = {
            "a": lambda: plan.swap(a, plan.layer_a),
            "b": lambda: plan.swap(b, plan.layer_b),
            "ring": lambda: plan.swap(ring, plan.ring_swap),
            "core": lambda: plan.swap(core, plan.core_swap),
        }
        return u, tuple(got[name]() for name in ORDER)

    for application in range(APPS):
        before = None
        for step in range(DEGREE):
            factors = (2.0 / RADIUS, -2.0 * CENTER / RADIUS, -1.0) if step else (1.0 / RADIUS, -CENTER / RADIUS, 0.0)
            u, halos = exchange(field)
            (part,) = inner(plan, factors, u, y, before, w_in, scale)
            leaving = application == APPS - 1 and step == DEGREE - 1
            new, *field = outer(plan, factors[0], part, u, w_out, scale, halos, leaving)
            before, y = y, new
    *field, exit_core = field
    u, halos = exchange(field)
    part, mass_gram = inner(plan, (1.0, 0.0, 0.0), u, y, None, w_in, scale, gram=True)
    got_core = plan.swap(exit_core, plan.core_swap)
    part, got_core = lax.optimization_barrier((part, got_core))
    kept = spread(leave(plan, y, got_core))
    grams = image(plan, part, u, w_out, scale, halos, y, mass_gram)
    grams = lax.all_to_all(grams, BOTH, 0, 0, tiled=True)
    rows = gram_pieces(plan)[0]
    stiff_gram, mass_gram = call(
        "sum", functools.partial(sum_kernel, plan), (shape(rows, plan.columns),) * 2, vm(1), (grams,), moved=1 << 17
    )
    filtered = arrive(plan, kept)
    return filtered.T, stiff_gram.T, mass_gram.T


def solution(mesh):
    placed = (P("mesh", "vec"), P("mesh"), P("mesh"), P("mesh"), P("mesh"), P("mesh"))

    def run(panel, orient, mass, diag, near, far):
        meshes, vecs = mesh.shape["mesh"], mesh.shape["vec"]
        plan = Plan(meshes, vecs, diag.shape[0] // meshes, diag.shape[1], panel.shape[1] // vecs)
        return jax.shard_map(
            functools.partial(shards, plan),
            mesh=mesh,
            in_specs=placed,
            out_specs=(P("mesh", "vec"), P("vec", "mesh"), P("vec", "mesh")),
            check_vma=False,
        )(panel, orient, mass, diag, near, far)

    return run
```

time: 150 us -> 111 us (0.74)
  waiting for transfers between devices: 54.7 us -> 30.5 us
  local copies, waits for them, and re-layouts: 13.2 us -> 0 us
  Pallas kernels: 24.8 us -> 20.8 us
  blocking collectives: 10.8 us -> 13.1 us
    ppermute x42 -> x46, waiting for transfers between devices: 50.2 us -> 26.5 us  [swap(): return lax.ppermute(x, BOTH, pairs)]
    unnamed x24 -> x0, local copies, waits for them, and re-layouts: 13.2 us -> none
    ppermute x42 -> x46, starting transfers between devices: 38.1 us -> 44.1 us  [swap(): return lax.ppermute(x, BOTH, pairs)]
    all_to_all x1 -> x0, starting transfers between devices: 5.3 us -> none  [shards(): lax.all_to_all(chunks, BOTH, 0, 0, tiled=True, axis_index_groups=groups)]
    pallas_call x24 -> x26, Pallas kernels: 24.8 us -> 20.8 us  [call(): pl.pallas_call(kernel, name=name, out_shape=outs, in_specs=ins, out_specs...]
    all_to_all x1, blocking collectives: 10.8 us -> 13.1 us  [shards(): grams = lax.all_to_all(grams, BOTH, 0, 0, tiled=True)]
  transfers between devices with their start and end apart: 44 -> 47, of which waited for: 17 -> 16; matrix products, arithmetic and copies ran while one was open for 0% -> 0% of each run, Pallas kernels for 9% -> 13%
where the time goes in v2:
time: 111 us
  starting transfers between devices  45.3 us (41%)
  waiting for transfers between devices  30.5 us (27%)
  Pallas kernels  20.8 us (19%)
  blocking collectives  13.1 us (12%)
    ppermute x46, starting transfers between devices, swap(): return lax.ppermute(x, BOTH, pairs)  44.1 us
    ppermute x46, waiting for transfers between devices, swap(): return lax.ppermute(x, BOTH, pairs)  26.5 us
    pallas_call x26, Pallas kernels, call(): pl.pallas_call(kernel, name=name, out_shape=outs, in_specs=ins, out_specs...  20.8 us
    all_to_all x1, blocking collectives, shards(): grams = lax.all_to_all(grams, BOTH, 0, 0, tiled=True)  13.1 us
    ppermute x1, waiting for transfers between devices, shards(): below = lax.ppermute(above, BOTH, pairs)  3.97 us
  transfers between devices with their start and end apart: 47, of which 16 were waited for; matrix products, arithmetic and copies ran while one was open for 0% of the time, Pallas kernels for 13%

profile of v2, /device:TPU:0, one launch (start us, length us, event | category | flops | bytes accessed | tf_op | source)
XLA Modules:
  0.0 110.7 jit_solution(12775093091014920798)
XLA Ops:
  0.6 1.7 %prepare.1 = (f32[64,128]{1,0:T(8,128)S(1)}, f32[4,2,32,512]{3,2,1,0:T(8,128)S(1)}, f32[4,2,32,512]{3,2,1,0:T(8,128)S(1)}, bf16[10,128,128]{2,1,0:T(8,128)(2,1)S(1)}) custom-call(f32[32,8192]{1,0:T(8,128)} %bitcast.6, s32[64,128]{1,0:T(8,128)} %bitcast.8, f32[64,128]{1,0:T(8,128)} %bitcast.9, bf16[64,128,128]{2,1,0:T(8,128)(2,1)} %diag.3, ...), custom_call_target="tpu_custom_call" | custom-call | bytes 4194304 | tf_op jit(solution)/shard_map/prepare/pallas_call | solution.py:132
  2.8 2.6 %collective-permute-start = (bf16[10,128,128]{2,1,0:T(8,128)(2,1)S(1)}, bf16[10,128,128]{2,1,0:T(8,128)(2,1)S(1)}, u32[]{:S(2)}, u32[]{:S(2)}) collective-permute-start(bf16[10,128,128]{2,1,0:T(8,128)(2,1)S(1)} %get-tuple-element.90), channel_id=1, source_target_pairs={{0,4},{1,5},{2,6},{3,7},{4,0},{5,1},{6,2},{7,3},{8,12},{9,13},{10,... | collective-permute-start | bytes 983048 | tf_op jit(solution)/shard_map/ppermute | solution.py:79
  6.2 1.8 %collective-permute-start.2 = (f32[2,2,32,512]{3,2,1,0:T(8,128)}, f32[2,2,32,512]{3,2,1,0:T(8,128)S(1)}, u32[]{:S(2)}, u32[]{:S(2)}) collective-permute-start(f32[2,2,32,512]{3,2,1,0:T(8,128)} %get-tuple-element.94), channel_id=1, source_target_pairs={{0,4},{1,5},{2,6},{3,7},{4,0},{5,1},{6,2},{7,3},{8,12},{9,13},{10,... | collective-permute-start | bytes 786440 | tf_op jit(solution)/shard_map/ppermute | solution.py:79
  9.7 1.6 %fetch.1 = (bf16[8,128,128]{2,1,0:T(8,128)(2,1)S(1)}, bf16[5,128,128]{2,1,0:T(8,128)(2,1)S(1)}, bf16[13,128,128]{2,1,0:T(8,128)(2,1)S(1)}, bf16[13,128,128]{2,1,0:T(8,128)(2,1)S(1)}) custom-call(bf16[64,128,128]{2,1,0:T(8,128)(2,1)} %diag.3, bf16[64,128,128]{2,1,0:T(8,128)(2,1)} %near.3, bf16[64,128,128]{2,1,0:T(8,128)(2,1)} %far.3), custom_call_target="tpu_custom_call" | custom-call | bytes 3145728 | tf_op jit(solution)/shard_map/fetch/pallas_call | solution.py:132
  11.3 2.7 %collective-permute-done.first = bf16[10,128,128]{2,1,0:T(8,128)(2,1)S(1)} collective-permute-done((bf16[10,128,128]{2,1,0:T(8,128)(2,1)S(1)}, bf16[10,128,128]{2,1,0:T(8,128)(2,1)S(1)}, u32[]{:S(2)}, u32[]{:S(2)}) %collective-permute-start) | collective-permute-done | bytes 327712 | tf_op jit(solution)/shard_map/ppermute | solution.py:79
  14.0 5.6 %collective-permute-done.2.refs_0_ = f32[2,2,32,512]{3,2,1,0:T(8,128)S(1)} collective-permute-done((f32[2,2,32,512]{3,2,1,0:T(8,128)}, f32[2,2,32,512]{3,2,1,0:T(8,128)S(1)}, u32[]{:S(2)}, u32[]{:S(2)}) %collective-permute-start.2) | collective-permute-done | bytes 262176 | tf_op jit(solution)/shard_map/ppermute | solution.py:79
  19.6 6.6 %collective-permute-done.3.refs_1_ = f32[2,2,32,512]{3,2,1,0:T(8,128)S(1)} collective-permute-done((f32[2,2,32,512]{3,2,1,0:T(8,128)S(1)}, f32[2,2,32,512]{3,2,1,0:T(8,128)S(1)}, u32[]{:S(2)}, u32[]{:S(2)}) %collective-permute-start.3) | collective-permute-done | bytes 262176 | tf_op jit(solution)/shard_map/ppermute | solution.py:79
  26.2 1.5 %collective-permute-start.5 = (bf16[13,128,128]{2,1,0:T(8,128)(2,1)S(1)}, bf16[13,128,128]{2,1,0:T(8,128)(2,1)S(1)}, u32[]{:S(2)}, u32[]{:S(2)}) collective-permute-start(bf16[13,128,128]{2,1,0:T(8,128)(2,1)S(1)} %get-tuple-element.108), channel_id=1, source_target_pairs={{0,4},{1,5},{2,6},{3,7},{4,0},{5,1},{6,2},{7,3},{8,12},{9,13},{10,... | collective-permute-start | bytes 1277960 | tf_op jit(solution)/shard_map/ppermute | solution.py:79
  29.8 2.6 %collective-permute-start.8 = (bf16[128,512]{1,0:T(8,128)(2,1)S(1)}, bf16[128,512]{1,0:T(8,128)(2,1)S(1)}, u32[]{:S(2)}, u32[]{:S(2)}) collective-permute-start(bf16[128,512]{1,0:T(8,128)(2,1)S(1)} %get-tuple-element.113), channel_id=1, source_target_pairs={{0,8},{1,9},{2,10},{3,11},{4,12},{5,13},{6,14},{7,15},{8,0},{9,1},... | collective-permute-start | bytes 393224 | tf_op jit(solution)/shard_map/ppermute | solution.py:79
  32.5 4.0 %collective-permute-done.6.below = bf16[5,128,128]{2,1,0:T(8,128)(2,1)S(1)} collective-permute-done((bf16[5,128,128]{2,1,0:T(8,128)(2,1)S(1)}, bf16[5,128,128]{2,1,0:T(8,128)(2,1)S(1)}, u32[]{:S(2)}, u32[]{:S(2)}) %collective-permute-start.6) | collective-permute-done | bytes 163872 | tf_op jit(solution)/shard_map/ppermute | solution.py:700
  39.8 1.6 %collective-permute-start.11 = (bf16[4,128,128]{2,1,0:T(8,128)(2,1)S(1)}, bf16[4,128,128]{2,1,0:T(8,128)(2,1)S(1)}, u32[]{:S(2)}, u32[]{:S(2)}) collective-permute-start(bf16[4,128,128]{2,1,0:T(8,128)(2,1)S(1)} %get-tuple-element.118), channel_id=1, source_target_pairs={{0,4},{1,3},{2,6},{3,1},{4,0},{5,7},{6,2},{7,5},{8,12},{9,11},{10,... | collective-permute-start | bytes 393224 | tf_op jit(solution)/shard_map/ppermute | solution.py:79
  41.3 1.6 %collective-permute-start.12 = (bf16[128,512]{1,0:T(8,128)(2,1)S(1)}, bf16[128,512]{1,0:T(8,128)(2,1)S(1)}, u32[]{:S(2)}, u32[]{:S(2)}) collective-permute-start(bf16[128,512]{1,0:T(8,128)(2,1)S(1)} %get-tuple-element.119), channel_id=1, source_target_pairs={{0,8},{1,9},{2,10},{3,11},{4,12},{5,13},{6,14},{7,15},{8,0},{9,1},... | collective-permute-start | bytes 393224 | tf_op jit(solution)/shard_map/ppermute | solution.py:79
  47.4 2.7 %collective-permute-start.16 = (bf16[128,512]{1,0:T(8,128)(2,1)S(1)}, bf16[128,512]{1,0:T(8,128)(2,1)S(1)}, u32[]{:S(2)}, u32[]{:S(2)}) collective-permute-start(bf16[128,512]{1,0:T(8,128)(2,1)S(1)} %get-tuple-element.125), channel_id=1, source_target_pairs={{0,8},{1,9},{2,10},{3,11},{4,12},{5,13},{6,14},{7,15},{8,0},{9,1},... | collective-permute-start | bytes 393224 | tf_op jit(solution)/shard_map/ppermute | solution.py:79
  53.5 1.6 %collective-permute-start.19 = (bf16[4,128,128]{2,1,0:T(8,128)(2,1)S(1)}, bf16[4,128,128]{2,1,0:T(8,128)(2,1)S(1)}, u32[]{:S(2)}, u32[]{:S(2)}) collective-permute-start(bf16[4,128,128]{2,1,0:T(8,128)(2,1)S(1)} %get-tuple-element.130), channel_id=1, source_target_pairs={{0,4},{1,3},{2,6},{3,1},{4,0},{5,7},{6,2},{7,5},{8,12},{9,11},{10,... | collective-permute-start | bytes 393224 | tf_op jit(solution)/shard_map/ppermute | solution.py:79
  55.1 2.0 %collective-permute-start.20 = (bf16[128,512]{1,0:T(8,128)(2,1)S(1)}, bf16[128,512]{1,0:T(8,128)(2,1)S(1)}, u32[]{:S(2)}, u32[]{:S(2)}) collective-permute-start(bf16[128,512]{1,0:T(8,128)(2,1)S(1)} %get-tuple-element.131), channel_id=1, source_target_pairs={{0,8},{1,9},{2,10},{3,11},{4,12},{5,13},{6,14},{7,15},{8,0},{9,1},... | collective-permute-start | bytes 393224 | tf_op jit(solution)/shard_map/ppermute | solution.py:79
  61.1 2.0 %collective-permute-start.24 = (bf16[128,512]{1,0:T(8,128)(2,1)S(1)}, bf16[128,512]{1,0:T(8,128)(2,1)S(1)}, u32[]{:S(2)}, u32[]{:S(2)}) collective-permute-start(bf16[128,512]{1,0:T(8,128)(2,1)S(1)} %get-tuple-element.137), channel_id=1, source_target_pairs={{0,8},{1,9},{2,10},{3,11},{4,12},{5,13},{6,14},{7,15},{8,0},{9,1},... | collective-permute-start | bytes 393224 | tf_op jit(solution)/shard_map/ppermute | solution.py:79
  66.6 1.6 %collective-permute-start.27 = (bf16[4,128,128]{2,1,0:T(8,128)(2,1)S(1)}, bf16[4,128,128]{2,1,0:T(8,128)(2,1)S(1)}, u32[]{:S(2)}, u32[]{:S(2)}) collective-permute-start(bf16[4,128,128]{2,1,0:T(8,128)(2,1)S(1)} %get-tuple-element.142), channel_id=1, source_target_pairs={{0,4},{1,3},{2,6},{3,1},{4,0},{5,7},{6,2},{7,5},{8,12},{9,11},{10,... | collective-permute-start | bytes 393224 | tf_op jit(solution)/shard_map/ppermute | solution.py:79
  68.2 2.0 %collective-permute-start.28 = (bf16[128,512]{1,0:T(8,128)(2,1)S(1)}, bf16[128,512]{1,0:T(8,128)(2,1)S(1)}, u32[]{:S(2)}, u32[]{:S(2)}) collective-permute-start(bf16[128,512]{1,0:T(8,128)(2,1)S(1)} %get-tuple-element.143), channel_id=1, source_target_pairs={{0,8},{1,9},{2,10},{3,11},{4,12},{5,13},{6,14},{7,15},{8,0},{9,1},... | collective-permute-start | bytes 393224 | tf_op jit(solution)/shard_map/ppermute | solution.py:79
  74.2 2.0 %collective-permute-start.32 = (bf16[128,512]{1,0:T(8,128)(2,1)S(1)}, bf16[128,512]{1,0:T(8,128)(2,1)S(1)}, u32[]{:S(2)}, u32[]{:S(2)}) collective-permute-start(bf16[128,512]{1,0:T(8,128)(2,1)S(1)} %get-tuple-element.149), channel_id=1, source_target_pairs={{0,8},{1,9},{2,10},{3,11},{4,12},{5,13},{6,14},{7,15},{8,0},{9,1},... | collective-permute-start | bytes 393224 | tf_op jit(solution)/shard_map/ppermute | solution.py:79
  79.7 1.6 %collective-permute-start.35 = (bf16[4,128,128]{2,1,0:T(8,128)(2,1)S(1)}, bf16[4,128,128]{2,1,0:T(8,128)(2,1)S(1)}, u32[]{:S(2)}, u32[]{:S(2)}) collective-permute-start(bf16[4,128,128]{2,1,0:T(8,128)(2,1)S(1)} %get-tuple-element.154), channel_id=1, source_target_pairs={{0,4},{1,3},{2,6},{3,1},{4,0},{5,7},{6,2},{7,5},{8,12},{9,11},{10,... | collective-permute-start | bytes 393224 | tf_op jit(solution)/shard_map/ppermute | solution.py:79
  81.2 2.0 %collective-permute-start.36 = (bf16[128,512]{1,0:T(8,128)(2,1)S(1)}, bf16[128,512]{1,0:T(8,128)(2,1)S(1)}, u32[]{:S(2)}, u32[]{:S(2)}) collective-permute-start(bf16[128,512]{1,0:T(8,128)(2,1)S(1)} %get-tuple-element.155), channel_id=1, source_target_pairs={{0,8},{1,9},{2,10},{3,11},{4,12},{5,13},{6,14},{7,15},{8,0},{9,1},... | collective-permute-start | bytes 393224 | tf_op jit(solution)/shard_map/ppermute | solution.py:79
  87.5 2.0 %collective-permute-start.44 = (bf16[128,512]{1,0:T(8,128)(2,1)S(1)}, bf16[128,512]{1,0:T(8,128)(2,1)S(1)}, u32[]{:S(2)}, u32[]{:S(2)}) collective-permute-start(bf16[128,512]{1,0:T(8,128)(2,1)S(1)} %get-tuple-element.169), channel_id=1, source_target_pairs={{0,8},{1,9},{2,10},{3,11},{4,12},{5,13},{6,14},{7,15},{8,0},{9,1},... | collective-permute-start | bytes 393224 | tf_op jit(solution)/shard_map/ppermute | solution.py:79
  91.3 1.6 %collective-permute-start.40 = (f32[2,2,32,512]{3,2,1,0:T(8,128)S(1)}, f32[2,2,32,512]{3,2,1,0:T(8,128)S(1)}, u32[]{:S(2)}, u32[]{:S(2)}) collective-permute-start(f32[2,2,32,512]{3,2,1,0:T(8,128)S(1)} %get-tuple-element.163), channel_id=1, source_target_pairs={{0,4},{1,5},{2,6},{3,7},{4,0},{5,1},{6,2},{7,3},{8,12},{9,13},{10,... | collective-permute-start | bytes 786440 | tf_op jit(solution)/shard_map/ppermute | solution.py:79
  95.7 13.1 %all_to_all.5.got = f32[32,8,128]{2,1,0:T(8,128)S(1)} all-to-all(f32[32,8,128]{2,1,0:T(8,128)S(1)} %image.1), channel_id=1, replica_groups=mesh['mesh'=8,'vec'=4] {'mesh','vec'}, dimensions={0} | all-to-all | bytes 262144 | tf_op jit(solution)/shard_map/all_to_all | solution.py:731
  (98 shorter events, 41.8 us)
Async XLA Ops:
  2.8 11.1 %collective-permute-start = (bf16[10,128,128]{2,1,0:T(8,128)(2,1)S(1)}, bf16[10,128,128]{2,1,0:T(8,128)(2,1)S(1)}, u32[]{:S(2)}, u32[]{:S(2)}) collective-permute-start(bf16[10,128,128]{2,1,0:T(8,128)(2,1)S(1)} %get-tuple-element.90), channel_id=1, source_target_pairs={{0,4},{1,5},{2,6},{3,7},{4,0},{5,1},{6,2},{7,3},{8,12},{9,13},{10,... | collective-permute-start | bytes 983048 | tf_op jit(solution)/shard_map/ppermute | solution.py:79
  6.2 13.4 %collective-permute-start.2 = (f32[2,2,32,512]{3,2,1,0:T(8,128)}, f32[2,2,32,512]{3,2,1,0:T(8,128)S(1)}, u32[]{:S(2)}, u32[]{:S(2)}) collective-permute-start(f32[2,2,32,512]{3,2,1,0:T(8,128)} %get-tuple-element.94), channel_id=1, source_target_pairs={{0,4},{1,5},{2,6},{3,7},{4,0},{5,1},{6,2},{7,3},{8,12},{9,13},{10,... | collective-permute-start | bytes 786440 | tf_op jit(solution)/shard_map/ppermute | solution.py:79
  8.0 18.2 %collective-permute-start.3 = (f32[2,2,32,512]{3,2,1,0:T(8,128)S(1)}, f32[2,2,32,512]{3,2,1,0:T(8,128)S(1)}, u32[]{:S(2)}, u32[]{:S(2)}) collective-permute-start(f32[2,2,32,512]{3,2,1,0:T(8,128)S(1)} %get-tuple-element.95), channel_id=1, source_target_pairs={{0,6},{1,7},{2,4},{3,5},{4,2},{5,3},{6,0},{7,1},{8,14},{9,15},{10,... | collective-permute-start | bytes 786440 | tf_op jit(solution)/shard_map/ppermute | solution.py:79
  9.5 16.7 %collective-permute-start.4 = (f32[2,2,32,512]{3,2,1,0:T(8,128)S(1)}, f32[2,2,32,512]{3,2,1,0:T(8,128)S(1)}, u32[]{:S(2)}, u32[]{:S(2)}) collective-permute-start(f32[2,2,32,512]{3,2,1,0:T(8,128)S(1)} %get-tuple-element.97), channel_id=1, source_target_pairs={{0,2},{1,3},{2,0},{3,1},{4,6},{5,7},{6,4},{7,5},{8,10},{9,11},{10,... | collective-permute-start | bytes 786440 | tf_op jit(solution)/shard_map/ppermute | solution.py:79
  26.2 11.4 %collective-permute-start.5 = (bf16[13,128,128]{2,1,0:T(8,128)(2,1)S(1)}, bf16[13,128,128]{2,1,0:T(8,128)(2,1)S(1)}, u32[]{:S(2)}, u32[]{:S(2)}) collective-permute-start(bf16[13,128,128]{2,1,0:T(8,128)(2,1)S(1)} %get-tuple-element.108), channel_id=1, source_target_pairs={{0,4},{1,5},{2,6},{3,7},{4,0},{5,1},{6,2},{7,3},{8,12},{9,13},{10,... | collective-permute-start | bytes 1277960 | tf_op jit(solution)/shard_map/ppermute | solution.py:79
  27.7 8.8 %collective-permute-start.6 = (bf16[5,128,128]{2,1,0:T(8,128)(2,1)S(1)}, bf16[5,128,128]{2,1,0:T(8,128)(2,1)S(1)}, u32[]{:S(2)}, u32[]{:S(2)}) collective-permute-start(bf16[5,128,128]{2,1,0:T(8,128)(2,1)S(1)} %slice_select_fusion), channel_id=1, source_target_pairs={{8,0},{9,1},{10,2},{11,3},{12,4},{13,5},{14,6},{15,7},{16,8},{17,9... | collective-permute-start | bytes 491528 | tf_op jit(solution)/shard_map/ppermute | solution.py:700
  29.2 10.0 %collective-permute-start.7 = (bf16[4,128,128]{2,1,0:T(8,128)(2,1)S(1)}, bf16[4,128,128]{2,1,0:T(8,128)(2,1)S(1)}, u32[]{:S(2)}, u32[]{:S(2)}) collective-permute-start(bf16[4,128,128]{2,1,0:T(8,128)(2,1)S(1)} %get-tuple-element.112), channel_id=1, source_target_pairs={{0,4},{1,3},{2,6},{3,1},{4,0},{5,7},{6,2},{7,5},{8,12},{9,11},{10,... | collective-permute-start | bytes 393224 | tf_op jit(solution)/shard_map/ppermute | solution.py:79
  29.8 9.4 %collective-permute-start.8 = (bf16[128,512]{1,0:T(8,128)(2,1)S(1)}, bf16[128,512]{1,0:T(8,128)(2,1)S(1)}, u32[]{:S(2)}, u32[]{:S(2)}) collective-permute-start(bf16[128,512]{1,0:T(8,128)(2,1)S(1)} %get-tuple-element.113), channel_id=1, source_target_pairs={{0,8},{1,9},{2,10},{3,11},{4,12},{5,13},{6,14},{7,15},{8,0},{9,1},... | collective-permute-start | bytes 393224 | tf_op jit(solution)/shard_map/ppermute | solution.py:79
  32.5 6.8 %collective-permute-start.9 = (bf16[128,512]{1,0:T(8,128)(2,1)S(1)}, bf16[128,512]{1,0:T(8,128)(2,1)S(1)}, u32[]{:S(2)}, u32[]{:S(2)}) collective-permute-start(bf16[128,512]{1,0:T(8,128)(2,1)S(1)} %get-tuple-element.114), channel_id=1, source_target_pairs={{0,1},{1,0},{2,3},{3,2},{4,5},{5,4},{6,7},{7,6},{8,16},{9,17},{10,... | collective-permute-start | bytes 393224 | tf_op jit(solution)/shard_map/ppermute | solution.py:79
  39.8 5.0 %collective-permute-start.11 = (bf16[4,128,128]{2,1,0:T(8,128)(2,1)S(1)}, bf16[4,128,128]{2,1,0:T(8,128)(2,1)S(1)}, u32[]{:S(2)}, u32[]{:S(2)}) collective-permute-start(bf16[4,128,128]{2,1,0:T(8,128)(2,1)S(1)} %get-tuple-element.118), channel_id=1, source_target_pairs={{0,4},{1,3},{2,6},{3,1},{4,0},{5,7},{6,2},{7,5},{8,12},{9,11},{10,... | collective-permute-start | bytes 393224 | tf_op jit(solution)/shard_map/ppermute | solution.py:79
  46.8 5.0 %collective-permute-start.15 = (bf16[4,128,128]{2,1,0:T(8,128)(2,1)S(1)}, bf16[4,128,128]{2,1,0:T(8,128)(2,1)S(1)}, u32[]{:S(2)}, u32[]{:S(2)}) collective-permute-start(bf16[4,128,128]{2,1,0:T(8,128)(2,1)S(1)} %get-tuple-element.124), channel_id=1, source_target_pairs={{0,4},{1,3},{2,6},{3,1},{4,0},{5,7},{6,2},{7,5},{8,12},{9,11},{10,... | collective-permute-start | bytes 393224 | tf_op jit(solution)/shard_map/ppermute | solution.py:79
  47.4 5.6 %collective-permute-start.16 = (bf16[128,512]{1,0:T(8,128)(2,1)S(1)}, bf16[128,512]{1,0:T(8,128)(2,1)S(1)}, u32[]{:S(2)}, u32[]{:S(2)}) collective-permute-start(bf16[128,512]{1,0:T(8,128)(2,1)S(1)} %get-tuple-element.125), channel_id=1, source_target_pairs={{0,8},{1,9},{2,10},{3,11},{4,12},{5,13},{6,14},{7,15},{8,0},{9,1},... | collective-permute-start | bytes 393224 | tf_op jit(solution)/shard_map/ppermute | solution.py:79
  53.5 5.1 %collective-permute-start.19 = (bf16[4,128,128]{2,1,0:T(8,128)(2,1)S(1)}, bf16[4,128,128]{2,1,0:T(8,128)(2,1)S(1)}, u32[]{:S(2)}, u32[]{:S(2)}) collective-permute-start(bf16[4,128,128]{2,1,0:T(8,128)(2,1)S(1)} %get-tuple-element.130), channel_id=1, source_target_pairs={{0,4},{1,3},{2,6},{3,1},{4,0},{5,7},{6,2},{7,5},{8,12},{9,11},{10,... | collective-permute-start | bytes 393224 | tf_op jit(solution)/shard_map/ppermute | solution.py:79
  60.5 5.0 %collective-permute-start.23 = (bf16[4,128,128]{2,1,0:T(8,128)(2,1)S(1)}, bf16[4,128,128]{2,1,0:T(8,128)(2,1)S(1)}, u32[]{:S(2)}, u32[]{:S(2)}) collective-permute-start(bf16[4,128,128]{2,1,0:T(8,128)(2,1)S(1)} %get-tuple-element.136), channel_id=1, source_target_pairs={{0,4},{1,3},{2,6},{3,1},{4,0},{5,7},{6,2},{7,5},{8,12},{9,11},{10,... | collective-permute-start | bytes 393224 | tf_op jit(solution)/shard_map/ppermute | solution.py:79
  66.6 5.1 %collective-permute-start.27 = (bf16[4,128,128]{2,1,0:T(8,128)(2,1)S(1)}, bf16[4,128,128]{2,1,0:T(8,128)(2,1)S(1)}, u32[]{:S(2)}, u32[]{:S(2)}) collective-permute-start(bf16[4,128,128]{2,1,0:T(8,128)(2,1)S(1)} %get-tuple-element.142), channel_id=1, source_target_pairs={{0,4},{1,3},{2,6},{3,1},{4,0},{5,7},{6,2},{7,5},{8,12},{9,11},{10,... | collective-permute-start | bytes 393224 | tf_op jit(solution)/shard_map/ppermute | solution.py:79
  73.6 5.0 %collective-permute-start.31 = (bf16[4,128,128]{2,1,0:T(8,128)(2,1)S(1)}, bf16[4,128,128]{2,1,0:T(8,128)(2,1)S(1)}, u32[]{:S(2)}, u32[]{:S(2)}) collective-permute-start(bf16[4,128,128]{2,1,0:T(8,128)(2,1)S(1)} %get-tuple-element.148), channel_id=1, source_target_pairs={{0,4},{1,3},{2,6},{3,1},{4,0},{5,7},{6,2},{7,5},{8,12},{9,11},{10,... | collective-permute-start | bytes 393224 | tf_op jit(solution)/shard_map/ppermute | solution.py:79
  79.7 5.1 %collective-permute-start.35 = (bf16[4,128,128]{2,1,0:T(8,128)(2,1)S(1)}, bf16[4,128,128]{2,1,0:T(8,128)(2,1)S(1)}, u32[]{:S(2)}, u32[]{:S(2)}) collective-permute-start(bf16[4,128,128]{2,1,0:T(8,128)(2,1)S(1)} %get-tuple-element.154), channel_id=1, source_target_pairs={{0,4},{1,3},{2,6},{3,1},{4,0},{5,7},{6,2},{7,5},{8,12},{9,11},{10,... | collective-permute-start | bytes 393224 | tf_op jit(solution)/shard_map/ppermute | solution.py:79
  86.9 5.9 %collective-permute-start.43 = (bf16[4,128,128]{2,1,0:T(8,128)(2,1)S(1)}, bf16[4,128,128]{2,1,0:T(8,128)(2,1)S(1)}, u32[]{:S(2)}, u32[]{:S(2)}) collective-permute-start(bf16[4,128,128]{2,1,0:T(8,128)(2,1)S(1)} %get-tuple-element.168), channel_id=1, source_target_pairs={{0,4},{1,3},{2,6},{3,1},{4,0},{5,7},{6,2},{7,5},{8,12},{9,11},{10,... | collective-permute-start | bytes 393224 | tf_op jit(solution)/shard_map/ppermute | solution.py:79
  87.5 6.2 %collective-permute-start.44 = (bf16[128,512]{1,0:T(8,128)(2,1)S(1)}, bf16[128,512]{1,0:T(8,128)(2,1)S(1)}, u32[]{:S(2)}, u32[]{:S(2)}) collective-permute-start(bf16[128,512]{1,0:T(8,128)(2,1)S(1)} %get-tuple-element.169), channel_id=1, source_target_pairs={{0,8},{1,9},{2,10},{3,11},{4,12},{5,13},{6,14},{7,15},{8,0},{9,1},... | collective-permute-start | bytes 393224 | tf_op jit(solution)/shard_map/ppermute | solution.py:79
  89.6 5.3 %collective-permute-start.45 = (bf16[128,512]{1,0:T(8,128)(2,1)S(1)}, bf16[128,512]{1,0:T(8,128)(2,1)S(1)}, u32[]{:S(2)}, u32[]{:S(2)}) collective-permute-start(bf16[128,512]{1,0:T(8,128)(2,1)S(1)} %get-tuple-element.170), channel_id=1, source_target_pairs={{0,1},{1,0},{2,3},{3,2},{4,5},{5,4},{6,7},{7,6},{8,16},{9,17},{10,... | collective-permute-start | bytes 393224 | tf_op jit(solution)/shard_map/ppermute | solution.py:79
  89.6 5.3 %collective-permute-start.46 = (bf16[4,128,128]{2,1,0:T(8,128)(2,1)S(1)}, bf16[4,128,128]{2,1,0:T(8,128)(2,1)S(1)}, u32[]{:S(2)}, u32[]{:S(2)}) collective-permute-start(bf16[4,128,128]{2,1,0:T(8,128)(2,1)S(1)} %get-tuple-element.171), channel_id=1, source_target_pairs={{0,1},{1,0},{2,3},{3,2},{4,5},{5,4},{6,7},{7,6},{8,9},{9,8},{10,11... | collective-permute-start | bytes 393224 | tf_op jit(solution)/shard_map/ppermute | solution.py:79
  91.3 18.2 %collective-permute-start.40 = (f32[2,2,32,512]{3,2,1,0:T(8,128)S(1)}, f32[2,2,32,512]{3,2,1,0:T(8,128)S(1)}, u32[]{:S(2)}, u32[]{:S(2)}) collective-permute-start(f32[2,2,32,512]{3,2,1,0:T(8,128)S(1)} %get-tuple-element.163), channel_id=1, source_target_pairs={{0,4},{1,5},{2,6},{3,7},{4,0},{5,1},{6,2},{7,3},{8,12},{9,13},{10,... | collective-permute-start | bytes 786440 | tf_op jit(solution)/shard_map/ppermute | solution.py:79
  92.9 16.7 %collective-permute-start.41 = (f32[2,2,32,512]{3,2,1,0:T(8,128)S(1)}, f32[2,2,32,512]{3,2,1,0:T(8,128)S(1)}, u32[]{:S(2)}, u32[]{:S(2)}) collective-permute-start(f32[2,2,32,512]{3,2,1,0:T(8,128)S(1)} %get-tuple-element.164), channel_id=1, source_target_pairs={{0,6},{1,7},{2,4},{3,5},{4,2},{5,3},{6,0},{7,1},{8,14},{9,15},{10,... | collective-permute-start | bytes 786440 | tf_op jit(solution)/shard_map/ppermute | solution.py:79
  93.7 15.9 %collective-permute-start.42 = (f32[2,2,32,512]{3,2,1,0:T(8,128)S(1)}, f32[2,2,32,512]{3,2,1,0:T(8,128)S(1)}, u32[]{:S(2)}, u32[]{:S(2)}) collective-permute-start(f32[2,2,32,512]{3,2,1,0:T(8,128)S(1)} %get-tuple-element.166), channel_id=1, source_target_pairs={{0,2},{1,3},{2,0},{3,1},{4,6},{5,7},{6,4},{7,5},{8,10},{9,11},{10,... | collective-permute-start | bytes 786440 | tf_op jit(solution)/shard_map/ppermute | solution.py:79
  (23 other events, 82.3 us)

commit v3 on v2

--- a/solution.py
+++ b/solution.py
@@ -37,38 +37,27 @@
         self.half = self.run // 2
         self.lanes = self.run * width
         self.vectors = vecs * columns
-        self.inner, self.outer = {}, {}
-        for i in range(self.rows):
+        self.count = self.own * self.run
+        self.first, self.rest, self.near = {("N", 0, self.half): 0}, {}, {}
+        for p in range(self.run):
+            self.first["F", 0, p] = len(self.first)
+        for p in range(self.run + 1):
+            self.first.setdefault(("N", 0, p), len(self.first))
+        for r in range(1, self.own):
+            for p in range(self.run + 1):
+                self.near["N", r, p] = len(self.near)
             for p in range(self.run):
-                self.inner["D", i, p] = len(self.inner)
-        for i in range(self.rows):
-            for p in range(1, self.run):
-                self.inner["N", i, p] = len(self.inner)
-        for i in range(1, self.rows):
-            for p in range(self.run):
-                self.inner["F", i, p] = len(self.inner)
+                self.rest["F", r, p] = len(self.rest)
+        self.aux = len(self.first)
+        self.n_rest = len(self.rest) + self.count // 2
+        self.outer = {}
         for p in range(self.run):
             self.outer["F", 0, p] = len(self.outer)
-        for p in range(self.run):
-            self.outer["F", self.rows, p] = len(self.outer)
         for i in range(self.rows):
             self.outer["N", i, 0] = len(self.outer)
             self.outer["N", i, self.run] = len(self.outer)
-        for i in (0, self.rows - 1, self.rows):
+        for i in (0, self.rows - 1):
             self.outer["N", i, self.half] = len(self.outer)
-        self.count = self.own * self.run
-        self.aux = self.run + 1
-        self.n_first = self.aux + 1 + self.count // 2
-        self.n_rest = self.own * (self.run + 1) - 1 + (self.own - 1) * self.run
-
-    def received(self, kind, r, p):
-        if kind == "N":
-            if r == 0 and p == self.half:
-                return 0, self.run
-            return 1, r * (self.run + 1) + p - (r > 0 or p > self.half)
-        if r == 0:
-            return 0, p
-        return 1, self.own * (self.run + 1) - 1 + (r - 1) * self.run + p
 
     def swap(self, x, partner):
         pairs = []
@@ -201,8 +190,8 @@
     copies.start(orient, signs)
     copies.start(mass, masses)
     for r in range(plan.own):
-        for p in range(plan.run):
-            copies.start(block_of(plan, diag, other, r, p), blocks.at[r * plan.run + p])
+        for p in range(1, plan.run, 2):
+            copies.start(block_of(plan, diag, other, r, p), blocks.at[(r * plan.run + p) // 2])
     for d in range(plan.segments):
         chip, at_core = divmod(d, 2)
         seg = plan.seg[d // plan.vecs, d % plan.vecs]
@@ -211,9 +200,8 @@
                 src = panel.at[:, pl.ds((r * SPAN + j) * plan.width, n * plan.width)]
                 lanes = pl.ds(p * plan.width, n * plan.width)
                 copies.start_one(core == at_core, src, own_enter.at[chip, r, :, lanes], enter.at[chip, r, :, lanes])
-    for p in range(plan.run):
-        copies.start(block_of(plan, far, other, 0, p), first.at[p])
-    copies.start(block_of(plan, near, other, 0, plan.half), first.at[plan.run])
+    for (kind, r, p), at in plan.first.items():
+        copies.start(block_of(plan, near if kind == "N" else far, other, r, p), first.at[at])
     copies.wait(0, 2)
     scale[...] = signs[...].astype(F32) * lax.rsqrt(masses[...])
     parts[...] = jnp.zeros_like(parts)
@@ -225,68 +213,85 @@
                 at = part * plan.count + r * plan.run + p
                 parts[at : at + 1, :] = rounded
                 value = value - rounded
-    copies.wait(2, 2 + plan.count)
-    keep, line = upper(plan.width), on_diagonal(plan.width)
+    copies.wait(2, 2 + plan.count // 2)
+    line = on_diagonal(plan.width)
     for k in range(plan.count // 2):
-        one, two = blocks[2 * k].astype(F32), blocks[2 * k + 1].astype(F32)
-        first[plan.aux + 1 + k] = jnp.where(keep, one, two).astype(BF16)
         at = 3 * plan.count + k
-        parts[at : at + 1, :] = jnp.sum(jnp.where(line, two, 0.0), axis=0, keepdims=True)
+        parts[at : at + 1, :] = jnp.sum(jnp.where(line, blocks[k].astype(F32), 0.0), axis=0, keepdims=True)
     first[plan.aux] = parts[...].astype(BF16)
-    copies.wait(2 + plan.count)
+    copies.wait(2 + plan.count // 2)
 
 
 def prepare(plan, panel, orient, mass, diag, near, far):
     w = plan.width
-    n_copies = 2 + plan.count + plan.run + 1
+    n_copies = 2 + plan.count // 2 + len(plan.first)
     n_copies += plan.own * sum(len(pieces(plan, seg)) for seg in range(plan.segments))
     args = [pltpu.with_memory_space_constraint(a, pltpu.HBM) for a in (panel, orient, mass, diag, near, far)]
     entering = shape(plan.segments // 2, plan.own, plan.columns, plan.lanes)
     return call(
         "prepare",
         functools.partial(prepare_kernel, plan),
-        (shape(plan.blocks, w), entering, entering, shape(plan.n_first, w, w, dtype=BF16)),
+        (shape(plan.blocks, w), entering, entering, shape(plan.aux + 1, w, w, dtype=BF16)),
         in_hbm(6),
         args,
         [
             pltpu.VMEM((plan.blocks, w), orient.dtype),
             pltpu.VMEM((plan.blocks, w), F32),
-            pltpu.VMEM((plan.count, w, w), BF16),
+            pltpu.VMEM((plan.count // 2, w, w), BF16),
             pltpu.VMEM((w, w), F32),
             pltpu.SemaphoreType.DMA((n_copies,)),
         ],
-        moved=4 << 20,
+        moved=3 << 20,
     )
 
 
-def fetch_kernel(plan, diag, near, far, own_diag, own_first, own_rest, rest, sems):
-    x, z, v, s = place(plan)
+def turned(block):
+    return block.astype(F32).T.astype(BF16)
+
+
+def fetch_kernel(plan, diag, near, far, own_first, own_near, own_rest, others, rest, near_turned, far_turned, blocks, sems):
+    x, z, v, s = place(plan)
+    other = plan.segments - 1 - s
     copies = Copies(sems)
-    for seg, heads, tail in ((plan.segments - 1 - s, None, rest), (s, own_first, own_rest)):
-        for kind, src in (("N", near), ("F", far)):
-            for r in range(plan.own):
-                for p in range(plan.run + (kind == "N")):
-                    which, at = plan.received(kind, r, p)
-                    if which == 1:
-                        copies.start(block_of(plan, src, seg, r, p), tail.at[at])
-                    elif heads is not None:
-                        copies.start(block_of(plan, src, seg, r, p), heads.at[at])
     for r in range(plan.own):
         for p in range(plan.run):
-            copies.start(block_of(plan, diag, s, r, p), own_diag.at[r * plan.run + p])
-    copies.wait()
+            copies.start(block_of(plan, diag, other, r, p), blocks.at[r * plan.run + p])
+    for src, table, theirs, mine in ((near, plan.near, others, own_near), (far, plan.rest, rest, own_rest)):
+        for (_, r, p), at in table.items():
+            copies.start(block_of(plan, src, other, r, p), theirs.at[at])
+            copies.start(block_of(plan, src, s, r, p), mine.at[at])
+    for (kind, r, p), at in plan.first.items():
+        copies.start(block_of(plan, near if kind == "N" else far, s, r, p), own_first.at[at])
+    for r in range(plan.own):
+        for p in range(plan.run):
+            copies.start(block_of(plan, diag, s, r, p), own_rest.at[len(plan.rest) + r * plan.run + p])
+    copies.wait(0, plan.count)
+    keep = upper(plan.width)
+    for k in range(plan.count // 2):
+        one, two = blocks[2 * k].astype(F32), blocks[2 * k + 1].astype(F32)
+        rest[len(plan.rest) + k] = jnp.where(keep, one, two).astype(BF16)
+    copies.wait(plan.count)
+    for r in range(plan.own):
+        for p in range(plan.run):
+            n, f = ("N", r, p), ("F", r, p)
+            near_turned[r * plan.run + p] = turned(own_near[plan.near[n]] if r else own_first[plan.first[n]])
+            far_turned[r * plan.run + p] = turned(own_rest[plan.rest[f]] if r else own_first[plan.first[f]])
 
 
 def fetch(plan, diag, near, far):
     w = plan.width
     args = [pltpu.with_memory_space_constraint(a, pltpu.HBM) for a in (diag, near, far)]
+    n_near, n_own = len(plan.near), len(plan.rest) + plan.count
     return call(
         "fetch",
         functools.partial(fetch_kernel, plan),
-        tuple(shape(n, w, w, dtype=BF16) for n in (plan.count, plan.run + 1, plan.n_rest, plan.n_rest)),
+        tuple(shape(n, w, w, dtype=BF16) for n in (len(plan.first), n_near, n_own, n_near, plan.n_rest, plan.count, plan.count)),
         in_hbm(3),
         args,
-        [pltpu.SemaphoreType.DMA((2 * plan.n_rest + plan.run + 1 + plan.count,))],
+        [
+            pltpu.VMEM((plan.count, w, w), BF16),
+            pltpu.SemaphoreType.DMA((plan.count + 2 * n_near + len(plan.rest) + len(plan.first) + n_own,)),
+        ],
         moved=3 << 20,
     )
 
@@ -386,90 +391,120 @@
     )
 
 
-def weights_kernel(plan, own_diag, own_first, own_rest, first, rest, below, inner, outer):
+def late_kernel(
+    plan, own_first, own_near, own_rest, first, others, rest, near_turned, far_turned, pairs, middle, ends, spans, outer
+):
     x, _, _, _ = place(plan)
-    keep, line = upper(plan.width), on_diagonal(plan.width)
-    lines = first[plan.aux].astype(F32)
+    w, last = plan.width, plan.rows - 1
+    keep, line = upper(w), on_diagonal(w)
+    diagonals = first[plan.aux].astype(F32)
+    theirs = []
     for k in range(plan.count // 2):
-        both = first[plan.aux + 1 + k].astype(F32)
-        turned = both.T
+        both = rest[len(plan.rest) + k].astype(F32)
+        flipped = both.T
         at = 3 * plan.count + k
-        found = jnp.where(keep, both, turned), jnp.where(line, lines[at : at + 1], jnp.where(keep, turned, both))
-        for at, value in zip((2 * k, 2 * k + 1), found, strict=True):
-            r, p = divmod(at, plan.run)
-            value = value.astype(BF16)
-            for half in range(2):
-                mine, theirs = plan.inner["D", half * plan.own + r, p], plan.inner["D", (1 - half) * plan.own + r, p]
-
-                @pl.when(x == half)
-                def _():
-                    inner[mine] = own_diag[at]
-                    inner[theirs] = value
-
+        theirs.append(jnp.where(keep, both, flipped).astype(BF16))
+        theirs.append(jnp.where(line, diagonals[at : at + 1], jnp.where(keep, flipped, both)).astype(BF16))
+    lo, hi = slice(0, w), slice(w, 2 * w)
     for half in range(2):
 
         @pl.when(x == half)
         def _():
-            for table, out in ((plan.inner, inner), (plan.outer, outer)):
-                for (kind, i, p), k in table.items():
-                    if i == plan.rows:
-                        out[k] = below[p if kind == "F" else plan.run]
-                    elif kind != "D":
-                        group, r = divmod(i, plan.own)
-                        which, index = plan.received(kind, r, p)
-                        source = (own_first, own_rest) if group == half else (first, rest)
-                        out[k] = source[which][index]
-
-
-def weights(plan, own_diag, own_first, own_rest, first, rest, below):
+            for i in range(plan.rows):
+                group, r = divmod(i, plan.own)
+                mine = group == half
+
+                def block(kind, p):
+                    key = kind, r, p
+                    if r == 0:
+                        return (own_first if mine else first)[plan.first[key]]
+                    if kind == "N":
+                        return (own_near if mine else others)[plan.near[key]]
+                    return (own_rest if mine else rest)[plan.rest[key]]
+
+                outer[plan.outer["N", i, plan.run]] = block("N", plan.run)
+                for p in range(plan.run):
+                    at, k, q = i * plan.run + p, (i * plan.run + p) // 2, p % 2
+                    own = own_rest[len(plan.rest) + r * plan.run + p] if mine else theirs[r * plan.run + p]
+                    pairs[k, (lo, hi)[q], (lo, hi)[q]] = own
+                    near = block("N", p)
+                    near_flipped = near_turned[r * plan.run + p] if mine else turned(near)
+                    if q:
+                        pairs[k, lo, hi] = near_flipped
+                        pairs[k, hi, lo] = near
+                    if p == 0:
+                        outer[plan.outer["N", i, 0]] = near_flipped
+                    if p == plan.half:
+                        spans[i] = near_flipped
+                        spans[plan.rows + i] = near
+                        if i == 0:
+                            outer[plan.outer["N", 0, p]] = near_flipped
+                        if i == last:
+                            outer[plan.outer["N", last, p]] = near
+                    far = block("F", p)
+                    far_flipped = far_turned[r * plan.run + p] if mine else turned(far)
+                    if i == 0:
+                        outer[plan.outer["F", 0, p]] = far_flipped
+                    elif i == last:
+                        ends[plan.run + p] = far_flipped
+                    else:
+                        middle[at - plan.run, lo] = far_flipped
+                    if i == 1:
+                        ends[p] = far
+                    elif i > 1:
+                        middle[at - 2 * plan.run, hi] = far
+
+
+def late(plan, *args):
     w = plan.width
     return call(
-        "weights",
-        functools.partial(weights_kernel, plan),
-        (shape(len(plan.inner), w, w, dtype=BF16), shape(len(plan.outer), w, w, dtype=BF16)),
-        vm(6),
-        (own_diag, own_first, own_rest, first, rest, below),
+        "late",
+        functools.partial(late_kernel, plan),
+        (
+            shape(plan.rows * plan.run // 2, 2 * w, 2 * w, dtype=BF16),
+            shape((plan.rows - 2) * plan.run, 2 * w, w, dtype=BF16),
+            shape(2 * plan.run, w, w, dtype=BF16),
+            shape(2 * plan.rows, w, w, dtype=BF16),
+            shape(len(plan.outer), w, w, dtype=BF16),
+        ),
+        vm(len(args)),
+        args,
         moved=4 << 20,
     )
 
 
-def inner_kernel(plan, factors, has_before, gram, *refs):
+def inner_kernel(plan, factors, has_before, gram, u, y, pairs, middle, ends, spans, scale, *refs):
     a, b, c = factors
-    refs = list(refs)
-    u, y = refs[:2]
-    before = refs[2] if has_before else None
-    w_in, scale, part = refs[2 + has_before : 5 + has_before]
+    before = refs[0] if has_before else None
+    part = refs[has_before]
     x, z, v, s = place(plan)
     wrap = (s == 0).astype(jnp.int32)
     width, half, last = plan.width, plan.half, plan.rows - 1
-    at = plan.inner
     for i in range(plan.rows):
-        for p in range(plan.run):
-            lanes = slice(p * width, (p + 1) * width)
-            total = dot(u[i, :, lanes], w_in[at["D", i, p]])
-            if p == half:
-                if i > 0:
-                    total += dot_turned(u[i - wrap, :, (p - 1) * width : p * width], w_in[at["N", i, p]])
-            elif p > 0:
-                total += dot_turned(u[i, :, (p - 1) * width : p * width], w_in[at["N", i, p]])
-            if p + 1 == half:
-                if i < last:
-                    near = at["N", i, half] + wrap * (plan.run - 1)
-                    total += dot(u[i + wrap, :, (p + 1) * width : (p + 2) * width], w_in[near])
-            elif p + 1 < plan.run:
-                total += dot(u[i, :, (p + 1) * width : (p + 2) * width], w_in[at["N", i, p + 1]])
-            if i > 0:
-                total += dot_turned(u[i - 1, :, lanes], w_in[at["F", i, p]])
-            if i < last:
-                total += dot(u[i + 1, :, lanes], w_in[at["F", i + 1, p]])
-            result = (a * scale[pl.ds(i * plan.run + p, 1), :]) * total
-            if b:
-                result += b * y[i, :, lanes]
-            if has_before:
-                result += c * before[i, :, lanes]
-            part[i, :, lanes] = result
+        for k in range(plan.run // 2):
+            two = dot(u[i, :, 2 * k * width : (2 * k + 2) * width], pairs[i * plan.run // 2 + k])
+            for p in (2 * k, 2 * k + 1):
+                lanes = slice(p * width, (p + 1) * width)
+                total = two[:, (p % 2) * width : (p % 2 + 1) * width]
+                if i == 0:
+                    total += dot(u[1, :, lanes], ends[p])
+                elif i == last:
+                    total += dot(u[last - 1, :, lanes], ends[plan.run + p])
+                else:
+                    around = jnp.concatenate([u[i - 1, :, lanes], u[i + 1, :, lanes]], axis=1)
+                    total += dot(around, middle[(i - 1) * plan.run + p])
+                if p == half and i > 0:
+                    total += dot(u[i - wrap, :, (half - 1) * width : half * width], spans[i])
+                if p == half - 1 and i < last:
+                    total += dot(u[i + wrap, :, half * width : (half + 1) * width], spans[plan.rows + i + wrap])
+                result = (a * scale[pl.ds(i * plan.run + p, 1), :]) * total
+                if b:
+                    result += b * y[i, :, lanes]
+                if has_before:
+                    result += c * before[i, :, lanes]
+                part[i, :, lanes] = result
     if gram:
-        mass = refs[5 + has_before]
+        mass = refs[1 + has_before]
         total = jnp.zeros(mass.shape, F32)
         for i in range(plan.rows):
             rounded = y[i].astype(BF16)
@@ -479,7 +514,7 @@
 
 def inner(plan, factors, u, y, before, w_in, scale, gram=False):
     has_before = before is not None
-    args = (u, y) + ((before,) if has_before else ()) + (w_in, scale)
+    args = (u, y, *w_in, scale) + ((before,) if has_before else ())
     outs = (shape(plan.rows, plan.vectors, plan.lanes),)
     if gram:
         outs += (shape(plan.vectors, plan.vectors),)
@@ -493,7 +528,7 @@
     )
 
 
-def halo_terms(plan, u, w_out, *gots):
+def halo_terms(plan, u, w_out, below, *gots):
     x, z, v, s = place(plan)
     even_layer, even_seg, wrap = lax.rem(z, 2) == 0, lax.rem(s, 2) == 0, s == 0
     width, half, last, at = plan.width, plan.half, plan.rows - 1, plan.outer
@@ -506,7 +541,7 @@
     right = [lax.select(even_seg, got_core[i], got_ring[i]) for i in range(plan.rows)]
 
     def row(i):
-        found = {0: dot_turned(left[i], w_out[at["N", i, 0]])}
+        found = {0: dot(left[i], w_out[at["N", i, 0]])}
         found[plan.run - 1] = dot(right[i], w_out[at["N", i, plan.run]])
 
         def add(p, term):
@@ -514,17 +549,16 @@
 
         if i == 0:
             for p in range(plan.run):
-                add(p, dot_turned(top[:, p * width : (p + 1) * width], w_out[at["F", 0, p]]))
+                add(p, dot(top[:, p * width : (p + 1) * width], w_out[at["F", 0, p]]))
             lanes = slice((half - 1) * width, half * width)
             before = lax.select(wrap, top[:, lanes], u[0, :, lanes])
-            add(half, dot_turned(before, w_out[at["N", 0, half]]))
+            add(half, dot(before, w_out[at["N", 0, half]]))
         if i == last:
             for p in range(plan.run):
-                add(p, dot(bottom[:, p * width : (p + 1) * width], w_out[at["F", plan.rows, p]]))
+                add(p, dot(bottom[:, p * width : (p + 1) * width], below[1 + p]))
             lanes = slice(half * width, (half + 1) * width)
             after = lax.select(wrap, bottom[:, lanes], u[last, :, lanes])
-            here, there = at["N", last, half], at["N", plan.rows, half]
-            add(half - 1, dot(after, w_out[here + wrap.astype(jnp.int32) * (there - here)]))
+            add(half - 1, dot(after, lax.select(wrap, below[0], w_out[at["N", last, half]])))
         return found
 
     return row
@@ -540,10 +574,10 @@
     return out
 
 
-def outer_kernel(plan, factor, leaving, part, u, w_out, scale, got_0, got_1, got_2, got_3, *refs):
+def outer_kernel(plan, factor, leaving, part, u, w_out, below, scale, got_0, got_1, got_2, got_3, *refs):
     refs = list(refs)
     y_out, u_out, send_a, send_b, send_core, send_ring = refs[:6]
-    row = halo_terms(plan, u, w_out, got_0, got_1, got_2, got_3)
+    row = halo_terms(plan, u, w_out, below, got_0, got_1, got_2, got_3)
     width = plan.width
     for i in range(plan.rows):
         values = finished_row(plan, i, part, scale, factor, row(i))
@@ -569,7 +603,7 @@
     outs = (shape(plan.rows, plan.vectors, plan.lanes),) + sends(plan)
     if leaving:
         outs += (exit_shape(plan, plan.segments // 2),)
-    args = (part, u, w_out, scale) + tuple(got)
+    args = (part, u, *w_out, scale) + tuple(got)
     return call(
         "outer", functools.partial(outer_kernel, plan, factor, leaving),
         outs,
@@ -588,42 +622,14 @@
         to_x = 1 - x if dx else x
         first = pl.multiple_of((2 * (at - to_x * (plan.vecs // 2)) + core) * plan.columns, plan.columns)
         for r in range(plan.own):
-            out[0, r] = y[to_x * plan.own + r, pl.ds(first, plan.columns), :]
-            out[1, r] = got_core[at, r]
+            out[0, r] = y[to_x * plan.own + r, pl.ds(first, plan.columns), :].astype(out.dtype)
+            out[1, r] = got_core[at, r].astype(out.dtype)
 
 
 def leave(plan, y, got_core):
-    n = len(chip_order(plan))
-    return call(
-        "leave", functools.partial(leave_kernel, plan), (exit_shape(plan, 2),) * n, vm(2), (y, got_core), moved=4 << 20
-    )
-
-
-def arrive_kernel(plan, *refs):
-    *gots, out = refs
-    x, z, v, s = place(plan)
-    core, chip = lax.rem(v, 2), lax.div(v, 2)
-    for (dx, dy), got in zip(chip_order(plan), gots, strict=True):
-        for other in range(2):
-            seg = jnp.int32(0)
-            for m in range(2):
-                for at in range(plan.vecs):
-                    source = plan.seg[m ^ dx, (at ^ other) ^ (2 * dy)]
-                    seg = seg + jnp.where((x == m) & (v == at), source, 0)
-            for r in range(plan.own):
-                for p in range(plan.run):
-                    to = pl.multiple_of((r * SPAN + column(plan, seg, p)) * plan.width, plan.width)
-                    out[:, pl.ds(to, plan.width)] = got[other, r, :, p * plan.width : (p + 1) * plan.width]
-
-
-def arrive(plan, gots):
-    return call(
-        "arrive", functools.partial(arrive_kernel, plan),
-        shape(plan.columns, plan.blocks * plan.width),
-        vm(len(gots)),
-        tuple(gots),
-        moved=2 << 20,
-    )
+    dims = (2, plan.own, plan.columns, plan.lanes)
+    outs = tuple(shape(*dims, dtype=F32) for _ in chip_order(plan))
+    return call("leave", functools.partial(leave_kernel, plan), outs, vm(2), (y, got_core), moved=4 << 20)
 
 
 def gram_pieces(plan):
@@ -632,8 +638,8 @@
     return rows, height, rows // height
 
 
-def image_kernel(plan, part, u, w_out, scale, got_0, got_1, got_2, got_3, y, mass, out):
-    row = halo_terms(plan, u, w_out, got_0, got_1, got_2, got_3)
+def image_kernel(plan, part, u, w_out, below, scale, got_0, got_1, got_2, got_3, y, mass, out):
+    row = halo_terms(plan, u, w_out, below, got_0, got_1, got_2, got_3)
     stiff = jnp.zeros((plan.vectors, plan.vectors), F32)
     for i in range(plan.rows):
         values = finished_row(plan, i, part, scale, 1.0, row(i))
@@ -652,7 +658,7 @@
 
 def image(plan, part, u, w_out, scale, got, y, mass):
     rows, height, count = gram_pieces(plan)
-    args = (part, u, w_out, scale) + tuple(got) + (y, mass)
+    args = (part, u, *w_out, scale) + tuple(got) + (y, mass)
     return call(
         "image", functools.partial(image_kernel, plan),
         shape(plan.meshes * plan.vecs, height, 2 * count * plan.columns),
@@ -672,12 +678,39 @@
             out[h * height : (h + 1) * height, :] = total[:, lo : lo + plan.columns]
 
 
+def total(plan, grams):
+    outs = (shape(gram_pieces(plan)[0], plan.columns),) * 2
+    return call("total", functools.partial(sum_kernel, plan), outs, vm(1), (grams,), moved=1 << 17)
+
+
+def arrive_kernel(plan, *refs):
+    *gots, out = refs
+    x, z, v, s = place(plan)
+    for (dx, dy), got in zip(chip_order(plan), gots, strict=True):
+        for other in range(2):
+            seg = jnp.int32(0)
+            for m in range(2):
+                for at in range(plan.vecs):
+                    source = plan.seg[m ^ dx, (at ^ other) ^ (2 * dy)]
+                    seg = seg + jnp.where((x == m) & (v == at), source, 0)
+            for r in range(plan.own):
+                for p in range(plan.run):
+                    to = pl.multiple_of((r * SPAN + column(plan, seg, p)) * plan.width, plan.width)
+                    value = got[other, r, :, p * plan.width : (p + 1) * plan.width]
+                    out[:, pl.ds(to, plan.width)] = value.astype(F32)
+
+
+def arrive(plan, gots):
+    out = shape(plan.columns, plan.blocks * plan.width)
+    return call("arrive", functools.partial(arrive_kernel, plan), out, vm(len(gots)), tuple(gots), moved=2 << 20)
+
+
 def shards(plan, panel, orient, mass, diag, near, far):
     w = plan.width
     panel = panel.T
     orient, mass = orient.reshape(plan.blocks, w), mass.reshape(plan.blocks, w)
     scale_own, entering, own_entering, first = prepare(plan, panel, orient, mass, diag, near, far)
-    own_diag, own_first, own_rest, rest = fetch(plan, diag, near, far)
+    own_first, own_near, own_rest, others, rest, near_turned, far_turned = fetch(plan, diag, near, far)
 
     def half(m, v):
         return m ^ 1, v
@@ -692,15 +725,18 @@
 
     first = plan.swap(first, half)
     parts = enter(plan, own_entering, plan.swap(entering, plan.core_swap))
+    others, *parts = lax.optimization_barrier((others, *parts))
     gots = spread(parts)
-    first, rest, *gots = lax.optimization_barrier((first, rest, *gots))
-    rest = plan.swap(rest, half)
-    above = jnp.where(lax.axis_index("mesh") % 2 == 0, own_first, first[: plan.run + 1])
+    gots[0], rest = lax.optimization_barrier((gots[0], rest))
+    others, rest = plan.swap(others, half), plan.swap(rest, half)
+    n_above = plan.run + 1
+    above = jnp.where(lax.axis_index("mesh") % 2 == 0, own_first[:n_above], first[:n_above])
     pairs = [(m * plan.vecs + v, (m - 2) * plan.vecs + v) for m in range(2, plan.meshes) for v in range(plan.vecs)]
     below = lax.ppermute(above, BOTH, pairs)
 
     y, scale, *field = begin(plan, gots, scale_own, first)
-    w_in, w_out = weights(plan, own_diag, own_first, own_rest, first, rest, below)
+    *w_in, w_out = late(plan, own_first, own_near, own_rest, first, others, rest, near_turned, far_turned)
+    w_out = (w_out, below)
 
     def exchange(field):
         u, a, b, core, ring = field
@@ -729,11 +765,8 @@
     kept = spread(leave(plan, y, got_core))
     grams = image(plan, part, u, w_out, scale, halos, y, mass_gram)
     grams = lax.all_to_all(grams, BOTH, 0, 0, tiled=True)
-    rows = gram_pieces(plan)[0]
-    stiff_gram, mass_gram = call(
-        "sum", functools.partial(sum_kernel, plan), (shape(rows, plan.columns),) * 2, vm(1), (grams,), moved=1 << 17
-    )
     filtered = arrive(plan, kept)
+    stiff_gram, mass_gram = total(plan, grams)
     return filtered.T, stiff_gram.T, mass_gram.T
 
 

time: 111 us -> 107 us (0.964)
  Pallas kernels: 20.8 us -> 17.1 us
  starting transfers between devices: 45.3 us -> 46.6 us
    ppermute x1, waiting for transfers between devices: 3.97 us -> 0.01 us  [shards(): below = lax.ppermute(above, BOTH, pairs)]
    pallas_call x26, Pallas kernels: 20.8 us -> 17.1 us  [call(): pl.pallas_call(kernel, name=name, out_shape=outs, in_specs=ins, out_specs...]
    ppermute x46 -> x47, waiting for transfers between devices: 26.5 us -> 30.1 us  [swap(): return lax.ppermute(x, BOTH, pairs)]
    ppermute x46 -> x47, starting transfers between devices: 44.1 us -> 45.3 us  [swap(): return lax.ppermute(x, BOTH, pairs)]
  transfers between devices with their start and end apart: 47 -> 48, of which waited for: 16 -> 18; matrix products, arithmetic and copies ran while one was open for 0% -> 0% of each run, Pallas kernels for 13% -> 10%
where the time goes in v3:
time: 107 us
  starting transfers between devices  46.6 us (44%)
  waiting for transfers between devices  30.1 us (28%)
  Pallas kernels  17.1 us (16%)
  blocking collectives  12.3 us (11%)
    ppermute x47, starting transfers between devices, swap(): return lax.ppermute(x, BOTH, pairs)  45.3 us
    ppermute x47, waiting for transfers between devices, swap(): return lax.ppermute(x, BOTH, pairs)  30.1 us
    pallas_call x26, Pallas kernels, call(): pl.pallas_call(kernel, name=name, out_shape=outs, in_specs=ins, out_specs...  17.1 us
    all_to_all x1, blocking collectives, shards(): grams = lax.all_to_all(grams, BOTH, 0, 0, tiled=True)  12.3 us
  transfers between devices with their start and end apart: 48, of which 18 were waited for; matrix products, arithmetic and copies ran while one was open for 0% of the time, Pallas kernels for 10%

profile of v3, /device:TPU:0, one launch (start us, length us, event | category | flops | bytes accessed | tf_op | source)
XLA Modules:
  0.0 107.0 jit_solution(5883826667320430721)
XLA Ops:
  0.6 1.6 %prepare.1 = (f32[64,128]{1,0:T(8,128)S(1)}, f32[4,2,32,512]{3,2,1,0:T(8,128)S(1)}, f32[4,2,32,512]{3,2,1,0:T(8,128)S(1)}, bf16[10,128,128]{2,1,0:T(8,128)(2,1)S(1)}) custom-call(f32[32,8192]{1,0:T(8,128)} %bitcast.6, s32[64,128]{1,0:T(8,128)} %bitcast.8, f32[64,128]{1,0:T(8,128)} %bitcast.9, bf16[64,128,128]{2,1,0:T(8,128)(2,1)} %diag.3, ...), custom_call_target="tpu_custom_call" | custom-call | bytes 3145728 | tf_op jit(solution)/shard_map/prepare/pallas_call | solution.py:121
  2.8 2.6 %collective-permute-start = (bf16[10,128,128]{2,1,0:T(8,128)(2,1)S(1)}, bf16[10,128,128]{2,1,0:T(8,128)(2,1)S(1)}, u32[]{:S(2)}, u32[]{:S(2)}) collective-permute-start(bf16[10,128,128]{2,1,0:T(8,128)(2,1)S(1)} %get-tuple-element.97), channel_id=1, source_target_pairs={{0,4},{1,5},{2,6},{3,7},{4,0},{5,1},{6,2},{7,3},{8,12},{9,13},{10,... | collective-permute-start | bytes 983048 | tf_op jit(solution)/shard_map/ppermute | solution.py:68
  5.4 1.9 %fetch.1 = (bf16[9,128,128]{2,1,0:T(8,128)(2,1)S(1)}, bf16[5,128,128]{2,1,0:T(8,128)(2,1)S(1)}, bf16[12,128,128]{2,1,0:T(8,128)(2,1)S(1)}, bf16[5,128,128]{2,1,0...) custom-call(bf16[64,128,128]{2,1,0:T(8,128)(2,1)} %diag.3, ...), custom_call_target="tpu_custom_call" | custom-call | bytes 3145728 | tf_op jit(solution)/shard_map/fetch/pallas_call | solution.py:121
  8.1 1.9 %collective-permute-start.5 = (bf16[5,128,128]{2,1,0:T(8,128)(2,1)S(1)}, bf16[5,128,128]{2,1,0:T(8,128)(2,1)S(1)}, u32[]{:S(2)}, u32[]{:S(2)}) collective-permute-start(bf16[5,128,128]{2,1,0:T(8,128)(2,1)S(1)} %get-tuple-element.116), channel_id=1, source_target_pairs={{0,4},{1,5},{2,6},{3,7},{4,0},{5,1},{6,2},{7,3},{8,12},{9,13},{10,... | collective-permute-start | bytes 491528 | tf_op jit(solution)/shard_map/ppermute | solution.py:68
  11.6 8.0 %collective-permute-done.2.refs_0_ = f32[2,2,32,512]{3,2,1,0:T(8,128)S(1)} collective-permute-done((f32[2,2,32,512]{3,2,1,0:T(8,128)}, f32[2,2,32,512]{3,2,1,0:T(8,128)S(1)}, u32[]{:S(2)}, u32[]{:S(2)}) %collective-permute-start.2) | collective-permute-done | bytes 262176 | tf_op jit(solution)/shard_map/ppermute | solution.py:68
  19.5 1.9 %collective-permute-start.6 = (bf16[8,128,128]{2,1,0:T(8,128)(2,1)S(1)}, bf16[8,128,128]{2,1,0:T(8,128)(2,1)S(1)}, u32[]{:S(2)}, u32[]{:S(2)}) collective-permute-start(bf16[8,128,128]{2,1,0:T(8,128)(2,1)S(1)} %get-tuple-element.117), channel_id=1, source_target_pairs={{0,4},{1,5},{2,6},{3,7},{4,0},{5,1},{6,2},{7,3},{8,12},{9,13},{10,... | collective-permute-start | bytes 786440 | tf_op jit(solution)/shard_map/ppermute | solution.py:68
  22.8 7.3 %collective-permute-done.3.refs_1_ = f32[2,2,32,512]{3,2,1,0:T(8,128)S(1)} collective-permute-done((f32[2,2,32,512]{3,2,1,0:T(8,128)S(1)}, f32[2,2,32,512]{3,2,1,0:T(8,128)S(1)}, u32[]{:S(2)}, u32[]{:S(2)}) %collective-permute-start.3) | collective-permute-done | bytes 262176 | tf_op jit(solution)/shard_map/ppermute | solution.py:68
  30.3 1.6 %collective-permute-start.8 = (bf16[4,128,128]{2,1,0:T(8,128)(2,1)S(1)}, bf16[4,128,128]{2,1,0:T(8,128)(2,1)S(1)}, u32[]{:S(2)}, u32[]{:S(2)}) collective-permute-start(bf16[4,128,128]{2,1,0:T(8,128)(2,1)S(1)} %get-tuple-element.126), channel_id=1, source_target_pairs={{0,4},{1,3},{2,6},{3,1},{4,0},{5,7},{6,2},{7,5},{8,12},{9,11},{10,... | collective-permute-start | bytes 393224 | tf_op jit(solution)/shard_map/ppermute | solution.py:68
  31.9 1.6 %collective-permute-start.9 = (bf16[128,512]{1,0:T(8,128)(2,1)S(1)}, bf16[128,512]{1,0:T(8,128)(2,1)S(1)}, u32[]{:S(2)}, u32[]{:S(2)}) collective-permute-start(bf16[128,512]{1,0:T(8,128)(2,1)S(1)} %get-tuple-element.127), channel_id=1, source_target_pairs={{0,8},{1,9},{2,10},{3,11},{4,12},{5,13},{6,14},{7,15},{8,0},{9,1},... | collective-permute-start | bytes 393224 | tf_op jit(solution)/shard_map/ppermute | solution.py:68
  37.9 2.7 %collective-permute-start.13 = (bf16[128,512]{1,0:T(8,128)(2,1)S(1)}, bf16[128,512]{1,0:T(8,128)(2,1)S(1)}, u32[]{:S(2)}, u32[]{:S(2)}) collective-permute-start(bf16[128,512]{1,0:T(8,128)(2,1)S(1)} %get-tuple-element.133), channel_id=1, source_target_pairs={{0,8},{1,9},{2,10},{3,11},{4,12},{5,13},{6,14},{7,15},{8,0},{9,1},... | collective-permute-start | bytes 393224 | tf_op jit(solution)/shard_map/ppermute | solution.py:68
  44.0 1.6 %collective-permute-start.16 = (bf16[4,128,128]{2,1,0:T(8,128)(2,1)S(1)}, bf16[4,128,128]{2,1,0:T(8,128)(2,1)S(1)}, u32[]{:S(2)}, u32[]{:S(2)}) collective-permute-start(bf16[4,128,128]{2,1,0:T(8,128)(2,1)S(1)} %get-tuple-element.138), channel_id=1, source_target_pairs={{0,4},{1,3},{2,6},{3,1},{4,0},{5,7},{6,2},{7,5},{8,12},{9,11},{10,... | collective-permute-start | bytes 393224 | tf_op jit(solution)/shard_map/ppermute | solution.py:68
  45.6 2.4 %collective-permute-start.17 = (bf16[128,512]{1,0:T(8,128)(2,1)S(1)}, bf16[128,512]{1,0:T(8,128)(2,1)S(1)}, u32[]{:S(2)}, u32[]{:S(2)}) collective-permute-start(bf16[128,512]{1,0:T(8,128)(2,1)S(1)} %get-tuple-element.139), channel_id=1, source_target_pairs={{0,8},{1,9},{2,10},{3,11},{4,12},{5,13},{6,14},{7,15},{8,0},{9,1},... | collective-permute-start | bytes 393224 | tf_op jit(solution)/shard_map/ppermute | solution.py:68
  49.1 1.8 %collective-permute-done.17.got_1 = bf16[128,512]{1,0:T(8,128)(2,1)S(1)} collective-permute-done((bf16[128,512]{1,0:T(8,128)(2,1)S(1)}, bf16[128,512]{1,0:T(8,128)(2,1)S(1)}, u32[]{:S(2)}, u32[]{:S(2)}) %collective-permute-start.17) | collective-permute-done | bytes 131104 | tf_op jit(solution)/shard_map/ppermute | solution.py:68
  52.0 2.0 %collective-permute-start.21 = (bf16[128,512]{1,0:T(8,128)(2,1)S(1)}, bf16[128,512]{1,0:T(8,128)(2,1)S(1)}, u32[]{:S(2)}, u32[]{:S(2)}) collective-permute-start(bf16[128,512]{1,0:T(8,128)(2,1)S(1)} %get-tuple-element.145), channel_id=1, source_target_pairs={{0,8},{1,9},{2,10},{3,11},{4,12},{5,13},{6,14},{7,15},{8,0},{9,1},... | collective-permute-start | bytes 393224 | tf_op jit(solution)/shard_map/ppermute | solution.py:68
  57.4 1.5 %collective-permute-start.24 = (bf16[4,128,128]{2,1,0:T(8,128)(2,1)S(1)}, bf16[4,128,128]{2,1,0:T(8,128)(2,1)S(1)}, u32[]{:S(2)}, u32[]{:S(2)}) collective-permute-start(bf16[4,128,128]{2,1,0:T(8,128)(2,1)S(1)} %get-tuple-element.150), channel_id=1, source_target_pairs={{0,4},{1,3},{2,6},{3,1},{4,0},{5,7},{6,2},{7,5},{8,12},{9,11},{10,... | collective-permute-start | bytes 393224 | tf_op jit(solution)/shard_map/ppermute | solution.py:68
  58.9 2.0 %collective-permute-start.25 = (bf16[128,512]{1,0:T(8,128)(2,1)S(1)}, bf16[128,512]{1,0:T(8,128)(2,1)S(1)}, u32[]{:S(2)}, u32[]{:S(2)}) collective-permute-start(bf16[128,512]{1,0:T(8,128)(2,1)S(1)} %get-tuple-element.151), channel_id=1, source_target_pairs={{0,8},{1,9},{2,10},{3,11},{4,12},{5,13},{6,14},{7,15},{8,0},{9,1},... | collective-permute-start | bytes 393224 | tf_op jit(solution)/shard_map/ppermute | solution.py:68
  65.0 2.0 %collective-permute-start.29 = (bf16[128,512]{1,0:T(8,128)(2,1)S(1)}, bf16[128,512]{1,0:T(8,128)(2,1)S(1)}, u32[]{:S(2)}, u32[]{:S(2)}) collective-permute-start(bf16[128,512]{1,0:T(8,128)(2,1)S(1)} %get-tuple-element.157), channel_id=1, source_target_pairs={{0,8},{1,9},{2,10},{3,11},{4,12},{5,13},{6,14},{7,15},{8,0},{9,1},... | collective-permute-start | bytes 393224 | tf_op jit(solution)/shard_map/ppermute | solution.py:68
  70.4 1.5 %collective-permute-start.32 = (bf16[4,128,128]{2,1,0:T(8,128)(2,1)S(1)}, bf16[4,128,128]{2,1,0:T(8,128)(2,1)S(1)}, u32[]{:S(2)}, u32[]{:S(2)}) collective-permute-start(bf16[4,128,128]{2,1,0:T(8,128)(2,1)S(1)} %get-tuple-element.162), channel_id=1, source_target_pairs={{0,4},{1,3},{2,6},{3,1},{4,0},{5,7},{6,2},{7,5},{8,12},{9,11},{10,... | collective-permute-start | bytes 393224 | tf_op jit(solution)/shard_map/ppermute | solution.py:68
  71.9 2.0 %collective-permute-start.33 = (bf16[128,512]{1,0:T(8,128)(2,1)S(1)}, bf16[128,512]{1,0:T(8,128)(2,1)S(1)}, u32[]{:S(2)}, u32[]{:S(2)}) collective-permute-start(bf16[128,512]{1,0:T(8,128)(2,1)S(1)} %get-tuple-element.163), channel_id=1, source_target_pairs={{0,8},{1,9},{2,10},{3,11},{4,12},{5,13},{6,14},{7,15},{8,0},{9,1},... | collective-permute-start | bytes 393224 | tf_op jit(solution)/shard_map/ppermute | solution.py:68
  78.0 2.0 %collective-permute-start.37 = (bf16[128,512]{1,0:T(8,128)(2,1)S(1)}, bf16[128,512]{1,0:T(8,128)(2,1)S(1)}, u32[]{:S(2)}, u32[]{:S(2)}) collective-permute-start(bf16[128,512]{1,0:T(8,128)(2,1)S(1)} %get-tuple-element.169), channel_id=1, source_target_pairs={{0,8},{1,9},{2,10},{3,11},{4,12},{5,13},{6,14},{7,15},{8,0},{9,1},... | collective-permute-start | bytes 393224 | tf_op jit(solution)/shard_map/ppermute | solution.py:68
  83.6 1.5 %collective-permute-start.44 = (bf16[4,128,128]{2,1,0:T(8,128)(2,1)S(1)}, bf16[4,128,128]{2,1,0:T(8,128)(2,1)S(1)}, u32[]{:S(2)}, u32[]{:S(2)}) collective-permute-start(bf16[4,128,128]{2,1,0:T(8,128)(2,1)S(1)} %get-tuple-element.182), channel_id=1, source_target_pairs={{0,4},{1,3},{2,6},{3,1},{4,0},{5,7},{6,2},{7,5},{8,12},{9,11},{10,... | collective-permute-start | bytes 393224 | tf_op jit(solution)/shard_map/ppermute | solution.py:68
  85.1 2.0 %collective-permute-start.45 = (bf16[128,512]{1,0:T(8,128)(2,1)S(1)}, bf16[128,512]{1,0:T(8,128)(2,1)S(1)}, u32[]{:S(2)}, u32[]{:S(2)}) collective-permute-start(bf16[128,512]{1,0:T(8,128)(2,1)S(1)} %get-tuple-element.183), channel_id=1, source_target_pairs={{0,8},{1,9},{2,10},{3,11},{4,12},{5,13},{6,14},{7,15},{8,0},{9,1},... | collective-permute-start | bytes 393224 | tf_op jit(solution)/shard_map/ppermute | solution.py:68
  90.5 1.5 %collective-permute-start.43 = (f32[2,2,32,512]{3,2,1,0:T(8,128)S(1)}, f32[2,2,32,512]{3,2,1,0:T(8,128)S(1)}, u32[]{:S(2)}, u32[]{:S(2)}) collective-permute-start(f32[2,2,32,512]{3,2,1,0:T(8,128)S(1)} %get-tuple-element.180), channel_id=1, source_target_pairs={{0,2},{1,3},{2,0},{3,1},{4,6},{5,7},{6,4},{7,5},{8,10},{9,11},{10,... | collective-permute-start | bytes 786440 | tf_op jit(solution)/shard_map/ppermute | solution.py:68
  92.8 12.3 %all_to_all.5.got = f32[32,8,128]{2,1,0:T(8,128)S(1)} all-to-all(f32[32,8,128]{2,1,0:T(8,128)S(1)} %image.1), channel_id=1, replica_groups=mesh['mesh'=8,'vec'=4] {'mesh','vec'}, dimensions={0} | all-to-all | bytes 262144 | tf_op jit(solution)/shard_map/all_to_all | solution.py:767
  (100 shorter events, 38.8 us)
Async XLA Ops:
  2.8 18.7 %collective-permute-start = (bf16[10,128,128]{2,1,0:T(8,128)(2,1)S(1)}, bf16[10,128,128]{2,1,0:T(8,128)(2,1)S(1)}, u32[]{:S(2)}, u32[]{:S(2)}) collective-permute-start(bf16[10,128,128]{2,1,0:T(8,128)(2,1)S(1)} %get-tuple-element.97), channel_id=1, source_target_pairs={{0,4},{1,5},{2,6},{3,7},{4,0},{5,1},{6,2},{7,3},{8,12},{9,13},{10,... | collective-permute-start | bytes 983048 | tf_op jit(solution)/shard_map/ppermute | solution.py:68
  8.0 11.5 %collective-permute-start.2 = (f32[2,2,32,512]{3,2,1,0:T(8,128)}, f32[2,2,32,512]{3,2,1,0:T(8,128)S(1)}, u32[]{:S(2)}, u32[]{:S(2)}) collective-permute-start(f32[2,2,32,512]{3,2,1,0:T(8,128)} %get-tuple-element.105), channel_id=1, source_target_pairs={{0,4},{1,5},{2,6},{3,7},{4,0},{5,1},{6,2},{7,3},{8,12},{9,13},{10,... | collective-permute-start | bytes 786440 | tf_op jit(solution)/shard_map/ppermute | solution.py:68
  8.1 25.4 %collective-permute-start.5 = (bf16[5,128,128]{2,1,0:T(8,128)(2,1)S(1)}, bf16[5,128,128]{2,1,0:T(8,128)(2,1)S(1)}, u32[]{:S(2)}, u32[]{:S(2)}) collective-permute-start(bf16[5,128,128]{2,1,0:T(8,128)(2,1)S(1)} %get-tuple-element.116), channel_id=1, source_target_pairs={{0,4},{1,5},{2,6},{3,7},{4,0},{5,1},{6,2},{7,3},{8,12},{9,13},{10,... | collective-permute-start | bytes 491528 | tf_op jit(solution)/shard_map/ppermute | solution.py:68
  10.0 20.0 %collective-permute-start.3 = (f32[2,2,32,512]{3,2,1,0:T(8,128)S(1)}, f32[2,2,32,512]{3,2,1,0:T(8,128)S(1)}, u32[]{:S(2)}, u32[]{:S(2)}) collective-permute-start(f32[2,2,32,512]{3,2,1,0:T(8,128)S(1)} %get-tuple-element.108), channel_id=1, source_target_pairs={{0,6},{1,7},{2,4},{3,5},{4,2},{5,3},{6,0},{7,1},{8,14},{9,15},{10,... | collective-permute-start | bytes 786440 | tf_op jit(solution)/shard_map/ppermute | solution.py:68
  11.5 18.5 %collective-permute-start.4 = (f32[2,2,32,512]{3,2,1,0:T(8,128)S(1)}, f32[2,2,32,512]{3,2,1,0:T(8,128)S(1)}, u32[]{:S(2)}, u32[]{:S(2)}) collective-permute-start(f32[2,2,32,512]{3,2,1,0:T(8,128)S(1)} %get-tuple-element.110), channel_id=1, source_target_pairs={{0,2},{1,3},{2,0},{3,1},{4,6},{5,7},{6,4},{7,5},{8,10},{9,11},{10,... | collective-permute-start | bytes 786440 | tf_op jit(solution)/shard_map/ppermute | solution.py:68
  19.5 14.5 %collective-permute-start.6 = (bf16[8,128,128]{2,1,0:T(8,128)(2,1)S(1)}, bf16[8,128,128]{2,1,0:T(8,128)(2,1)S(1)}, u32[]{:S(2)}, u32[]{:S(2)}) collective-permute-start(bf16[8,128,128]{2,1,0:T(8,128)(2,1)S(1)} %get-tuple-element.117), channel_id=1, source_target_pairs={{0,4},{1,5},{2,6},{3,7},{4,0},{5,1},{6,2},{7,3},{8,12},{9,13},{10,... | collective-permute-start | bytes 786440 | tf_op jit(solution)/shard_map/ppermute | solution.py:68
  21.5 13.8 %collective-permute-start.7 = (bf16[5,128,128]{2,1,0:T(8,128)(2,1)S(1)}, bf16[5,128,128]{2,1,0:T(8,128)(2,1)S(1)}, u32[]{:S(2)}, u32[]{:S(2)}) collective-permute-start(bf16[5,128,128]{2,1,0:T(8,128)(2,1)S(1)} %slice_select_fusion), channel_id=1, source_target_pairs={{8,0},{9,1},{10,2},{11,3},{12,4},{13,5},{14,6},{15,7},{16,8},{17,9... | collective-permute-start | bytes 491528 | tf_op jit(solution)/shard_map/ppermute | solution.py:735
  30.3 5.1 %collective-permute-start.8 = (bf16[4,128,128]{2,1,0:T(8,128)(2,1)S(1)}, bf16[4,128,128]{2,1,0:T(8,128)(2,1)S(1)}, u32[]{:S(2)}, u32[]{:S(2)}) collective-permute-start(bf16[4,128,128]{2,1,0:T(8,128)(2,1)S(1)} %get-tuple-element.126), channel_id=1, source_target_pairs={{0,4},{1,3},{2,6},{3,1},{4,0},{5,7},{6,2},{7,5},{8,12},{9,11},{10,... | collective-permute-start | bytes 393224 | tf_op jit(solution)/shard_map/ppermute | solution.py:68
  37.3 5.0 %collective-permute-start.12 = (bf16[4,128,128]{2,1,0:T(8,128)(2,1)S(1)}, bf16[4,128,128]{2,1,0:T(8,128)(2,1)S(1)}, u32[]{:S(2)}, u32[]{:S(2)}) collective-permute-start(bf16[4,128,128]{2,1,0:T(8,128)(2,1)S(1)} %get-tuple-element.132), channel_id=1, source_target_pairs={{0,4},{1,3},{2,6},{3,1},{4,0},{5,7},{6,2},{7,5},{8,12},{9,11},{10,... | collective-permute-start | bytes 393224 | tf_op jit(solution)/shard_map/ppermute | solution.py:68
  37.9 5.7 %collective-permute-start.13 = (bf16[128,512]{1,0:T(8,128)(2,1)S(1)}, bf16[128,512]{1,0:T(8,128)(2,1)S(1)}, u32[]{:S(2)}, u32[]{:S(2)}) collective-permute-start(bf16[128,512]{1,0:T(8,128)(2,1)S(1)} %get-tuple-element.133), channel_id=1, source_target_pairs={{0,8},{1,9},{2,10},{3,11},{4,12},{5,13},{6,14},{7,15},{8,0},{9,1},... | collective-permute-start | bytes 393224 | tf_op jit(solution)/shard_map/ppermute | solution.py:68
  44.0 5.0 %collective-permute-start.16 = (bf16[4,128,128]{2,1,0:T(8,128)(2,1)S(1)}, bf16[4,128,128]{2,1,0:T(8,128)(2,1)S(1)}, u32[]{:S(2)}, u32[]{:S(2)}) collective-permute-start(bf16[4,128,128]{2,1,0:T(8,128)(2,1)S(1)} %get-tuple-element.138), channel_id=1, source_target_pairs={{0,4},{1,3},{2,6},{3,1},{4,0},{5,7},{6,2},{7,5},{8,12},{9,11},{10,... | collective-permute-start | bytes 393224 | tf_op jit(solution)/shard_map/ppermute | solution.py:68
  45.6 5.3 %collective-permute-start.17 = (bf16[128,512]{1,0:T(8,128)(2,1)S(1)}, bf16[128,512]{1,0:T(8,128)(2,1)S(1)}, u32[]{:S(2)}, u32[]{:S(2)}) collective-permute-start(bf16[128,512]{1,0:T(8,128)(2,1)S(1)} %get-tuple-element.139), channel_id=1, source_target_pairs={{0,8},{1,9},{2,10},{3,11},{4,12},{5,13},{6,14},{7,15},{8,0},{9,1},... | collective-permute-start | bytes 393224 | tf_op jit(solution)/shard_map/ppermute | solution.py:68
  51.3 5.0 %collective-permute-start.20 = (bf16[4,128,128]{2,1,0:T(8,128)(2,1)S(1)}, bf16[4,128,128]{2,1,0:T(8,128)(2,1)S(1)}, u32[]{:S(2)}, u32[]{:S(2)}) collective-permute-start(bf16[4,128,128]{2,1,0:T(8,128)(2,1)S(1)} %get-tuple-element.144), channel_id=1, source_target_pairs={{0,4},{1,3},{2,6},{3,1},{4,0},{5,7},{6,2},{7,5},{8,12},{9,11},{10,... | collective-permute-start | bytes 393224 | tf_op jit(solution)/shard_map/ppermute | solution.py:68
  52.0 5.0 %collective-permute-start.21 = (bf16[128,512]{1,0:T(8,128)(2,1)S(1)}, bf16[128,512]{1,0:T(8,128)(2,1)S(1)}, u32[]{:S(2)}, u32[]{:S(2)}) collective-permute-start(bf16[128,512]{1,0:T(8,128)(2,1)S(1)} %get-tuple-element.145), channel_id=1, source_target_pairs={{0,8},{1,9},{2,10},{3,11},{4,12},{5,13},{6,14},{7,15},{8,0},{9,1},... | collective-permute-start | bytes 393224 | tf_op jit(solution)/shard_map/ppermute | solution.py:68
  57.4 5.0 %collective-permute-start.24 = (bf16[4,128,128]{2,1,0:T(8,128)(2,1)S(1)}, bf16[4,128,128]{2,1,0:T(8,128)(2,1)S(1)}, u32[]{:S(2)}, u32[]{:S(2)}) collective-permute-start(bf16[4,128,128]{2,1,0:T(8,128)(2,1)S(1)} %get-tuple-element.150), channel_id=1, source_target_pairs={{0,4},{1,3},{2,6},{3,1},{4,0},{5,7},{6,2},{7,5},{8,12},{9,11},{10,... | collective-permute-start | bytes 393224 | tf_op jit(solution)/shard_map/ppermute | solution.py:68
  58.9 5.0 %collective-permute-start.25 = (bf16[128,512]{1,0:T(8,128)(2,1)S(1)}, bf16[128,512]{1,0:T(8,128)(2,1)S(1)}, u32[]{:S(2)}, u32[]{:S(2)}) collective-permute-start(bf16[128,512]{1,0:T(8,128)(2,1)S(1)} %get-tuple-element.151), channel_id=1, source_target_pairs={{0,8},{1,9},{2,10},{3,11},{4,12},{5,13},{6,14},{7,15},{8,0},{9,1},... | collective-permute-start | bytes 393224 | tf_op jit(solution)/shard_map/ppermute | solution.py:68
  64.3 5.0 %collective-permute-start.28 = (bf16[4,128,128]{2,1,0:T(8,128)(2,1)S(1)}, bf16[4,128,128]{2,1,0:T(8,128)(2,1)S(1)}, u32[]{:S(2)}, u32[]{:S(2)}) collective-permute-start(bf16[4,128,128]{2,1,0:T(8,128)(2,1)S(1)} %get-tuple-element.156), channel_id=1, source_target_pairs={{0,4},{1,3},{2,6},{3,1},{4,0},{5,7},{6,2},{7,5},{8,12},{9,11},{10,... | collective-permute-start | bytes 393224 | tf_op jit(solution)/shard_map/ppermute | solution.py:68
  70.4 5.0 %collective-permute-start.32 = (bf16[4,128,128]{2,1,0:T(8,128)(2,1)S(1)}, bf16[4,128,128]{2,1,0:T(8,128)(2,1)S(1)}, u32[]{:S(2)}, u32[]{:S(2)}) collective-permute-start(bf16[4,128,128]{2,1,0:T(8,128)(2,1)S(1)} %get-tuple-element.162), channel_id=1, source_target_pairs={{0,4},{1,3},{2,6},{3,1},{4,0},{5,7},{6,2},{7,5},{8,12},{9,11},{10,... | collective-permute-start | bytes 393224 | tf_op jit(solution)/shard_map/ppermute | solution.py:68
  77.3 5.0 %collective-permute-start.36 = (bf16[4,128,128]{2,1,0:T(8,128)(2,1)S(1)}, bf16[4,128,128]{2,1,0:T(8,128)(2,1)S(1)}, u32[]{:S(2)}, u32[]{:S(2)}) collective-permute-start(bf16[4,128,128]{2,1,0:T(8,128)(2,1)S(1)} %get-tuple-element.168), channel_id=1, source_target_pairs={{0,4},{1,3},{2,6},{3,1},{4,0},{5,7},{6,2},{7,5},{8,12},{9,11},{10,... | collective-permute-start | bytes 393224 | tf_op jit(solution)/shard_map/ppermute | solution.py:68
  83.6 5.5 %collective-permute-start.44 = (bf16[4,128,128]{2,1,0:T(8,128)(2,1)S(1)}, bf16[4,128,128]{2,1,0:T(8,128)(2,1)S(1)}, u32[]{:S(2)}, u32[]{:S(2)}) collective-permute-start(bf16[4,128,128]{2,1,0:T(8,128)(2,1)S(1)} %get-tuple-element.182), channel_id=1, source_target_pairs={{0,4},{1,3},{2,6},{3,1},{4,0},{5,7},{6,2},{7,5},{8,12},{9,11},{10,... | collective-permute-start | bytes 393224 | tf_op jit(solution)/shard_map/ppermute | solution.py:68
  85.1 5.4 %collective-permute-start.45 = (bf16[128,512]{1,0:T(8,128)(2,1)S(1)}, bf16[128,512]{1,0:T(8,128)(2,1)S(1)}, u32[]{:S(2)}, u32[]{:S(2)}) collective-permute-start(bf16[128,512]{1,0:T(8,128)(2,1)S(1)} %get-tuple-element.183), channel_id=1, source_target_pairs={{0,8},{1,9},{2,10},{3,11},{4,12},{5,13},{6,14},{7,15},{8,0},{9,1},... | collective-permute-start | bytes 393224 | tf_op jit(solution)/shard_map/ppermute | solution.py:68
  88.4 17.3 %collective-permute-start.41 = (f32[2,2,32,512]{3,2,1,0:T(8,128)S(1)}, f32[2,2,32,512]{3,2,1,0:T(8,128)S(1)}, u32[]{:S(2)}, u32[]{:S(2)}) collective-permute-start(f32[2,2,32,512]{3,2,1,0:T(8,128)S(1)} %get-tuple-element.177), channel_id=1, source_target_pairs={{0,4},{1,5},{2,6},{3,7},{4,0},{5,1},{6,2},{7,3},{8,12},{9,13},{10,... | collective-permute-start | bytes 786440 | tf_op jit(solution)/shard_map/ppermute | solution.py:68
  89.1 16.7 %collective-permute-start.42 = (f32[2,2,32,512]{3,2,1,0:T(8,128)S(1)}, f32[2,2,32,512]{3,2,1,0:T(8,128)S(1)}, u32[]{:S(2)}, u32[]{:S(2)}) collective-permute-start(f32[2,2,32,512]{3,2,1,0:T(8,128)S(1)} %get-tuple-element.178), channel_id=1, source_target_pairs={{0,6},{1,7},{2,4},{3,5},{4,2},{5,3},{6,0},{7,1},{8,14},{9,15},{10,... | collective-permute-start | bytes 786440 | tf_op jit(solution)/shard_map/ppermute | solution.py:68
  90.5 15.3 %collective-permute-start.43 = (f32[2,2,32,512]{3,2,1,0:T(8,128)S(1)}, f32[2,2,32,512]{3,2,1,0:T(8,128)S(1)}, u32[]{:S(2)}, u32[]{:S(2)}) collective-permute-start(f32[2,2,32,512]{3,2,1,0:T(8,128)S(1)} %get-tuple-element.180), channel_id=1, source_target_pairs={{0,2},{1,3},{2,0},{3,1},{4,6},{5,7},{6,4},{7,5},{8,10},{9,11},{10,... | collective-permute-start | bytes 786440 | tf_op jit(solution)/shard_map/ppermute | solution.py:68
  (24 other events, 87.0 us)

commit v4 on v3

--- a/solution.py
+++ b/solution.py
@@ -333,16 +333,19 @@
     return to_x * (plan.vecs // 2) + to_chip
 
 
-def emit(plan, u_out, send_a, send_b, send_core, send_ring):
+def emit(plan, u, u_out, send_a, send_b, send_core, send_ring):
     x, z, v, s = place(plan)
     last, width = plan.rows - 1, plan.width
     even_layer, even_seg = lax.rem(z, 2) == 0, lax.rem(s, 2) == 0
-    send_a[...] = lax.select(even_layer, u_out[last], u_out[0])
-    send_b[...] = lax.select(even_layer, u_out[0], u_out[last])
     for i in range(plan.rows):
-        left, right = u_out[i, :, :width], u_out[i, :, plan.lanes - width :]
-        send_core[i] = lax.select(even_seg, right, left)
-        send_ring[i] = lax.select(even_seg, left, right)
+        for p in range(plan.run):
+            u_out[i, :, p * width : (p + 1) * width] = u[i][p]
+        send_core[i] = lax.select(even_seg, u[i][-1], u[i][0])
+        send_ring[i] = lax.select(even_seg, u[i][0], u[i][-1])
+    for p in range(plan.run):
+        lanes = slice(p * width, (p + 1) * width)
+        send_a[:, lanes] = lax.select(even_layer, u[last][p], u[0][p])
+        send_b[:, lanes] = lax.select(even_layer, u[0][p], u[last][p])
 
 
 def sends(plan):
@@ -367,6 +370,7 @@
             lo = pl.multiple_of((2 * from_chip + core) * plan.columns, plan.columns)
             for r in range(plan.own):
                 y_out[from_x * plan.own + r, pl.ds(lo, plan.columns), :] = got[core, r]
+    u = []
     for i in range(plan.rows):
         half, r = divmod(i, plan.own)
         for p in range(plan.run):
@@ -375,10 +379,11 @@
                 x == half, mine, theirs[r * plan.run + p : r * plan.run + p + 1]
             )
     for i in range(plan.rows):
+        u.append([])
         for p in range(plan.run):
             row, lanes = scale_out[pl.ds(i * plan.run + p, 1), :], slice(p * plan.width, (p + 1) * plan.width)
-            u_out[i, :, lanes] = (row * y_out[i, :, lanes]).astype(BF16)
-    emit(plan, u_out, send_a, send_b, send_core, send_ring)
+            u[i].append((row * y_out[i, :, lanes]).astype(BF16))
+    emit(plan, u, u_out, send_a, send_b, send_core, send_ring)
 
 
 def begin(plan, gots, scale_own, first):
@@ -579,12 +584,14 @@
     y_out, u_out, send_a, send_b, send_core, send_ring = refs[:6]
     row = halo_terms(plan, u, w_out, below, got_0, got_1, got_2, got_3)
     width = plan.width
+    fields = []
     for i in range(plan.rows):
         values = finished_row(plan, i, part, scale, factor, row(i))
+        fields.append([])
         for p, value in enumerate(values):
             y_out[i, :, p * width : (p + 1) * width] = value
-            u_out[i, :, p * width : (p + 1) * width] = (scale[pl.ds(i * plan.run + p, 1), :] * value).astype(BF16)
-    emit(plan, u_out, send_a, send_b, send_core, send_ring)
+            fields[i].append((scale[pl.ds(i * plan.run + p, 1), :] * value).astype(BF16))
+    emit(plan, fields, u_out, send_a, send_b, send_core, send_ring)
     if leaving:
         exit_core = refs[6]
         core = lax.rem(lax.axis_index("vec"), 2)
@@ -669,22 +676,14 @@
     )
 
 
-def sum_kernel(plan, got, stiff, mass):
+def finish_kernel(plan, grams, *refs):
+    *gots, out, stiff, mass = refs
     rows, height, count = gram_pieces(plan)
-    total = jnp.sum(got[...], axis=0)
-    for k, out in enumerate((stiff, mass)):
+    total = jnp.sum(grams[...], axis=0)
+    for k, gram in enumerate((stiff, mass)):
         for h in range(count):
             lo = (k * count + h) * plan.columns
-            out[h * height : (h + 1) * height, :] = total[:, lo : lo + plan.columns]
-
-
-def total(plan, grams):
-    outs = (shape(gram_pieces(plan)[0], plan.columns),) * 2
-    return call("total", functools.partial(sum_kernel, plan), outs, vm(1), (grams,), moved=1 << 17)
-
-
-def arrive_kernel(plan, *refs):
-    *gots, out = refs
+            gram[h * height : (h + 1) * height, :] = total[:, lo : lo + plan.columns]
     x, z, v, s = place(plan)
     for (dx, dy), got in zip(chip_order(plan), gots, strict=True):
         for other in range(2):
@@ -700,9 +699,16 @@
                     out[:, pl.ds(to, plan.width)] = value.astype(F32)
 
 
-def arrive(plan, gots):
-    out = shape(plan.columns, plan.blocks * plan.width)
-    return call("arrive", functools.partial(arrive_kernel, plan), out, vm(len(gots)), tuple(gots), moved=2 << 20)
+def finish(plan, grams, gots):
+    rows = gram_pieces(plan)[0]
+    return call(
+        "finish",
+        functools.partial(finish_kernel, plan),
+        (shape(plan.columns, plan.blocks * plan.width),) + (shape(rows, plan.columns),) * 2,
+        vm(1 + len(gots)),
+        (grams, *gots),
+        moved=3 << 20,
+    )
 
 
 def shards(plan, panel, orient, mass, diag, near, far):
@@ -765,8 +771,7 @@
     kept = spread(leave(plan, y, got_core))
     grams = image(plan, part, u, w_out, scale, halos, y, mass_gram)
     grams = lax.all_to_all(grams, BOTH, 0, 0, tiled=True)
-    filtered = arrive(plan, kept)
-    stiff_gram, mass_gram = total(plan, grams)
+    filtered, stiff_gram, mass_gram = finish(plan, grams, kept)
     return filtered.T, stiff_gram.T, mass_gram.T
 
 

time: 107 us -> 107 us (level)
    pallas_call x26 -> x25, Pallas kernels: 17.1 us -> 16.4 us  [call(): pl.pallas_call(kernel, name=name, out_shape=outs, in_specs=ins, out_specs...]
  transfers between devices with their start and end apart: 48 -> 48, of which waited for: 18 -> 19; matrix products, arithmetic and copies ran while one was open for 0% -> 0% of each run, Pallas kernels for 10% -> 9%
where the time goes in v4:
time: 107 us; the launch traced here: 106 us
  starting transfers between devices  46.5 us (43%)
  waiting for transfers between devices  30.1 us (28%)
  Pallas kernels  16.4 us (15%)
  blocking collectives  12.3 us (11%)
    ppermute x47, starting transfers between devices, swap(): return lax.ppermute(x, BOTH, pairs)  45.2 us
    ppermute x47, waiting for transfers between devices, swap(): return lax.ppermute(x, BOTH, pairs)  30.1 us
    pallas_call x25, Pallas kernels, call(): pl.pallas_call(kernel, name=name, out_shape=outs, in_specs=ins, out_specs...  16.4 us
    all_to_all x1, blocking collectives, shards(): grams = lax.all_to_all(grams, BOTH, 0, 0, tiled=True)  12.3 us
  transfers between devices with their start and end apart: 48, of which 19 were waited for; matrix products, arithmetic and copies ran while one was open for 0% of the time, Pallas kernels for 9%

profile of v4, /device:TPU:0, one launch (start us, length us, event | category | flops | bytes accessed | tf_op | source)
XLA Modules:
  0.0 106.2 jit_solution(1206694181747827848)
XLA Ops:
  0.6 1.6 %prepare.1 = (f32[64,128]{1,0:T(8,128)S(1)}, f32[4,2,32,512]{3,2,1,0:T(8,128)S(1)}, f32[4,2,32,512]{3,2,1,0:T(8,128)S(1)}, bf16[10,128,128]{2,1,0:T(8,128)(2,1)S(1)}) custom-call(f32[32,8192]{1,0:T(8,128)} %bitcast.6, s32[64,128]{1,0:T(8,128)} %bitcast.7, f32[64,128]{1,0:T(8,128)} %bitcast.8, bf16[64,128,128]{2,1,0:T(8,128)(2,1)} %diag.3, ...), custom_call_target="tpu_custom_call" | custom-call | bytes 3145728 | tf_op jit(solution)/shard_map/prepare/pallas_call | solution.py:121
  2.8 2.6 %collective-permute-start = (bf16[10,128,128]{2,1,0:T(8,128)(2,1)S(1)}, bf16[10,128,128]{2,1,0:T(8,128)(2,1)S(1)}, u32[]{:S(2)}, u32[]{:S(2)}) collective-permute-start(bf16[10,128,128]{2,1,0:T(8,128)(2,1)S(1)} %get-tuple-element.98), channel_id=1, source_target_pairs={{0,4},{1,5},{2,6},{3,7},{4,0},{5,1},{6,2},{7,3},{8,12},{9,13},{10,... | collective-permute-start | bytes 983048 | tf_op jit(solution)/shard_map/ppermute | solution.py:68
  5.4 1.9 %fetch.1 = (bf16[9,128,128]{2,1,0:T(8,128)(2,1)S(1)}, bf16[5,128,128]{2,1,0:T(8,128)(2,1)S(1)}, bf16[12,128,128]{2,1,0:T(8,128)(2,1)S(1)}, bf16[5,128,128]{2,1,0...) custom-call(bf16[64,128,128]{2,1,0:T(8,128)(2,1)} %diag.3, ...), custom_call_target="tpu_custom_call" | custom-call | bytes 3145728 | tf_op jit(solution)/shard_map/fetch/pallas_call | solution.py:121
  8.1 1.9 %collective-permute-start.5 = (bf16[5,128,128]{2,1,0:T(8,128)(2,1)S(1)}, bf16[5,128,128]{2,1,0:T(8,128)(2,1)S(1)}, u32[]{:S(2)}, u32[]{:S(2)}) collective-permute-start(bf16[5,128,128]{2,1,0:T(8,128)(2,1)S(1)} %get-tuple-element.117), channel_id=1, source_target_pairs={{0,4},{1,5},{2,6},{3,7},{4,0},{5,1},{6,2},{7,3},{8,12},{9,13},{10,... | collective-permute-start | bytes 491528 | tf_op jit(solution)/shard_map/ppermute | solution.py:68
  11.6 8.0 %collective-permute-done.2.refs_0_ = f32[2,2,32,512]{3,2,1,0:T(8,128)S(1)} collective-permute-done((f32[2,2,32,512]{3,2,1,0:T(8,128)}, f32[2,2,32,512]{3,2,1,0:T(8,128)S(1)}, u32[]{:S(2)}, u32[]{:S(2)}) %collective-permute-start.2) | collective-permute-done | bytes 262176 | tf_op jit(solution)/shard_map/ppermute | solution.py:68
  19.5 1.9 %collective-permute-start.6 = (bf16[8,128,128]{2,1,0:T(8,128)(2,1)S(1)}, bf16[8,128,128]{2,1,0:T(8,128)(2,1)S(1)}, u32[]{:S(2)}, u32[]{:S(2)}) collective-permute-start(bf16[8,128,128]{2,1,0:T(8,128)(2,1)S(1)} %get-tuple-element.118), channel_id=1, source_target_pairs={{0,4},{1,5},{2,6},{3,7},{4,0},{5,1},{6,2},{7,3},{8,12},{9,13},{10,... | collective-permute-start | bytes 786440 | tf_op jit(solution)/shard_map/ppermute | solution.py:68
  22.8 7.3 %collective-permute-done.3.refs_1_ = f32[2,2,32,512]{3,2,1,0:T(8,128)S(1)} collective-permute-done((f32[2,2,32,512]{3,2,1,0:T(8,128)S(1)}, f32[2,2,32,512]{3,2,1,0:T(8,128)S(1)}, u32[]{:S(2)}, u32[]{:S(2)}) %collective-permute-start.3) | collective-permute-done | bytes 262176 | tf_op jit(solution)/shard_map/ppermute | solution.py:68
  30.4 1.6 %collective-permute-start.8 = (bf16[4,128,128]{2,1,0:T(8,128)(2,1)S(1)}, bf16[4,128,128]{2,1,0:T(8,128)(2,1)S(1)}, u32[]{:S(2)}, u32[]{:S(2)}) collective-permute-start(bf16[4,128,128]{2,1,0:T(8,128)(2,1)S(1)} %get-tuple-element.127), channel_id=1, source_target_pairs={{0,4},{1,3},{2,6},{3,1},{4,0},{5,7},{6,2},{7,5},{8,12},{9,11},{10,... | collective-permute-start | bytes 393224 | tf_op jit(solution)/shard_map/ppermute | solution.py:68
  32.0 1.6 %collective-permute-start.9 = (bf16[128,512]{1,0:T(8,128)(2,1)S(1)}, bf16[128,512]{1,0:T(8,128)(2,1)S(1)}, u32[]{:S(2)}, u32[]{:S(2)}) collective-permute-start(bf16[128,512]{1,0:T(8,128)(2,1)S(1)} %get-tuple-element.128), channel_id=1, source_target_pairs={{0,8},{1,9},{2,10},{3,11},{4,12},{5,13},{6,14},{7,15},{8,0},{9,1},... | collective-permute-start | bytes 393224 | tf_op jit(solution)/shard_map/ppermute | solution.py:68
  38.0 2.7 %collective-permute-start.13 = (bf16[128,512]{1,0:T(8,128)(2,1)S(1)}, bf16[128,512]{1,0:T(8,128)(2,1)S(1)}, u32[]{:S(2)}, u32[]{:S(2)}) collective-permute-start(bf16[128,512]{1,0:T(8,128)(2,1)S(1)} %get-tuple-element.134), channel_id=1, source_target_pairs={{0,8},{1,9},{2,10},{3,11},{4,12},{5,13},{6,14},{7,15},{8,0},{9,1},... | collective-permute-start | bytes 393224 | tf_op jit(solution)/shard_map/ppermute | solution.py:68
  44.1 1.6 %collective-permute-start.16 = (bf16[4,128,128]{2,1,0:T(8,128)(2,1)S(1)}, bf16[4,128,128]{2,1,0:T(8,128)(2,1)S(1)}, u32[]{:S(2)}, u32[]{:S(2)}) collective-permute-start(bf16[4,128,128]{2,1,0:T(8,128)(2,1)S(1)} %get-tuple-element.139), channel_id=1, source_target_pairs={{0,4},{1,3},{2,6},{3,1},{4,0},{5,7},{6,2},{7,5},{8,12},{9,11},{10,... | collective-permute-start | bytes 393224 | tf_op jit(solution)/shard_map/ppermute | solution.py:68
  45.6 2.3 %collective-permute-start.17 = (bf16[128,512]{1,0:T(8,128)(2,1)S(1)}, bf16[128,512]{1,0:T(8,128)(2,1)S(1)}, u32[]{:S(2)}, u32[]{:S(2)}) collective-permute-start(bf16[128,512]{1,0:T(8,128)(2,1)S(1)} %get-tuple-element.140), channel_id=1, source_target_pairs={{0,8},{1,9},{2,10},{3,11},{4,12},{5,13},{6,14},{7,15},{8,0},{9,1},... | collective-permute-start | bytes 393224 | tf_op jit(solution)/shard_map/ppermute | solution.py:68
  49.1 1.8 %collective-permute-done.17.got_1 = bf16[128,512]{1,0:T(8,128)(2,1)S(1)} collective-permute-done((bf16[128,512]{1,0:T(8,128)(2,1)S(1)}, bf16[128,512]{1,0:T(8,128)(2,1)S(1)}, u32[]{:S(2)}, u32[]{:S(2)}) %collective-permute-start.17) | collective-permute-done | bytes 131104 | tf_op jit(solution)/shard_map/ppermute | solution.py:68
  51.9 2.0 %collective-permute-start.21 = (bf16[128,512]{1,0:T(8,128)(2,1)S(1)}, bf16[128,512]{1,0:T(8,128)(2,1)S(1)}, u32[]{:S(2)}, u32[]{:S(2)}) collective-permute-start(bf16[128,512]{1,0:T(8,128)(2,1)S(1)} %get-tuple-element.146), channel_id=1, source_target_pairs={{0,8},{1,9},{2,10},{3,11},{4,12},{5,13},{6,14},{7,15},{8,0},{9,1},... | collective-permute-start | bytes 393224 | tf_op jit(solution)/shard_map/ppermute | solution.py:68
  57.3 1.5 %collective-permute-start.24 = (bf16[4,128,128]{2,1,0:T(8,128)(2,1)S(1)}, bf16[4,128,128]{2,1,0:T(8,128)(2,1)S(1)}, u32[]{:S(2)}, u32[]{:S(2)}) collective-permute-start(bf16[4,128,128]{2,1,0:T(8,128)(2,1)S(1)} %get-tuple-element.151), channel_id=1, source_target_pairs={{0,4},{1,3},{2,6},{3,1},{4,0},{5,7},{6,2},{7,5},{8,12},{9,11},{10,... | collective-permute-start | bytes 393224 | tf_op jit(solution)/shard_map/ppermute | solution.py:68
  58.9 2.0 %collective-permute-start.25 = (bf16[128,512]{1,0:T(8,128)(2,1)S(1)}, bf16[128,512]{1,0:T(8,128)(2,1)S(1)}, u32[]{:S(2)}, u32[]{:S(2)}) collective-permute-start(bf16[128,512]{1,0:T(8,128)(2,1)S(1)} %get-tuple-element.152), channel_id=1, source_target_pairs={{0,8},{1,9},{2,10},{3,11},{4,12},{5,13},{6,14},{7,15},{8,0},{9,1},... | collective-permute-start | bytes 393224 | tf_op jit(solution)/shard_map/ppermute | solution.py:68
  64.9 2.0 %collective-permute-start.29 = (bf16[128,512]{1,0:T(8,128)(2,1)S(1)}, bf16[128,512]{1,0:T(8,128)(2,1)S(1)}, u32[]{:S(2)}, u32[]{:S(2)}) collective-permute-start(bf16[128,512]{1,0:T(8,128)(2,1)S(1)} %get-tuple-element.158), channel_id=1, source_target_pairs={{0,8},{1,9},{2,10},{3,11},{4,12},{5,13},{6,14},{7,15},{8,0},{9,1},... | collective-permute-start | bytes 393224 | tf_op jit(solution)/shard_map/ppermute | solution.py:68
  70.3 1.5 %collective-permute-start.32 = (bf16[4,128,128]{2,1,0:T(8,128)(2,1)S(1)}, bf16[4,128,128]{2,1,0:T(8,128)(2,1)S(1)}, u32[]{:S(2)}, u32[]{:S(2)}) collective-permute-start(bf16[4,128,128]{2,1,0:T(8,128)(2,1)S(1)} %get-tuple-element.163), channel_id=1, source_target_pairs={{0,4},{1,3},{2,6},{3,1},{4,0},{5,7},{6,2},{7,5},{8,12},{9,11},{10,... | collective-permute-start | bytes 393224 | tf_op jit(solution)/shard_map/ppermute | solution.py:68
  71.9 2.0 %collective-permute-start.33 = (bf16[128,512]{1,0:T(8,128)(2,1)S(1)}, bf16[128,512]{1,0:T(8,128)(2,1)S(1)}, u32[]{:S(2)}, u32[]{:S(2)}) collective-permute-start(bf16[128,512]{1,0:T(8,128)(2,1)S(1)} %get-tuple-element.164), channel_id=1, source_target_pairs={{0,8},{1,9},{2,10},{3,11},{4,12},{5,13},{6,14},{7,15},{8,0},{9,1},... | collective-permute-start | bytes 393224 | tf_op jit(solution)/shard_map/ppermute | solution.py:68
  77.9 2.0 %collective-permute-start.37 = (bf16[128,512]{1,0:T(8,128)(2,1)S(1)}, bf16[128,512]{1,0:T(8,128)(2,1)S(1)}, u32[]{:S(2)}, u32[]{:S(2)}) collective-permute-start(bf16[128,512]{1,0:T(8,128)(2,1)S(1)} %get-tuple-element.170), channel_id=1, source_target_pairs={{0,8},{1,9},{2,10},{3,11},{4,12},{5,13},{6,14},{7,15},{8,0},{9,1},... | collective-permute-start | bytes 393224 | tf_op jit(solution)/shard_map/ppermute | solution.py:68
  83.5 1.5 %collective-permute-start.41 = (bf16[4,128,128]{2,1,0:T(8,128)(2,1)S(1)}, bf16[4,128,128]{2,1,0:T(8,128)(2,1)S(1)}, u32[]{:S(2)}, u32[]{:S(2)}) collective-permute-start(bf16[4,128,128]{2,1,0:T(8,128)(2,1)S(1)} %get-tuple-element.178), channel_id=1, source_target_pairs={{0,4},{1,3},{2,6},{3,1},{4,0},{5,7},{6,2},{7,5},{8,12},{9,11},{10,... | collective-permute-start | bytes 393224 | tf_op jit(solution)/shard_map/ppermute | solution.py:68
  85.0 2.0 %collective-permute-start.42 = (bf16[128,512]{1,0:T(8,128)(2,1)S(1)}, bf16[128,512]{1,0:T(8,128)(2,1)S(1)}, u32[]{:S(2)}, u32[]{:S(2)}) collective-permute-start(bf16[128,512]{1,0:T(8,128)(2,1)S(1)} %get-tuple-element.179), channel_id=1, source_target_pairs={{0,8},{1,9},{2,10},{3,11},{4,12},{5,13},{6,14},{7,15},{8,0},{9,1},... | collective-permute-start | bytes 393224 | tf_op jit(solution)/shard_map/ppermute | solution.py:68
  90.4 1.5 %collective-permute-start.47 = (f32[2,2,32,512]{3,2,1,0:T(8,128)S(1)}, f32[2,2,32,512]{3,2,1,0:T(8,128)S(1)}, u32[]{:S(2)}, u32[]{:S(2)}) collective-permute-start(f32[2,2,32,512]{3,2,1,0:T(8,128)S(1)} %get-tuple-element.187), channel_id=1, source_target_pairs={{0,2},{1,3},{2,0},{3,1},{4,6},{5,7},{6,4},{7,5},{8,10},{9,11},{10,... | collective-permute-start | bytes 786440 | tf_op jit(solution)/shard_map/ppermute | solution.py:68
  92.7 12.3 %all_to_all.5.grams = f32[32,8,128]{2,1,0:T(8,128)S(1)} all-to-all(f32[32,8,128]{2,1,0:T(8,128)S(1)} %image.1), channel_id=1, replica_groups=mesh['mesh'=8,'vec'=4] {'mesh','vec'}, dimensions={0} | all-to-all | bytes 262144 | tf_op jit(solution)/shard_map/all_to_all | solution.py:773
  (99 shorter events, 38.1 us)
Async XLA Ops:
  2.8 18.7 %collective-permute-start = (bf16[10,128,128]{2,1,0:T(8,128)(2,1)S(1)}, bf16[10,128,128]{2,1,0:T(8,128)(2,1)S(1)}, u32[]{:S(2)}, u32[]{:S(2)}) collective-permute-start(bf16[10,128,128]{2,1,0:T(8,128)(2,1)S(1)} %get-tuple-element.98), channel_id=1, source_target_pairs={{0,4},{1,5},{2,6},{3,7},{4,0},{5,1},{6,2},{7,3},{8,12},{9,13},{10,... | collective-permute-start | bytes 983048 | tf_op jit(solution)/shard_map/ppermute | solution.py:68
  8.0 11.5 %collective-permute-start.2 = (f32[2,2,32,512]{3,2,1,0:T(8,128)}, f32[2,2,32,512]{3,2,1,0:T(8,128)S(1)}, u32[]{:S(2)}, u32[]{:S(2)}) collective-permute-start(f32[2,2,32,512]{3,2,1,0:T(8,128)} %get-tuple-element.106), channel_id=1, source_target_pairs={{0,4},{1,5},{2,6},{3,7},{4,0},{5,1},{6,2},{7,3},{8,12},{9,13},{10,... | collective-permute-start | bytes 786440 | tf_op jit(solution)/shard_map/ppermute | solution.py:68
  8.1 25.5 %collective-permute-start.5 = (bf16[5,128,128]{2,1,0:T(8,128)(2,1)S(1)}, bf16[5,128,128]{2,1,0:T(8,128)(2,1)S(1)}, u32[]{:S(2)}, u32[]{:S(2)}) collective-permute-start(bf16[5,128,128]{2,1,0:T(8,128)(2,1)S(1)} %get-tuple-element.117), channel_id=1, source_target_pairs={{0,4},{1,5},{2,6},{3,7},{4,0},{5,1},{6,2},{7,3},{8,12},{9,13},{10,... | collective-permute-start | bytes 491528 | tf_op jit(solution)/shard_map/ppermute | solution.py:68
  10.0 20.0 %collective-permute-start.3 = (f32[2,2,32,512]{3,2,1,0:T(8,128)S(1)}, f32[2,2,32,512]{3,2,1,0:T(8,128)S(1)}, u32[]{:S(2)}, u32[]{:S(2)}) collective-permute-start(f32[2,2,32,512]{3,2,1,0:T(8,128)S(1)} %get-tuple-element.109), channel_id=1, source_target_pairs={{0,6},{1,7},{2,4},{3,5},{4,2},{5,3},{6,0},{7,1},{8,14},{9,15},{10,... | collective-permute-start | bytes 786440 | tf_op jit(solution)/shard_map/ppermute | solution.py:68
  11.5 18.5 %collective-permute-start.4 = (f32[2,2,32,512]{3,2,1,0:T(8,128)S(1)}, f32[2,2,32,512]{3,2,1,0:T(8,128)S(1)}, u32[]{:S(2)}, u32[]{:S(2)}) collective-permute-start(f32[2,2,32,512]{3,2,1,0:T(8,128)S(1)} %get-tuple-element.111), channel_id=1, source_target_pairs={{0,2},{1,3},{2,0},{3,1},{4,6},{5,7},{6,4},{7,5},{8,10},{9,11},{10,... | collective-permute-start | bytes 786440 | tf_op jit(solution)/shard_map/ppermute | solution.py:68
  19.5 14.5 %collective-permute-start.6 = (bf16[8,128,128]{2,1,0:T(8,128)(2,1)S(1)}, bf16[8,128,128]{2,1,0:T(8,128)(2,1)S(1)}, u32[]{:S(2)}, u32[]{:S(2)}) collective-permute-start(bf16[8,128,128]{2,1,0:T(8,128)(2,1)S(1)} %get-tuple-element.118), channel_id=1, source_target_pairs={{0,4},{1,5},{2,6},{3,7},{4,0},{5,1},{6,2},{7,3},{8,12},{9,13},{10,... | collective-permute-start | bytes 786440 | tf_op jit(solution)/shard_map/ppermute | solution.py:68
  21.5 13.8 %collective-permute-start.7 = (bf16[5,128,128]{2,1,0:T(8,128)(2,1)S(1)}, bf16[5,128,128]{2,1,0:T(8,128)(2,1)S(1)}, u32[]{:S(2)}, u32[]{:S(2)}) collective-permute-start(bf16[5,128,128]{2,1,0:T(8,128)(2,1)S(1)} %slice_select_fusion), channel_id=1, source_target_pairs={{8,0},{9,1},{10,2},{11,3},{12,4},{13,5},{14,6},{15,7},{16,8},{17,9... | collective-permute-start | bytes 491528 | tf_op jit(solution)/shard_map/ppermute | solution.py:741
  30.4 5.0 %collective-permute-start.8 = (bf16[4,128,128]{2,1,0:T(8,128)(2,1)S(1)}, bf16[4,128,128]{2,1,0:T(8,128)(2,1)S(1)}, u32[]{:S(2)}, u32[]{:S(2)}) collective-permute-start(bf16[4,128,128]{2,1,0:T(8,128)(2,1)S(1)} %get-tuple-element.127), channel_id=1, source_target_pairs={{0,4},{1,3},{2,6},{3,1},{4,0},{5,7},{6,2},{7,5},{8,12},{9,11},{10,... | collective-permute-start | bytes 393224 | tf_op jit(solution)/shard_map/ppermute | solution.py:68
  37.4 5.0 %collective-permute-start.12 = (bf16[4,128,128]{2,1,0:T(8,128)(2,1)S(1)}, bf16[4,128,128]{2,1,0:T(8,128)(2,1)S(1)}, u32[]{:S(2)}, u32[]{:S(2)}) collective-permute-start(bf16[4,128,128]{2,1,0:T(8,128)(2,1)S(1)} %get-tuple-element.133), channel_id=1, source_target_pairs={{0,4},{1,3},{2,6},{3,1},{4,0},{5,7},{6,2},{7,5},{8,12},{9,11},{10,... | collective-permute-start | bytes 393224 | tf_op jit(solution)/shard_map/ppermute | solution.py:68
  38.0 5.6 %collective-permute-start.13 = (bf16[128,512]{1,0:T(8,128)(2,1)S(1)}, bf16[128,512]{1,0:T(8,128)(2,1)S(1)}, u32[]{:S(2)}, u32[]{:S(2)}) collective-permute-start(bf16[128,512]{1,0:T(8,128)(2,1)S(1)} %get-tuple-element.134), channel_id=1, source_target_pairs={{0,8},{1,9},{2,10},{3,11},{4,12},{5,13},{6,14},{7,15},{8,0},{9,1},... | collective-permute-start | bytes 393224 | tf_op jit(solution)/shard_map/ppermute | solution.py:68
  44.1 5.0 %collective-permute-start.16 = (bf16[4,128,128]{2,1,0:T(8,128)(2,1)S(1)}, bf16[4,128,128]{2,1,0:T(8,128)(2,1)S(1)}, u32[]{:S(2)}, u32[]{:S(2)}) collective-permute-start(bf16[4,128,128]{2,1,0:T(8,128)(2,1)S(1)} %get-tuple-element.139), channel_id=1, source_target_pairs={{0,4},{1,3},{2,6},{3,1},{4,0},{5,7},{6,2},{7,5},{8,12},{9,11},{10,... | collective-permute-start | bytes 393224 | tf_op jit(solution)/shard_map/ppermute | solution.py:68
  45.6 5.2 %collective-permute-start.17 = (bf16[128,512]{1,0:T(8,128)(2,1)S(1)}, bf16[128,512]{1,0:T(8,128)(2,1)S(1)}, u32[]{:S(2)}, u32[]{:S(2)}) collective-permute-start(bf16[128,512]{1,0:T(8,128)(2,1)S(1)} %get-tuple-element.140), channel_id=1, source_target_pairs={{0,8},{1,9},{2,10},{3,11},{4,12},{5,13},{6,14},{7,15},{8,0},{9,1},... | collective-permute-start | bytes 393224 | tf_op jit(solution)/shard_map/ppermute | solution.py:68
  51.3 5.0 %collective-permute-start.20 = (bf16[4,128,128]{2,1,0:T(8,128)(2,1)S(1)}, bf16[4,128,128]{2,1,0:T(8,128)(2,1)S(1)}, u32[]{:S(2)}, u32[]{:S(2)}) collective-permute-start(bf16[4,128,128]{2,1,0:T(8,128)(2,1)S(1)} %get-tuple-element.145), channel_id=1, source_target_pairs={{0,4},{1,3},{2,6},{3,1},{4,0},{5,7},{6,2},{7,5},{8,12},{9,11},{10,... | collective-permute-start | bytes 393224 | tf_op jit(solution)/shard_map/ppermute | solution.py:68
  51.9 5.0 %collective-permute-start.21 = (bf16[128,512]{1,0:T(8,128)(2,1)S(1)}, bf16[128,512]{1,0:T(8,128)(2,1)S(1)}, u32[]{:S(2)}, u32[]{:S(2)}) collective-permute-start(bf16[128,512]{1,0:T(8,128)(2,1)S(1)} %get-tuple-element.146), channel_id=1, source_target_pairs={{0,8},{1,9},{2,10},{3,11},{4,12},{5,13},{6,14},{7,15},{8,0},{9,1},... | collective-permute-start | bytes 393224 | tf_op jit(solution)/shard_map/ppermute | solution.py:68
  57.3 5.0 %collective-permute-start.24 = (bf16[4,128,128]{2,1,0:T(8,128)(2,1)S(1)}, bf16[4,128,128]{2,1,0:T(8,128)(2,1)S(1)}, u32[]{:S(2)}, u32[]{:S(2)}) collective-permute-start(bf16[4,128,128]{2,1,0:T(8,128)(2,1)S(1)} %get-tuple-element.151), channel_id=1, source_target_pairs={{0,4},{1,3},{2,6},{3,1},{4,0},{5,7},{6,2},{7,5},{8,12},{9,11},{10,... | collective-permute-start | bytes 393224 | tf_op jit(solution)/shard_map/ppermute | solution.py:68
  58.9 5.0 %collective-permute-start.25 = (bf16[128,512]{1,0:T(8,128)(2,1)S(1)}, bf16[128,512]{1,0:T(8,128)(2,1)S(1)}, u32[]{:S(2)}, u32[]{:S(2)}) collective-permute-start(bf16[128,512]{1,0:T(8,128)(2,1)S(1)} %get-tuple-element.152), channel_id=1, source_target_pairs={{0,8},{1,9},{2,10},{3,11},{4,12},{5,13},{6,14},{7,15},{8,0},{9,1},... | collective-permute-start | bytes 393224 | tf_op jit(solution)/shard_map/ppermute | solution.py:68
  64.3 5.0 %collective-permute-start.28 = (bf16[4,128,128]{2,1,0:T(8,128)(2,1)S(1)}, bf16[4,128,128]{2,1,0:T(8,128)(2,1)S(1)}, u32[]{:S(2)}, u32[]{:S(2)}) collective-permute-start(bf16[4,128,128]{2,1,0:T(8,128)(2,1)S(1)} %get-tuple-element.157), channel_id=1, source_target_pairs={{0,4},{1,3},{2,6},{3,1},{4,0},{5,7},{6,2},{7,5},{8,12},{9,11},{10,... | collective-permute-start | bytes 393224 | tf_op jit(solution)/shard_map/ppermute | solution.py:68
  70.3 5.0 %collective-permute-start.32 = (bf16[4,128,128]{2,1,0:T(8,128)(2,1)S(1)}, bf16[4,128,128]{2,1,0:T(8,128)(2,1)S(1)}, u32[]{:S(2)}, u32[]{:S(2)}) collective-permute-start(bf16[4,128,128]{2,1,0:T(8,128)(2,1)S(1)} %get-tuple-element.163), channel_id=1, source_target_pairs={{0,4},{1,3},{2,6},{3,1},{4,0},{5,7},{6,2},{7,5},{8,12},{9,11},{10,... | collective-permute-start | bytes 393224 | tf_op jit(solution)/shard_map/ppermute | solution.py:68
  77.3 5.0 %collective-permute-start.36 = (bf16[4,128,128]{2,1,0:T(8,128)(2,1)S(1)}, bf16[4,128,128]{2,1,0:T(8,128)(2,1)S(1)}, u32[]{:S(2)}, u32[]{:S(2)}) collective-permute-start(bf16[4,128,128]{2,1,0:T(8,128)(2,1)S(1)} %get-tuple-element.169), channel_id=1, source_target_pairs={{0,4},{1,3},{2,6},{3,1},{4,0},{5,7},{6,2},{7,5},{8,12},{9,11},{10,... | collective-permute-start | bytes 393224 | tf_op jit(solution)/shard_map/ppermute | solution.py:68
  83.5 5.5 %collective-permute-start.41 = (bf16[4,128,128]{2,1,0:T(8,128)(2,1)S(1)}, bf16[4,128,128]{2,1,0:T(8,128)(2,1)S(1)}, u32[]{:S(2)}, u32[]{:S(2)}) collective-permute-start(bf16[4,128,128]{2,1,0:T(8,128)(2,1)S(1)} %get-tuple-element.178), channel_id=1, source_target_pairs={{0,4},{1,3},{2,6},{3,1},{4,0},{5,7},{6,2},{7,5},{8,12},{9,11},{10,... | collective-permute-start | bytes 393224 | tf_op jit(solution)/shard_map/ppermute | solution.py:68
  85.0 5.4 %collective-permute-start.42 = (bf16[128,512]{1,0:T(8,128)(2,1)S(1)}, bf16[128,512]{1,0:T(8,128)(2,1)S(1)}, u32[]{:S(2)}, u32[]{:S(2)}) collective-permute-start(bf16[128,512]{1,0:T(8,128)(2,1)S(1)} %get-tuple-element.179), channel_id=1, source_target_pairs={{0,8},{1,9},{2,10},{3,11},{4,12},{5,13},{6,14},{7,15},{8,0},{9,1},... | collective-permute-start | bytes 393224 | tf_op jit(solution)/shard_map/ppermute | solution.py:68
  88.4 16.6 %collective-permute-start.45 = (f32[2,2,32,512]{3,2,1,0:T(8,128)S(1)}, f32[2,2,32,512]{3,2,1,0:T(8,128)S(1)}, u32[]{:S(2)}, u32[]{:S(2)}) collective-permute-start(f32[2,2,32,512]{3,2,1,0:T(8,128)S(1)} %get-tuple-element.184), channel_id=1, source_target_pairs={{0,4},{1,5},{2,6},{3,7},{4,0},{5,1},{6,2},{7,3},{8,12},{9,13},{10,... | collective-permute-start | bytes 786440 | tf_op jit(solution)/shard_map/ppermute | solution.py:68
  89.0 16.0 %collective-permute-start.46 = (f32[2,2,32,512]{3,2,1,0:T(8,128)S(1)}, f32[2,2,32,512]{3,2,1,0:T(8,128)S(1)}, u32[]{:S(2)}, u32[]{:S(2)}) collective-permute-start(f32[2,2,32,512]{3,2,1,0:T(8,128)S(1)} %get-tuple-element.185), channel_id=1, source_target_pairs={{0,6},{1,7},{2,4},{3,5},{4,2},{5,3},{6,0},{7,1},{8,14},{9,15},{10,... | collective-permute-start | bytes 786440 | tf_op jit(solution)/shard_map/ppermute | solution.py:68
  90.4 14.6 %collective-permute-start.47 = (f32[2,2,32,512]{3,2,1,0:T(8,128)S(1)}, f32[2,2,32,512]{3,2,1,0:T(8,128)S(1)}, u32[]{:S(2)}, u32[]{:S(2)}) collective-permute-start(f32[2,2,32,512]{3,2,1,0:T(8,128)S(1)} %get-tuple-element.187), channel_id=1, source_target_pairs={{0,2},{1,3},{2,0},{3,1},{4,6},{5,7},{6,4},{7,5},{8,10},{9,11},{10,... | collective-permute-start | bytes 786440 | tf_op jit(solution)/shard_map/ppermute | solution.py:68
  (24 other events, 87.0 us)

commit v5 on v4

--- a/solution.py
+++ b/solution.py
@@ -320,7 +320,7 @@
 
 def chip_order(plan):
     pairs = [(dx, dy) for dx in range(2) for dy in range(plan.vecs // 2)]
-    return pairs[plan.vecs // 2 :] + pairs[: plan.vecs // 2]
+    return pairs[plan.vecs // 2 :][::-1] + pairs[: plan.vecs // 2]
 
 
 def chip_at(plan, x, chip, dx, dy):
@@ -733,7 +733,7 @@
     parts = enter(plan, own_entering, plan.swap(entering, plan.core_swap))
     others, *parts = lax.optimization_barrier((others, *parts))
     gots = spread(parts)
-    gots[0], rest = lax.optimization_barrier((gots[0], rest))
+    gots[1], rest = lax.optimization_barrier((gots[1], rest))
     others, rest = plan.swap(others, half), plan.swap(rest, half)
     n_above = plan.run + 1
     above = jnp.where(lax.axis_index("mesh") % 2 == 0, own_first[:n_above], first[:n_above])

time: 107 us -> 106 us (level)
  no operation moved by 1% of the time
where the time goes in v5:
time: 106 us
  starting transfers between devices  46.5 us (44%)
  waiting for transfers between devices  30.1 us (28%)
  Pallas kernels  16.4 us (15%)
  blocking collectives  12 us (11%)
    ppermute x47, starting transfers between devices, swap(): return lax.ppermute(x, BOTH, pairs)  45.2 us
    ppermute x47, waiting for transfers between devices, swap(): return lax.ppermute(x, BOTH, pairs)  30.1 us
    pallas_call x25, Pallas kernels, call(): pl.pallas_call(kernel, name=name, out_shape=outs, in_specs=ins, out_specs...  16.4 us
    all_to_all x1, blocking collectives, shards(): grams = lax.all_to_all(grams, BOTH, 0, 0, tiled=True)  12 us
  transfers between devices with their start and end apart: 48, of which 19 were waited for; matrix products, arithmetic and copies ran while one was open for 0% of the time, Pallas kernels for 9%

profile of v5, /device:TPU:0, one launch (start us, length us, event | category | flops | bytes accessed | tf_op | source)
XLA Modules:
  0.0 105.9 jit_solution(4511435262788613455)
XLA Ops:
  0.6 1.6 %prepare.1 = (f32[64,128]{1,0:T(8,128)S(1)}, f32[4,2,32,512]{3,2,1,0:T(8,128)S(1)}, f32[4,2,32,512]{3,2,1,0:T(8,128)S(1)}, bf16[10,128,128]{2,1,0:T(8,128)(2,1)S(1)}) custom-call(f32[32,8192]{1,0:T(8,128)} %bitcast.6, s32[64,128]{1,0:T(8,128)} %bitcast.7, f32[64,128]{1,0:T(8,128)} %bitcast.8, bf16[64,128,128]{2,1,0:T(8,128)(2,1)} %diag.3, ...), custom_call_target="tpu_custom_call" | custom-call | bytes 3145728 | tf_op jit(solution)/shard_map/prepare/pallas_call | solution.py:121
  2.8 2.6 %collective-permute-start = (bf16[10,128,128]{2,1,0:T(8,128)(2,1)S(1)}, bf16[10,128,128]{2,1,0:T(8,128)(2,1)S(1)}, u32[]{:S(2)}, u32[]{:S(2)}) collective-permute-start(bf16[10,128,128]{2,1,0:T(8,128)(2,1)S(1)} %get-tuple-element.98), channel_id=1, source_target_pairs={{0,4},{1,5},{2,6},{3,7},{4,0},{5,1},{6,2},{7,3},{8,12},{9,13},{10,... | collective-permute-start | bytes 983048 | tf_op jit(solution)/shard_map/ppermute | solution.py:68
  5.4 1.9 %fetch.1 = (bf16[9,128,128]{2,1,0:T(8,128)(2,1)S(1)}, bf16[5,128,128]{2,1,0:T(8,128)(2,1)S(1)}, bf16[12,128,128]{2,1,0:T(8,128)(2,1)S(1)}, bf16[5,128,128]{2,1,0...) custom-call(bf16[64,128,128]{2,1,0:T(8,128)(2,1)} %diag.3, ...), custom_call_target="tpu_custom_call" | custom-call | bytes 3145728 | tf_op jit(solution)/shard_map/fetch/pallas_call | solution.py:121
  8.1 1.9 %collective-permute-start.5 = (bf16[5,128,128]{2,1,0:T(8,128)(2,1)S(1)}, bf16[5,128,128]{2,1,0:T(8,128)(2,1)S(1)}, u32[]{:S(2)}, u32[]{:S(2)}) collective-permute-start(bf16[5,128,128]{2,1,0:T(8,128)(2,1)S(1)} %get-tuple-element.117), channel_id=1, source_target_pairs={{0,4},{1,5},{2,6},{3,7},{4,0},{5,1},{6,2},{7,3},{8,12},{9,13},{10,... | collective-permute-start | bytes 491528 | tf_op jit(solution)/shard_map/ppermute | solution.py:68
  11.6 8.0 %collective-permute-done.3.refs_1_ = f32[2,2,32,512]{3,2,1,0:T(8,128)S(1)} collective-permute-done((f32[2,2,32,512]{3,2,1,0:T(8,128)}, f32[2,2,32,512]{3,2,1,0:T(8,128)S(1)}, u32[]{:S(2)}, u32[]{:S(2)}) %collective-permute-start.3) | collective-permute-done | bytes 262176 | tf_op jit(solution)/shard_map/ppermute | solution.py:68
  19.5 1.9 %collective-permute-start.6 = (bf16[8,128,128]{2,1,0:T(8,128)(2,1)S(1)}, bf16[8,128,128]{2,1,0:T(8,128)(2,1)S(1)}, u32[]{:S(2)}, u32[]{:S(2)}) collective-permute-start(bf16[8,128,128]{2,1,0:T(8,128)(2,1)S(1)} %get-tuple-element.118), channel_id=1, source_target_pairs={{0,4},{1,5},{2,6},{3,7},{4,0},{5,1},{6,2},{7,3},{8,12},{9,13},{10,... | collective-permute-start | bytes 786440 | tf_op jit(solution)/shard_map/ppermute | solution.py:68
  22.8 7.3 %collective-permute-done.2.refs_0_ = f32[2,2,32,512]{3,2,1,0:T(8,128)S(1)} collective-permute-done((f32[2,2,32,512]{3,2,1,0:T(8,128)S(1)}, f32[2,2,32,512]{3,2,1,0:T(8,128)S(1)}, u32[]{:S(2)}, u32[]{:S(2)}) %collective-permute-start.2) | collective-permute-done | bytes 262176 | tf_op jit(solution)/shard_map/ppermute | solution.py:68
  30.4 1.6 %collective-permute-start.8 = (bf16[4,128,128]{2,1,0:T(8,128)(2,1)S(1)}, bf16[4,128,128]{2,1,0:T(8,128)(2,1)S(1)}, u32[]{:S(2)}, u32[]{:S(2)}) collective-permute-start(bf16[4,128,128]{2,1,0:T(8,128)(2,1)S(1)} %get-tuple-element.127), channel_id=1, source_target_pairs={{0,4},{1,3},{2,6},{3,1},{4,0},{5,7},{6,2},{7,5},{8,12},{9,11},{10,... | collective-permute-start | bytes 393224 | tf_op jit(solution)/shard_map/ppermute | solution.py:68
  32.0 1.6 %collective-permute-start.9 = (bf16[128,512]{1,0:T(8,128)(2,1)S(1)}, bf16[128,512]{1,0:T(8,128)(2,1)S(1)}, u32[]{:S(2)}, u32[]{:S(2)}) collective-permute-start(bf16[128,512]{1,0:T(8,128)(2,1)S(1)} %get-tuple-element.128), channel_id=1, source_target_pairs={{0,8},{1,9},{2,10},{3,11},{4,12},{5,13},{6,14},{7,15},{8,0},{9,1},... | collective-permute-start | bytes 393224 | tf_op jit(solution)/shard_map/ppermute | solution.py:68
  38.0 2.7 %collective-permute-start.13 = (bf16[128,512]{1,0:T(8,128)(2,1)S(1)}, bf16[128,512]{1,0:T(8,128)(2,1)S(1)}, u32[]{:S(2)}, u32[]{:S(2)}) collective-permute-start(bf16[128,512]{1,0:T(8,128)(2,1)S(1)} %get-tuple-element.134), channel_id=1, source_target_pairs={{0,8},{1,9},{2,10},{3,11},{4,12},{5,13},{6,14},{7,15},{8,0},{9,1},... | collective-permute-start | bytes 393224 | tf_op jit(solution)/shard_map/ppermute | solution.py:68
  44.1 1.6 %collective-permute-start.16 = (bf16[4,128,128]{2,1,0:T(8,128)(2,1)S(1)}, bf16[4,128,128]{2,1,0:T(8,128)(2,1)S(1)}, u32[]{:S(2)}, u32[]{:S(2)}) collective-permute-start(bf16[4,128,128]{2,1,0:T(8,128)(2,1)S(1)} %get-tuple-element.139), channel_id=1, source_target_pairs={{0,4},{1,3},{2,6},{3,1},{4,0},{5,7},{6,2},{7,5},{8,12},{9,11},{10,... | collective-permute-start | bytes 393224 | tf_op jit(solution)/shard_map/ppermute | solution.py:68
  45.6 2.3 %collective-permute-start.17 = (bf16[128,512]{1,0:T(8,128)(2,1)S(1)}, bf16[128,512]{1,0:T(8,128)(2,1)S(1)}, u32[]{:S(2)}, u32[]{:S(2)}) collective-permute-start(bf16[128,512]{1,0:T(8,128)(2,1)S(1)} %get-tuple-element.140), channel_id=1, source_target_pairs={{0,8},{1,9},{2,10},{3,11},{4,12},{5,13},{6,14},{7,15},{8,0},{9,1},... | collective-permute-start | bytes 393224 | tf_op jit(solution)/shard_map/ppermute | solution.py:68
  49.1 1.8 %collective-permute-done.17.got_1 = bf16[128,512]{1,0:T(8,128)(2,1)S(1)} collective-permute-done((bf16[128,512]{1,0:T(8,128)(2,1)S(1)}, bf16[128,512]{1,0:T(8,128)(2,1)S(1)}, u32[]{:S(2)}, u32[]{:S(2)}) %collective-permute-start.17) | collective-permute-done | bytes 131104 | tf_op jit(solution)/shard_map/ppermute | solution.py:68
  51.9 2.0 %collective-permute-start.21 = (bf16[128,512]{1,0:T(8,128)(2,1)S(1)}, bf16[128,512]{1,0:T(8,128)(2,1)S(1)}, u32[]{:S(2)}, u32[]{:S(2)}) collective-permute-start(bf16[128,512]{1,0:T(8,128)(2,1)S(1)} %get-tuple-element.146), channel_id=1, source_target_pairs={{0,8},{1,9},{2,10},{3,11},{4,12},{5,13},{6,14},{7,15},{8,0},{9,1},... | collective-permute-start | bytes 393224 | tf_op jit(solution)/shard_map/ppermute | solution.py:68
  57.3 1.5 %collective-permute-start.24 = (bf16[4,128,128]{2,1,0:T(8,128)(2,1)S(1)}, bf16[4,128,128]{2,1,0:T(8,128)(2,1)S(1)}, u32[]{:S(2)}, u32[]{:S(2)}) collective-permute-start(bf16[4,128,128]{2,1,0:T(8,128)(2,1)S(1)} %get-tuple-element.151), channel_id=1, source_target_pairs={{0,4},{1,3},{2,6},{3,1},{4,0},{5,7},{6,2},{7,5},{8,12},{9,11},{10,... | collective-permute-start | bytes 393224 | tf_op jit(solution)/shard_map/ppermute | solution.py:68
  58.9 2.0 %collective-permute-start.25 = (bf16[128,512]{1,0:T(8,128)(2,1)S(1)}, bf16[128,512]{1,0:T(8,128)(2,1)S(1)}, u32[]{:S(2)}, u32[]{:S(2)}) collective-permute-start(bf16[128,512]{1,0:T(8,128)(2,1)S(1)} %get-tuple-element.152), channel_id=1, source_target_pairs={{0,8},{1,9},{2,10},{3,11},{4,12},{5,13},{6,14},{7,15},{8,0},{9,1},... | collective-permute-start | bytes 393224 | tf_op jit(solution)/shard_map/ppermute | solution.py:68
  64.9 2.0 %collective-permute-start.29 = (bf16[128,512]{1,0:T(8,128)(2,1)S(1)}, bf16[128,512]{1,0:T(8,128)(2,1)S(1)}, u32[]{:S(2)}, u32[]{:S(2)}) collective-permute-start(bf16[128,512]{1,0:T(8,128)(2,1)S(1)} %get-tuple-element.158), channel_id=1, source_target_pairs={{0,8},{1,9},{2,10},{3,11},{4,12},{5,13},{6,14},{7,15},{8,0},{9,1},... | collective-permute-start | bytes 393224 | tf_op jit(solution)/shard_map/ppermute | solution.py:68
  70.3 1.5 %collective-permute-start.32 = (bf16[4,128,128]{2,1,0:T(8,128)(2,1)S(1)}, bf16[4,128,128]{2,1,0:T(8,128)(2,1)S(1)}, u32[]{:S(2)}, u32[]{:S(2)}) collective-permute-start(bf16[4,128,128]{2,1,0:T(8,128)(2,1)S(1)} %get-tuple-element.163), channel_id=1, source_target_pairs={{0,4},{1,3},{2,6},{3,1},{4,0},{5,7},{6,2},{7,5},{8,12},{9,11},{10,... | collective-permute-start | bytes 393224 | tf_op jit(solution)/shard_map/ppermute | solution.py:68
  71.9 2.0 %collective-permute-start.33 = (bf16[128,512]{1,0:T(8,128)(2,1)S(1)}, bf16[128,512]{1,0:T(8,128)(2,1)S(1)}, u32[]{:S(2)}, u32[]{:S(2)}) collective-permute-start(bf16[128,512]{1,0:T(8,128)(2,1)S(1)} %get-tuple-element.164), channel_id=1, source_target_pairs={{0,8},{1,9},{2,10},{3,11},{4,12},{5,13},{6,14},{7,15},{8,0},{9,1},... | collective-permute-start | bytes 393224 | tf_op jit(solution)/shard_map/ppermute | solution.py:68
  77.9 2.0 %collective-permute-start.37 = (bf16[128,512]{1,0:T(8,128)(2,1)S(1)}, bf16[128,512]{1,0:T(8,128)(2,1)S(1)}, u32[]{:S(2)}, u32[]{:S(2)}) collective-permute-start(bf16[128,512]{1,0:T(8,128)(2,1)S(1)} %get-tuple-element.170), channel_id=1, source_target_pairs={{0,8},{1,9},{2,10},{3,11},{4,12},{5,13},{6,14},{7,15},{8,0},{9,1},... | collective-permute-start | bytes 393224 | tf_op jit(solution)/shard_map/ppermute | solution.py:68
  83.5 1.5 %collective-permute-start.41 = (bf16[4,128,128]{2,1,0:T(8,128)(2,1)S(1)}, bf16[4,128,128]{2,1,0:T(8,128)(2,1)S(1)}, u32[]{:S(2)}, u32[]{:S(2)}) collective-permute-start(bf16[4,128,128]{2,1,0:T(8,128)(2,1)S(1)} %get-tuple-element.178), channel_id=1, source_target_pairs={{0,4},{1,3},{2,6},{3,1},{4,0},{5,7},{6,2},{7,5},{8,12},{9,11},{10,... | collective-permute-start | bytes 393224 | tf_op jit(solution)/shard_map/ppermute | solution.py:68
  85.0 2.0 %collective-permute-start.42 = (bf16[128,512]{1,0:T(8,128)(2,1)S(1)}, bf16[128,512]{1,0:T(8,128)(2,1)S(1)}, u32[]{:S(2)}, u32[]{:S(2)}) collective-permute-start(bf16[128,512]{1,0:T(8,128)(2,1)S(1)} %get-tuple-element.179), channel_id=1, source_target_pairs={{0,8},{1,9},{2,10},{3,11},{4,12},{5,13},{6,14},{7,15},{8,0},{9,1},... | collective-permute-start | bytes 393224 | tf_op jit(solution)/shard_map/ppermute | solution.py:68
  90.4 1.5 %collective-permute-start.47 = (f32[2,2,32,512]{3,2,1,0:T(8,128)S(1)}, f32[2,2,32,512]{3,2,1,0:T(8,128)S(1)}, u32[]{:S(2)}, u32[]{:S(2)}) collective-permute-start(f32[2,2,32,512]{3,2,1,0:T(8,128)S(1)} %get-tuple-element.187), channel_id=1, source_target_pairs={{0,2},{1,3},{2,0},{3,1},{4,6},{5,7},{6,4},{7,5},{8,10},{9,11},{10,... | collective-permute-start | bytes 786440 | tf_op jit(solution)/shard_map/ppermute | solution.py:68
  92.7 12.0 %all_to_all.5.grams = f32[32,8,128]{2,1,0:T(8,128)S(1)} all-to-all(f32[32,8,128]{2,1,0:T(8,128)S(1)} %image.1), channel_id=1, replica_groups=mesh['mesh'=8,'vec'=4] {'mesh','vec'}, dimensions={0} | all-to-all | bytes 262144 | tf_op jit(solution)/shard_map/all_to_all | solution.py:773
  (99 shorter events, 38.1 us)
Async XLA Ops:
  2.8 18.7 %collective-permute-start = (bf16[10,128,128]{2,1,0:T(8,128)(2,1)S(1)}, bf16[10,128,128]{2,1,0:T(8,128)(2,1)S(1)}, u32[]{:S(2)}, u32[]{:S(2)}) collective-permute-start(bf16[10,128,128]{2,1,0:T(8,128)(2,1)S(1)} %get-tuple-element.98), channel_id=1, source_target_pairs={{0,4},{1,5},{2,6},{3,7},{4,0},{5,1},{6,2},{7,3},{8,12},{9,13},{10,... | collective-permute-start | bytes 983048 | tf_op jit(solution)/shard_map/ppermute | solution.py:68
  8.0 11.5 %collective-permute-start.3 = (f32[2,2,32,512]{3,2,1,0:T(8,128)}, f32[2,2,32,512]{3,2,1,0:T(8,128)S(1)}, u32[]{:S(2)}, u32[]{:S(2)}) collective-permute-start(f32[2,2,32,512]{3,2,1,0:T(8,128)} %get-tuple-element.107), channel_id=1, source_target_pairs={{0,4},{1,5},{2,6},{3,7},{4,0},{5,1},{6,2},{7,3},{8,12},{9,13},{10,... | collective-permute-start | bytes 786440 | tf_op jit(solution)/shard_map/ppermute | solution.py:68
  8.1 25.5 %collective-permute-start.5 = (bf16[5,128,128]{2,1,0:T(8,128)(2,1)S(1)}, bf16[5,128,128]{2,1,0:T(8,128)(2,1)S(1)}, u32[]{:S(2)}, u32[]{:S(2)}) collective-permute-start(bf16[5,128,128]{2,1,0:T(8,128)(2,1)S(1)} %get-tuple-element.117), channel_id=1, source_target_pairs={{0,4},{1,5},{2,6},{3,7},{4,0},{5,1},{6,2},{7,3},{8,12},{9,13},{10,... | collective-permute-start | bytes 491528 | tf_op jit(solution)/shard_map/ppermute | solution.py:68
  10.0 20.0 %collective-permute-start.2 = (f32[2,2,32,512]{3,2,1,0:T(8,128)S(1)}, f32[2,2,32,512]{3,2,1,0:T(8,128)S(1)}, u32[]{:S(2)}, u32[]{:S(2)}) collective-permute-start(f32[2,2,32,512]{3,2,1,0:T(8,128)S(1)} %get-tuple-element.106), channel_id=1, source_target_pairs={{0,6},{1,7},{2,4},{3,5},{4,2},{5,3},{6,0},{7,1},{8,14},{9,15},{10,... | collective-permute-start | bytes 786440 | tf_op jit(solution)/shard_map/ppermute | solution.py:68
  11.5 18.5 %collective-permute-start.4 = (f32[2,2,32,512]{3,2,1,0:T(8,128)S(1)}, f32[2,2,32,512]{3,2,1,0:T(8,128)S(1)}, u32[]{:S(2)}, u32[]{:S(2)}) collective-permute-start(f32[2,2,32,512]{3,2,1,0:T(8,128)S(1)} %get-tuple-element.111), channel_id=1, source_target_pairs={{0,2},{1,3},{2,0},{3,1},{4,6},{5,7},{6,4},{7,5},{8,10},{9,11},{10,... | collective-permute-start | bytes 786440 | tf_op jit(solution)/shard_map/ppermute | solution.py:68
  19.5 14.5 %collective-permute-start.6 = (bf16[8,128,128]{2,1,0:T(8,128)(2,1)S(1)}, bf16[8,128,128]{2,1,0:T(8,128)(2,1)S(1)}, u32[]{:S(2)}, u32[]{:S(2)}) collective-permute-start(bf16[8,128,128]{2,1,0:T(8,128)(2,1)S(1)} %get-tuple-element.118), channel_id=1, source_target_pairs={{0,4},{1,5},{2,6},{3,7},{4,0},{5,1},{6,2},{7,3},{8,12},{9,13},{10,... | collective-permute-start | bytes 786440 | tf_op jit(solution)/shard_map/ppermute | solution.py:68
  21.5 13.8 %collective-permute-start.7 = (bf16[5,128,128]{2,1,0:T(8,128)(2,1)S(1)}, bf16[5,128,128]{2,1,0:T(8,128)(2,1)S(1)}, u32[]{:S(2)}, u32[]{:S(2)}) collective-permute-start(bf16[5,128,128]{2,1,0:T(8,128)(2,1)S(1)} %slice_select_fusion), channel_id=1, source_target_pairs={{8,0},{9,1},{10,2},{11,3},{12,4},{13,5},{14,6},{15,7},{16,8},{17,9... | collective-permute-start | bytes 491528 | tf_op jit(solution)/shard_map/ppermute | solution.py:741
  30.4 5.0 %collective-permute-start.8 = (bf16[4,128,128]{2,1,0:T(8,128)(2,1)S(1)}, bf16[4,128,128]{2,1,0:T(8,128)(2,1)S(1)}, u32[]{:S(2)}, u32[]{:S(2)}) collective-permute-start(bf16[4,128,128]{2,1,0:T(8,128)(2,1)S(1)} %get-tuple-element.127), channel_id=1, source_target_pairs={{0,4},{1,3},{2,6},{3,1},{4,0},{5,7},{6,2},{7,5},{8,12},{9,11},{10,... | collective-permute-start | bytes 393224 | tf_op jit(solution)/shard_map/ppermute | solution.py:68
  37.4 5.0 %collective-permute-start.12 = (bf16[4,128,128]{2,1,0:T(8,128)(2,1)S(1)}, bf16[4,128,128]{2,1,0:T(8,128)(2,1)S(1)}, u32[]{:S(2)}, u32[]{:S(2)}) collective-permute-start(bf16[4,128,128]{2,1,0:T(8,128)(2,1)S(1)} %get-tuple-element.133), channel_id=1, source_target_pairs={{0,4},{1,3},{2,6},{3,1},{4,0},{5,7},{6,2},{7,5},{8,12},{9,11},{10,... | collective-permute-start | bytes 393224 | tf_op jit(solution)/shard_map/ppermute | solution.py:68
  38.0 5.7 %collective-permute-start.13 = (bf16[128,512]{1,0:T(8,128)(2,1)S(1)}, bf16[128,512]{1,0:T(8,128)(2,1)S(1)}, u32[]{:S(2)}, u32[]{:S(2)}) collective-permute-start(bf16[128,512]{1,0:T(8,128)(2,1)S(1)} %get-tuple-element.134), channel_id=1, source_target_pairs={{0,8},{1,9},{2,10},{3,11},{4,12},{5,13},{6,14},{7,15},{8,0},{9,1},... | collective-permute-start | bytes 393224 | tf_op jit(solution)/shard_map/ppermute | solution.py:68
  44.1 5.0 %collective-permute-start.16 = (bf16[4,128,128]{2,1,0:T(8,128)(2,1)S(1)}, bf16[4,128,128]{2,1,0:T(8,128)(2,1)S(1)}, u32[]{:S(2)}, u32[]{:S(2)}) collective-permute-start(bf16[4,128,128]{2,1,0:T(8,128)(2,1)S(1)} %get-tuple-element.139), channel_id=1, source_target_pairs={{0,4},{1,3},{2,6},{3,1},{4,0},{5,7},{6,2},{7,5},{8,12},{9,11},{10,... | collective-permute-start | bytes 393224 | tf_op jit(solution)/shard_map/ppermute | solution.py:68
  45.6 5.2 %collective-permute-start.17 = (bf16[128,512]{1,0:T(8,128)(2,1)S(1)}, bf16[128,512]{1,0:T(8,128)(2,1)S(1)}, u32[]{:S(2)}, u32[]{:S(2)}) collective-permute-start(bf16[128,512]{1,0:T(8,128)(2,1)S(1)} %get-tuple-element.140), channel_id=1, source_target_pairs={{0,8},{1,9},{2,10},{3,11},{4,12},{5,13},{6,14},{7,15},{8,0},{9,1},... | collective-permute-start | bytes 393224 | tf_op jit(solution)/shard_map/ppermute | solution.py:68
  51.3 5.0 %collective-permute-start.20 = (bf16[4,128,128]{2,1,0:T(8,128)(2,1)S(1)}, bf16[4,128,128]{2,1,0:T(8,128)(2,1)S(1)}, u32[]{:S(2)}, u32[]{:S(2)}) collective-permute-start(bf16[4,128,128]{2,1,0:T(8,128)(2,1)S(1)} %get-tuple-element.145), channel_id=1, source_target_pairs={{0,4},{1,3},{2,6},{3,1},{4,0},{5,7},{6,2},{7,5},{8,12},{9,11},{10,... | collective-permute-start | bytes 393224 | tf_op jit(solution)/shard_map/ppermute | solution.py:68
  51.9 5.0 %collective-permute-start.21 = (bf16[128,512]{1,0:T(8,128)(2,1)S(1)}, bf16[128,512]{1,0:T(8,128)(2,1)S(1)}, u32[]{:S(2)}, u32[]{:S(2)}) collective-permute-start(bf16[128,512]{1,0:T(8,128)(2,1)S(1)} %get-tuple-element.146), channel_id=1, source_target_pairs={{0,8},{1,9},{2,10},{3,11},{4,12},{5,13},{6,14},{7,15},{8,0},{9,1},... | collective-permute-start | bytes 393224 | tf_op jit(solution)/shard_map/ppermute | solution.py:68
  57.3 5.0 %collective-permute-start.24 = (bf16[4,128,128]{2,1,0:T(8,128)(2,1)S(1)}, bf16[4,128,128]{2,1,0:T(8,128)(2,1)S(1)}, u32[]{:S(2)}, u32[]{:S(2)}) collective-permute-start(bf16[4,128,128]{2,1,0:T(8,128)(2,1)S(1)} %get-tuple-element.151), channel_id=1, source_target_pairs={{0,4},{1,3},{2,6},{3,1},{4,0},{5,7},{6,2},{7,5},{8,12},{9,11},{10,... | collective-permute-start | bytes 393224 | tf_op jit(solution)/shard_map/ppermute | solution.py:68
  64.3 5.0 %collective-permute-start.28 = (bf16[4,128,128]{2,1,0:T(8,128)(2,1)S(1)}, bf16[4,128,128]{2,1,0:T(8,128)(2,1)S(1)}, u32[]{:S(2)}, u32[]{:S(2)}) collective-permute-start(bf16[4,128,128]{2,1,0:T(8,128)(2,1)S(1)} %get-tuple-element.157), channel_id=1, source_target_pairs={{0,4},{1,3},{2,6},{3,1},{4,0},{5,7},{6,2},{7,5},{8,12},{9,11},{10,... | collective-permute-start | bytes 393224 | tf_op jit(solution)/shard_map/ppermute | solution.py:68
  70.3 5.0 %collective-permute-start.32 = (bf16[4,128,128]{2,1,0:T(8,128)(2,1)S(1)}, bf16[4,128,128]{2,1,0:T(8,128)(2,1)S(1)}, u32[]{:S(2)}, u32[]{:S(2)}) collective-permute-start(bf16[4,128,128]{2,1,0:T(8,128)(2,1)S(1)} %get-tuple-element.163), channel_id=1, source_target_pairs={{0,4},{1,3},{2,6},{3,1},{4,0},{5,7},{6,2},{7,5},{8,12},{9,11},{10,... | collective-permute-start | bytes 393224 | tf_op jit(solution)/shard_map/ppermute | solution.py:68
  71.9 5.0 %collective-permute-start.33 = (bf16[128,512]{1,0:T(8,128)(2,1)S(1)}, bf16[128,512]{1,0:T(8,128)(2,1)S(1)}, u32[]{:S(2)}, u32[]{:S(2)}) collective-permute-start(bf16[128,512]{1,0:T(8,128)(2,1)S(1)} %get-tuple-element.164), channel_id=1, source_target_pairs={{0,8},{1,9},{2,10},{3,11},{4,12},{5,13},{6,14},{7,15},{8,0},{9,1},... | collective-permute-start | bytes 393224 | tf_op jit(solution)/shard_map/ppermute | solution.py:68
  77.3 5.0 %collective-permute-start.36 = (bf16[4,128,128]{2,1,0:T(8,128)(2,1)S(1)}, bf16[4,128,128]{2,1,0:T(8,128)(2,1)S(1)}, u32[]{:S(2)}, u32[]{:S(2)}) collective-permute-start(bf16[4,128,128]{2,1,0:T(8,128)(2,1)S(1)} %get-tuple-element.169), channel_id=1, source_target_pairs={{0,4},{1,3},{2,6},{3,1},{4,0},{5,7},{6,2},{7,5},{8,12},{9,11},{10,... | collective-permute-start | bytes 393224 | tf_op jit(solution)/shard_map/ppermute | solution.py:68
  83.5 5.9 %collective-permute-start.41 = (bf16[4,128,128]{2,1,0:T(8,128)(2,1)S(1)}, bf16[4,128,128]{2,1,0:T(8,128)(2,1)S(1)}, u32[]{:S(2)}, u32[]{:S(2)}) collective-permute-start(bf16[4,128,128]{2,1,0:T(8,128)(2,1)S(1)} %get-tuple-element.178), channel_id=1, source_target_pairs={{0,4},{1,3},{2,6},{3,1},{4,0},{5,7},{6,2},{7,5},{8,12},{9,11},{10,... | collective-permute-start | bytes 393224 | tf_op jit(solution)/shard_map/ppermute | solution.py:68
  85.0 5.4 %collective-permute-start.42 = (bf16[128,512]{1,0:T(8,128)(2,1)S(1)}, bf16[128,512]{1,0:T(8,128)(2,1)S(1)}, u32[]{:S(2)}, u32[]{:S(2)}) collective-permute-start(bf16[128,512]{1,0:T(8,128)(2,1)S(1)} %get-tuple-element.179), channel_id=1, source_target_pairs={{0,8},{1,9},{2,10},{3,11},{4,12},{5,13},{6,14},{7,15},{8,0},{9,1},... | collective-permute-start | bytes 393224 | tf_op jit(solution)/shard_map/ppermute | solution.py:68
  88.4 16.4 %collective-permute-start.45 = (f32[2,2,32,512]{3,2,1,0:T(8,128)S(1)}, f32[2,2,32,512]{3,2,1,0:T(8,128)S(1)}, u32[]{:S(2)}, u32[]{:S(2)}) collective-permute-start(f32[2,2,32,512]{3,2,1,0:T(8,128)S(1)} %get-tuple-element.184), channel_id=1, source_target_pairs={{0,6},{1,7},{2,4},{3,5},{4,2},{5,3},{6,0},{7,1},{8,14},{9,15},{10,... | collective-permute-start | bytes 786440 | tf_op jit(solution)/shard_map/ppermute | solution.py:68
  89.4 15.3 %collective-permute-start.46 = (f32[2,2,32,512]{3,2,1,0:T(8,128)S(1)}, f32[2,2,32,512]{3,2,1,0:T(8,128)S(1)}, u32[]{:S(2)}, u32[]{:S(2)}) collective-permute-start(f32[2,2,32,512]{3,2,1,0:T(8,128)S(1)} %get-tuple-element.185), channel_id=1, source_target_pairs={{0,4},{1,5},{2,6},{3,7},{4,0},{5,1},{6,2},{7,3},{8,12},{9,13},{10,... | collective-permute-start | bytes 786440 | tf_op jit(solution)/shard_map/ppermute | solution.py:68
  90.4 14.3 %collective-permute-start.47 = (f32[2,2,32,512]{3,2,1,0:T(8,128)S(1)}, f32[2,2,32,512]{3,2,1,0:T(8,128)S(1)}, u32[]{:S(2)}, u32[]{:S(2)}) collective-permute-start(f32[2,2,32,512]{3,2,1,0:T(8,128)S(1)} %get-tuple-element.187), channel_id=1, source_target_pairs={{0,2},{1,3},{2,0},{3,1},{4,6},{5,7},{6,4},{7,5},{8,10},{9,11},{10,... | collective-permute-start | bytes 786440 | tf_op jit(solution)/shard_map/ppermute | solution.py:68
  (24 other events, 87.0 us)

commit v6 on v5

--- a/solution.py
+++ b/solution.py
@@ -731,9 +731,8 @@
 
     first = plan.swap(first, half)
     parts = enter(plan, own_entering, plan.swap(entering, plan.core_swap))
-    others, *parts = lax.optimization_barrier((others, *parts))
     gots = spread(parts)
-    gots[1], rest = lax.optimization_barrier((gots[1], rest))
+    gots[1], others, rest = lax.optimization_barrier((gots[1], others, rest))
     others, rest = plan.swap(others, half), plan.swap(rest, half)
     n_above = plan.run + 1
     above = jnp.where(lax.axis_index("mesh") % 2 == 0, own_first[:n_above], first[:n_above])

time: 106 us -> 107 us (level)
  transfers between devices with their start and end apart: 48 -> 48, of which waited for: 19 -> 18; matrix products, arithmetic and copies ran while one was open for 0% -> 0% of each run, Pallas kernels for 9% -> 9%
where the time goes in v6:
time: 107 us; the launch traced here: 106 us
  starting transfers between devices  46 us (43%)
  waiting for transfers between devices  30.8 us (29%)
  Pallas kernels  16.4 us (15%)
  blocking collectives  12.1 us (11%)
    ppermute x47, starting transfers between devices, swap(): return lax.ppermute(x, BOTH, pairs)  44.7 us
    ppermute x47, waiting for transfers between devices, swap(): return lax.ppermute(x, BOTH, pairs)  30.8 us
    pallas_call x25, Pallas kernels, call(): pl.pallas_call(kernel, name=name, out_shape=outs, in_specs=ins, out_specs...  16.4 us
    all_to_all x1, blocking collectives, shards(): grams = lax.all_to_all(grams, BOTH, 0, 0, tiled=True)  12.1 us
  transfers between devices with their start and end apart: 48, of which 18 were waited for; matrix products, arithmetic and copies ran while one was open for 0% of the time, Pallas kernels for 9%

profile of v6, /device:TPU:0, one launch (start us, length us, event | category | flops | bytes accessed | tf_op | source)
XLA Modules:
  0.0 106.2 jit_solution(16745091658225076855)
XLA Ops:
  0.6 1.6 %prepare.1 = (f32[64,128]{1,0:T(8,128)S(1)}, f32[4,2,32,512]{3,2,1,0:T(8,128)S(1)}, f32[4,2,32,512]{3,2,1,0:T(8,128)S(1)}, bf16[10,128,128]{2,1,0:T(8,128)(2,1)S(1)}) custom-call(f32[32,8192]{1,0:T(8,128)} %bitcast.6, s32[64,128]{1,0:T(8,128)} %bitcast.7, f32[64,128]{1,0:T(8,128)} %bitcast.8, bf16[64,128,128]{2,1,0:T(8,128)(2,1)} %diag.3, ...), custom_call_target="tpu_custom_call" | custom-call | bytes 3145728 | tf_op jit(solution)/shard_map/prepare/pallas_call | solution.py:121
  2.8 2.6 %collective-permute-start = (bf16[10,128,128]{2,1,0:T(8,128)(2,1)S(1)}, bf16[10,128,128]{2,1,0:T(8,128)(2,1)S(1)}, u32[]{:S(2)}, u32[]{:S(2)}) collective-permute-start(bf16[10,128,128]{2,1,0:T(8,128)(2,1)S(1)} %get-tuple-element.94), channel_id=1, source_target_pairs={{0,4},{1,5},{2,6},{3,7},{4,0},{5,1},{6,2},{7,3},{8,12},{9,13},{10,... | collective-permute-start | bytes 983048 | tf_op jit(solution)/shard_map/ppermute | solution.py:68
  6.1 1.8 %collective-permute-start.3 = (f32[2,2,32,512]{3,2,1,0:T(8,128)}, f32[2,2,32,512]{3,2,1,0:T(8,128)S(1)}, u32[]{:S(2)}, u32[]{:S(2)}) collective-permute-start(f32[2,2,32,512]{3,2,1,0:T(8,128)} %get-tuple-element.98), channel_id=1, source_target_pairs={{0,4},{1,5},{2,6},{3,7},{4,0},{5,1},{6,2},{7,3},{8,12},{9,13},{10,... | collective-permute-start | bytes 786440 | tf_op jit(solution)/shard_map/ppermute | solution.py:68
  8.0 1.9 %fetch.1 = (bf16[9,128,128]{2,1,0:T(8,128)(2,1)S(1)}, bf16[5,128,128]{2,1,0:T(8,128)(2,1)S(1)}, bf16[12,128,128]{2,1,0:T(8,128)(2,1)S(1)}, bf16[5,128,128]{2,1,0...) custom-call(bf16[64,128,128]{2,1,0:T(8,128)(2,1)} %diag.3, ...), custom_call_target="tpu_custom_call" | custom-call | bytes 3145728 | tf_op jit(solution)/shard_map/fetch/pallas_call | solution.py:121
  9.8 1.6 %collective-permute-start.2 = (f32[2,2,32,512]{3,2,1,0:T(8,128)S(1)}, f32[2,2,32,512]{3,2,1,0:T(8,128)S(1)}, u32[]{:S(2)}, u32[]{:S(2)}) collective-permute-start(f32[2,2,32,512]{3,2,1,0:T(8,128)S(1)} %get-tuple-element.97), channel_id=1, source_target_pairs={{0,6},{1,7},{2,4},{3,5},{4,2},{5,3},{6,0},{7,1},{8,14},{9,15},{10,... | collective-permute-start | bytes 786440 | tf_op jit(solution)/shard_map/ppermute | solution.py:68
  11.6 8.0 %collective-permute-done.3.refs_1_ = f32[2,2,32,512]{3,2,1,0:T(8,128)S(1)} collective-permute-done((f32[2,2,32,512]{3,2,1,0:T(8,128)}, f32[2,2,32,512]{3,2,1,0:T(8,128)S(1)}, u32[]{:S(2)}, u32[]{:S(2)}) %collective-permute-start.3) | collective-permute-done | bytes 262176 | tf_op jit(solution)/shard_map/ppermute | solution.py:68
  19.5 1.9 %collective-permute-start.5 = (bf16[5,128,128]{2,1,0:T(8,128)(2,1)S(1)}, bf16[5,128,128]{2,1,0:T(8,128)(2,1)S(1)}, u32[]{:S(2)}, u32[]{:S(2)}) collective-permute-start(bf16[5,128,128]{2,1,0:T(8,128)(2,1)S(1)} %get-tuple-element.109), channel_id=1, source_target_pairs={{0,4},{1,5},{2,6},{3,7},{4,0},{5,1},{6,2},{7,3},{8,12},{9,13},{10,... | collective-permute-start | bytes 491528 | tf_op jit(solution)/shard_map/ppermute | solution.py:68
  22.9 3.7 %collective-permute-done.2.refs_0_ = f32[2,2,32,512]{3,2,1,0:T(8,128)S(1)} collective-permute-done((f32[2,2,32,512]{3,2,1,0:T(8,128)S(1)}, f32[2,2,32,512]{3,2,1,0:T(8,128)S(1)}, u32[]{:S(2)}, u32[]{:S(2)}) %collective-permute-start.2) | collective-permute-done | bytes 262176 | tf_op jit(solution)/shard_map/ppermute | solution.py:68
  26.9 1.6 %collective-permute-start.8 = (bf16[4,128,128]{2,1,0:T(8,128)(2,1)S(1)}, bf16[4,128,128]{2,1,0:T(8,128)(2,1)S(1)}, u32[]{:S(2)}, u32[]{:S(2)}) collective-permute-start(bf16[4,128,128]{2,1,0:T(8,128)(2,1)S(1)} %get-tuple-element.119), channel_id=1, source_target_pairs={{0,4},{1,3},{2,6},{3,1},{4,0},{5,7},{6,2},{7,5},{8,12},{9,11},{10,... | collective-permute-start | bytes 393224 | tf_op jit(solution)/shard_map/ppermute | solution.py:68
  28.5 1.6 %collective-permute-start.9 = (bf16[128,512]{1,0:T(8,128)(2,1)S(1)}, bf16[128,512]{1,0:T(8,128)(2,1)S(1)}, u32[]{:S(2)}, u32[]{:S(2)}) collective-permute-start(bf16[128,512]{1,0:T(8,128)(2,1)S(1)} %get-tuple-element.120), channel_id=1, source_target_pairs={{0,8},{1,9},{2,10},{3,11},{4,12},{5,13},{6,14},{7,15},{8,0},{9,1},... | collective-permute-start | bytes 393224 | tf_op jit(solution)/shard_map/ppermute | solution.py:68
  30.0 4.0 %collective-permute-done.6.rest = bf16[8,128,128]{2,1,0:T(8,128)(2,1)S(1)} collective-permute-done((bf16[8,128,128]{2,1,0:T(8,128)(2,1)S(1)}, bf16[8,128,128]{2,1,0:T(8,128)(2,1)S(1)}, u32[]{:S(2)}, u32[]{:S(2)}) %collective-permute-start.6) | collective-permute-done | bytes 262176 | tf_op jit(solution)/shard_map/ppermute | solution.py:68
  35.9 1.8 %collective-permute-start.12 = (bf16[4,128,128]{2,1,0:T(8,128)(2,1)S(1)}, bf16[4,128,128]{2,1,0:T(8,128)(2,1)S(1)}, u32[]{:S(2)}, u32[]{:S(2)}) collective-permute-start(bf16[4,128,128]{2,1,0:T(8,128)(2,1)S(1)} %get-tuple-element.125), channel_id=1, source_target_pairs={{0,4},{1,3},{2,6},{3,1},{4,0},{5,7},{6,2},{7,5},{8,12},{9,11},{10,... | collective-permute-start | bytes 393224 | tf_op jit(solution)/shard_map/ppermute | solution.py:68
  37.7 1.6 %collective-permute-start.13 = (bf16[128,512]{1,0:T(8,128)(2,1)S(1)}, bf16[128,512]{1,0:T(8,128)(2,1)S(1)}, u32[]{:S(2)}, u32[]{:S(2)}) collective-permute-start(bf16[128,512]{1,0:T(8,128)(2,1)S(1)} %get-tuple-element.126), channel_id=1, source_target_pairs={{0,8},{1,9},{2,10},{3,11},{4,12},{5,13},{6,14},{7,15},{8,0},{9,1},... | collective-permute-start | bytes 393224 | tf_op jit(solution)/shard_map/ppermute | solution.py:68
  40.9 2.3 %collective-permute-done.13.got_1 = bf16[128,512]{1,0:T(8,128)(2,1)S(1)} collective-permute-done((bf16[128,512]{1,0:T(8,128)(2,1)S(1)}, bf16[128,512]{1,0:T(8,128)(2,1)S(1)}, u32[]{:S(2)}, u32[]{:S(2)}) %collective-permute-start.13) | collective-permute-done | bytes 131104 | tf_op jit(solution)/shard_map/ppermute | solution.py:68
  44.6 3.1 %collective-permute-start.17 = (bf16[128,512]{1,0:T(8,128)(2,1)S(1)}, bf16[128,512]{1,0:T(8,128)(2,1)S(1)}, u32[]{:S(2)}, u32[]{:S(2)}) collective-permute-start(bf16[128,512]{1,0:T(8,128)(2,1)S(1)} %get-tuple-element.132), channel_id=1, source_target_pairs={{0,8},{1,9},{2,10},{3,11},{4,12},{5,13},{6,14},{7,15},{8,0},{9,1},... | collective-permute-start | bytes 393224 | tf_op jit(solution)/shard_map/ppermute | solution.py:68
  48.9 1.8 %collective-permute-done.17.got_1 = bf16[128,512]{1,0:T(8,128)(2,1)S(1)} collective-permute-done((bf16[128,512]{1,0:T(8,128)(2,1)S(1)}, bf16[128,512]{1,0:T(8,128)(2,1)S(1)}, u32[]{:S(2)}, u32[]{:S(2)}) %collective-permute-start.17) | collective-permute-done | bytes 131104 | tf_op jit(solution)/shard_map/ppermute | solution.py:68
  52.1 1.9 %collective-permute-start.21 = (bf16[128,512]{1,0:T(8,128)(2,1)S(1)}, bf16[128,512]{1,0:T(8,128)(2,1)S(1)}, u32[]{:S(2)}, u32[]{:S(2)}) collective-permute-start(bf16[128,512]{1,0:T(8,128)(2,1)S(1)} %get-tuple-element.138), channel_id=1, source_target_pairs={{0,8},{1,9},{2,10},{3,11},{4,12},{5,13},{6,14},{7,15},{8,0},{9,1},... | collective-permute-start | bytes 393224 | tf_op jit(solution)/shard_map/ppermute | solution.py:68
  59.1 1.7 %collective-permute-start.25 = (bf16[128,512]{1,0:T(8,128)(2,1)S(1)}, bf16[128,512]{1,0:T(8,128)(2,1)S(1)}, u32[]{:S(2)}, u32[]{:S(2)}) collective-permute-start(bf16[128,512]{1,0:T(8,128)(2,1)S(1)} %get-tuple-element.144), channel_id=1, source_target_pairs={{0,8},{1,9},{2,10},{3,11},{4,12},{5,13},{6,14},{7,15},{8,0},{9,1},... | collective-permute-start | bytes 393224 | tf_op jit(solution)/shard_map/ppermute | solution.py:68
  65.1 2.0 %collective-permute-start.29 = (bf16[128,512]{1,0:T(8,128)(2,1)S(1)}, bf16[128,512]{1,0:T(8,128)(2,1)S(1)}, u32[]{:S(2)}, u32[]{:S(2)}) collective-permute-start(bf16[128,512]{1,0:T(8,128)(2,1)S(1)} %get-tuple-element.150), channel_id=1, source_target_pairs={{0,8},{1,9},{2,10},{3,11},{4,12},{5,13},{6,14},{7,15},{8,0},{9,1},... | collective-permute-start | bytes 393224 | tf_op jit(solution)/shard_map/ppermute | solution.py:68
  72.0 2.0 %collective-permute-start.33 = (bf16[128,512]{1,0:T(8,128)(2,1)S(1)}, bf16[128,512]{1,0:T(8,128)(2,1)S(1)}, u32[]{:S(2)}, u32[]{:S(2)}) collective-permute-start(bf16[128,512]{1,0:T(8,128)(2,1)S(1)} %get-tuple-element.156), channel_id=1, source_target_pairs={{0,8},{1,9},{2,10},{3,11},{4,12},{5,13},{6,14},{7,15},{8,0},{9,1},... | collective-permute-start | bytes 393224 | tf_op jit(solution)/shard_map/ppermute | solution.py:68
  78.1 2.0 %collective-permute-start.37 = (bf16[128,512]{1,0:T(8,128)(2,1)S(1)}, bf16[128,512]{1,0:T(8,128)(2,1)S(1)}, u32[]{:S(2)}, u32[]{:S(2)}) collective-permute-start(bf16[128,512]{1,0:T(8,128)(2,1)S(1)} %get-tuple-element.162), channel_id=1, source_target_pairs={{0,8},{1,9},{2,10},{3,11},{4,12},{5,13},{6,14},{7,15},{8,0},{9,1},... | collective-permute-start | bytes 393224 | tf_op jit(solution)/shard_map/ppermute | solution.py:68
  85.2 2.0 %collective-permute-start.42 = (bf16[128,512]{1,0:T(8,128)(2,1)S(1)}, bf16[128,512]{1,0:T(8,128)(2,1)S(1)}, u32[]{:S(2)}, u32[]{:S(2)}) collective-permute-start(bf16[128,512]{1,0:T(8,128)(2,1)S(1)} %get-tuple-element.171), channel_id=1, source_target_pairs={{0,8},{1,9},{2,10},{3,11},{4,12},{5,13},{6,14},{7,15},{8,0},{9,1},... | collective-permute-start | bytes 393224 | tf_op jit(solution)/shard_map/ppermute | solution.py:68
  88.5 1.7 %collective-permute-start.45 = (f32[2,2,32,512]{3,2,1,0:T(8,128)S(1)}, f32[2,2,32,512]{3,2,1,0:T(8,128)S(1)}, u32[]{:S(2)}, u32[]{:S(2)}) collective-permute-start(f32[2,2,32,512]{3,2,1,0:T(8,128)S(1)} %get-tuple-element.176), channel_id=1, source_target_pairs={{0,6},{1,7},{2,4},{3,5},{4,2},{5,3},{6,0},{7,1},{8,14},{9,15},{10,... | collective-permute-start | bytes 786440 | tf_op jit(solution)/shard_map/ppermute | solution.py:68
  92.9 12.1 %all_to_all.5.grams = f32[32,8,128]{2,1,0:T(8,128)S(1)} all-to-all(f32[32,8,128]{2,1,0:T(8,128)S(1)} %image.1), channel_id=1, replica_groups=mesh['mesh'=8,'vec'=4] {'mesh','vec'}, dimensions={0} | all-to-all | bytes 262144 | tf_op jit(solution)/shard_map/all_to_all | solution.py:772
  (99 shorter events, 38.9 us)
Async XLA Ops:
  2.8 18.8 %collective-permute-start = (bf16[10,128,128]{2,1,0:T(8,128)(2,1)S(1)}, bf16[10,128,128]{2,1,0:T(8,128)(2,1)S(1)}, u32[]{:S(2)}, u32[]{:S(2)}) collective-permute-start(bf16[10,128,128]{2,1,0:T(8,128)(2,1)S(1)} %get-tuple-element.94), channel_id=1, source_target_pairs={{0,4},{1,5},{2,6},{3,7},{4,0},{5,1},{6,2},{7,3},{8,12},{9,13},{10,... | collective-permute-start | bytes 983048 | tf_op jit(solution)/shard_map/ppermute | solution.py:68
  6.1 13.4 %collective-permute-start.3 = (f32[2,2,32,512]{3,2,1,0:T(8,128)}, f32[2,2,32,512]{3,2,1,0:T(8,128)S(1)}, u32[]{:S(2)}, u32[]{:S(2)}) collective-permute-start(f32[2,2,32,512]{3,2,1,0:T(8,128)} %get-tuple-element.98), channel_id=1, source_target_pairs={{0,4},{1,5},{2,6},{3,7},{4,0},{5,1},{6,2},{7,3},{8,12},{9,13},{10,... | collective-permute-start | bytes 786440 | tf_op jit(solution)/shard_map/ppermute | solution.py:68
  9.8 16.7 %collective-permute-start.2 = (f32[2,2,32,512]{3,2,1,0:T(8,128)S(1)}, f32[2,2,32,512]{3,2,1,0:T(8,128)S(1)}, u32[]{:S(2)}, u32[]{:S(2)}) collective-permute-start(f32[2,2,32,512]{3,2,1,0:T(8,128)S(1)} %get-tuple-element.97), channel_id=1, source_target_pairs={{0,6},{1,7},{2,4},{3,5},{4,2},{5,3},{6,0},{7,1},{8,14},{9,15},{10,... | collective-permute-start | bytes 786440 | tf_op jit(solution)/shard_map/ppermute | solution.py:68
  11.4 15.2 %collective-permute-start.4 = (f32[2,2,32,512]{3,2,1,0:T(8,128)S(1)}, f32[2,2,32,512]{3,2,1,0:T(8,128)S(1)}, u32[]{:S(2)}, u32[]{:S(2)}) collective-permute-start(f32[2,2,32,512]{3,2,1,0:T(8,128)S(1)} %get-tuple-element.103), channel_id=1, source_target_pairs={{0,2},{1,3},{2,0},{3,1},{4,6},{5,7},{6,4},{7,5},{8,10},{9,11},{10,... | collective-permute-start | bytes 786440 | tf_op jit(solution)/shard_map/ppermute | solution.py:68
  19.5 10.5 %collective-permute-start.5 = (bf16[5,128,128]{2,1,0:T(8,128)(2,1)S(1)}, bf16[5,128,128]{2,1,0:T(8,128)(2,1)S(1)}, u32[]{:S(2)}, u32[]{:S(2)}) collective-permute-start(bf16[5,128,128]{2,1,0:T(8,128)(2,1)S(1)} %get-tuple-element.109), channel_id=1, source_target_pairs={{0,4},{1,5},{2,6},{3,7},{4,0},{5,1},{6,2},{7,3},{8,12},{9,13},{10,... | collective-permute-start | bytes 491528 | tf_op jit(solution)/shard_map/ppermute | solution.py:68
  21.5 12.5 %collective-permute-start.6 = (bf16[8,128,128]{2,1,0:T(8,128)(2,1)S(1)}, bf16[8,128,128]{2,1,0:T(8,128)(2,1)S(1)}, u32[]{:S(2)}, u32[]{:S(2)}) collective-permute-start(bf16[8,128,128]{2,1,0:T(8,128)(2,1)S(1)} %get-tuple-element.110), channel_id=1, source_target_pairs={{0,4},{1,5},{2,6},{3,7},{4,0},{5,1},{6,2},{7,3},{8,12},{9,13},{10,... | collective-permute-start | bytes 786440 | tf_op jit(solution)/shard_map/ppermute | solution.py:68
  21.6 13.7 %collective-permute-start.7 = (bf16[5,128,128]{2,1,0:T(8,128)(2,1)S(1)}, bf16[5,128,128]{2,1,0:T(8,128)(2,1)S(1)}, u32[]{:S(2)}, u32[]{:S(2)}) collective-permute-start(bf16[5,128,128]{2,1,0:T(8,128)(2,1)S(1)} %slice_select_fusion), channel_id=1, source_target_pairs={{8,0},{9,1},{10,2},{11,3},{12,4},{13,5},{14,6},{15,7},{16,8},{17,9... | collective-permute-start | bytes 491528 | tf_op jit(solution)/shard_map/ppermute | solution.py:740
  26.9 8.5 %collective-permute-start.8 = (bf16[4,128,128]{2,1,0:T(8,128)(2,1)S(1)}, bf16[4,128,128]{2,1,0:T(8,128)(2,1)S(1)}, u32[]{:S(2)}, u32[]{:S(2)}) collective-permute-start(bf16[4,128,128]{2,1,0:T(8,128)(2,1)S(1)} %get-tuple-element.119), channel_id=1, source_target_pairs={{0,4},{1,3},{2,6},{3,1},{4,0},{5,7},{6,2},{7,5},{8,12},{9,11},{10,... | collective-permute-start | bytes 393224 | tf_op jit(solution)/shard_map/ppermute | solution.py:68
  28.5 7.0 %collective-permute-start.9 = (bf16[128,512]{1,0:T(8,128)(2,1)S(1)}, bf16[128,512]{1,0:T(8,128)(2,1)S(1)}, u32[]{:S(2)}, u32[]{:S(2)}) collective-permute-start(bf16[128,512]{1,0:T(8,128)(2,1)S(1)} %get-tuple-element.120), channel_id=1, source_target_pairs={{0,8},{1,9},{2,10},{3,11},{4,12},{5,13},{6,14},{7,15},{8,0},{9,1},... | collective-permute-start | bytes 393224 | tf_op jit(solution)/shard_map/ppermute | solution.py:68
  30.0 5.4 %collective-permute-start.10 = (bf16[128,512]{1,0:T(8,128)(2,1)S(1)}, bf16[128,512]{1,0:T(8,128)(2,1)S(1)}, u32[]{:S(2)}, u32[]{:S(2)}) collective-permute-start(bf16[128,512]{1,0:T(8,128)(2,1)S(1)} %get-tuple-element.121), channel_id=1, source_target_pairs={{0,1},{1,0},{2,3},{3,2},{4,5},{5,4},{6,7},{7,6},{8,16},{9,17},{10,... | collective-permute-start | bytes 393224 | tf_op jit(solution)/shard_map/ppermute | solution.py:68
  35.9 5.0 %collective-permute-start.12 = (bf16[4,128,128]{2,1,0:T(8,128)(2,1)S(1)}, bf16[4,128,128]{2,1,0:T(8,128)(2,1)S(1)}, u32[]{:S(2)}, u32[]{:S(2)}) collective-permute-start(bf16[4,128,128]{2,1,0:T(8,128)(2,1)S(1)} %get-tuple-element.125), channel_id=1, source_target_pairs={{0,4},{1,3},{2,6},{3,1},{4,0},{5,7},{6,2},{7,5},{8,12},{9,11},{10,... | collective-permute-start | bytes 393224 | tf_op jit(solution)/shard_map/ppermute | solution.py:68
  37.7 5.5 %collective-permute-start.13 = (bf16[128,512]{1,0:T(8,128)(2,1)S(1)}, bf16[128,512]{1,0:T(8,128)(2,1)S(1)}, u32[]{:S(2)}, u32[]{:S(2)}) collective-permute-start(bf16[128,512]{1,0:T(8,128)(2,1)S(1)} %get-tuple-element.126), channel_id=1, source_target_pairs={{0,8},{1,9},{2,10},{3,11},{4,12},{5,13},{6,14},{7,15},{8,0},{9,1},... | collective-permute-start | bytes 393224 | tf_op jit(solution)/shard_map/ppermute | solution.py:68
  43.7 5.2 %collective-permute-start.16 = (bf16[4,128,128]{2,1,0:T(8,128)(2,1)S(1)}, bf16[4,128,128]{2,1,0:T(8,128)(2,1)S(1)}, u32[]{:S(2)}, u32[]{:S(2)}) collective-permute-start(bf16[4,128,128]{2,1,0:T(8,128)(2,1)S(1)} %get-tuple-element.131), channel_id=1, source_target_pairs={{0,4},{1,3},{2,6},{3,1},{4,0},{5,7},{6,2},{7,5},{8,12},{9,11},{10,... | collective-permute-start | bytes 393224 | tf_op jit(solution)/shard_map/ppermute | solution.py:68
  44.6 6.1 %collective-permute-start.17 = (bf16[128,512]{1,0:T(8,128)(2,1)S(1)}, bf16[128,512]{1,0:T(8,128)(2,1)S(1)}, u32[]{:S(2)}, u32[]{:S(2)}) collective-permute-start(bf16[128,512]{1,0:T(8,128)(2,1)S(1)} %get-tuple-element.132), channel_id=1, source_target_pairs={{0,8},{1,9},{2,10},{3,11},{4,12},{5,13},{6,14},{7,15},{8,0},{9,1},... | collective-permute-start | bytes 393224 | tf_op jit(solution)/shard_map/ppermute | solution.py:68
  51.1 5.0 %collective-permute-start.20 = (bf16[4,128,128]{2,1,0:T(8,128)(2,1)S(1)}, bf16[4,128,128]{2,1,0:T(8,128)(2,1)S(1)}, u32[]{:S(2)}, u32[]{:S(2)}) collective-permute-start(bf16[4,128,128]{2,1,0:T(8,128)(2,1)S(1)} %get-tuple-element.137), channel_id=1, source_target_pairs={{0,4},{1,3},{2,6},{3,1},{4,0},{5,7},{6,2},{7,5},{8,12},{9,11},{10,... | collective-permute-start | bytes 393224 | tf_op jit(solution)/shard_map/ppermute | solution.py:68
  57.5 5.0 %collective-permute-start.24 = (bf16[4,128,128]{2,1,0:T(8,128)(2,1)S(1)}, bf16[4,128,128]{2,1,0:T(8,128)(2,1)S(1)}, u32[]{:S(2)}, u32[]{:S(2)}) collective-permute-start(bf16[4,128,128]{2,1,0:T(8,128)(2,1)S(1)} %get-tuple-element.143), channel_id=1, source_target_pairs={{0,4},{1,3},{2,6},{3,1},{4,0},{5,7},{6,2},{7,5},{8,12},{9,11},{10,... | collective-permute-start | bytes 393224 | tf_op jit(solution)/shard_map/ppermute | solution.py:68
  64.5 5.0 %collective-permute-start.28 = (bf16[4,128,128]{2,1,0:T(8,128)(2,1)S(1)}, bf16[4,128,128]{2,1,0:T(8,128)(2,1)S(1)}, u32[]{:S(2)}, u32[]{:S(2)}) collective-permute-start(bf16[4,128,128]{2,1,0:T(8,128)(2,1)S(1)} %get-tuple-element.149), channel_id=1, source_target_pairs={{0,4},{1,3},{2,6},{3,1},{4,0},{5,7},{6,2},{7,5},{8,12},{9,11},{10,... | collective-permute-start | bytes 393224 | tf_op jit(solution)/shard_map/ppermute | solution.py:68
  70.5 5.0 %collective-permute-start.32 = (bf16[4,128,128]{2,1,0:T(8,128)(2,1)S(1)}, bf16[4,128,128]{2,1,0:T(8,128)(2,1)S(1)}, u32[]{:S(2)}, u32[]{:S(2)}) collective-permute-start(bf16[4,128,128]{2,1,0:T(8,128)(2,1)S(1)} %get-tuple-element.155), channel_id=1, source_target_pairs={{0,4},{1,3},{2,6},{3,1},{4,0},{5,7},{6,2},{7,5},{8,12},{9,11},{10,... | collective-permute-start | bytes 393224 | tf_op jit(solution)/shard_map/ppermute | solution.py:68
  77.5 5.0 %collective-permute-start.36 = (bf16[4,128,128]{2,1,0:T(8,128)(2,1)S(1)}, bf16[4,128,128]{2,1,0:T(8,128)(2,1)S(1)}, u32[]{:S(2)}, u32[]{:S(2)}) collective-permute-start(bf16[4,128,128]{2,1,0:T(8,128)(2,1)S(1)} %get-tuple-element.161), channel_id=1, source_target_pairs={{0,4},{1,3},{2,6},{3,1},{4,0},{5,7},{6,2},{7,5},{8,12},{9,11},{10,... | collective-permute-start | bytes 393224 | tf_op jit(solution)/shard_map/ppermute | solution.py:68
  83.6 6.6 %collective-permute-start.41 = (bf16[4,128,128]{2,1,0:T(8,128)(2,1)S(1)}, bf16[4,128,128]{2,1,0:T(8,128)(2,1)S(1)}, u32[]{:S(2)}, u32[]{:S(2)}) collective-permute-start(bf16[4,128,128]{2,1,0:T(8,128)(2,1)S(1)} %get-tuple-element.170), channel_id=1, source_target_pairs={{0,4},{1,3},{2,6},{3,1},{4,0},{5,7},{6,2},{7,5},{8,12},{9,11},{10,... | collective-permute-start | bytes 393224 | tf_op jit(solution)/shard_map/ppermute | solution.py:68
  85.2 6.0 %collective-permute-start.42 = (bf16[128,512]{1,0:T(8,128)(2,1)S(1)}, bf16[128,512]{1,0:T(8,128)(2,1)S(1)}, u32[]{:S(2)}, u32[]{:S(2)}) collective-permute-start(bf16[128,512]{1,0:T(8,128)(2,1)S(1)} %get-tuple-element.171), channel_id=1, source_target_pairs={{0,8},{1,9},{2,10},{3,11},{4,12},{5,13},{6,14},{7,15},{8,0},{9,1},... | collective-permute-start | bytes 393224 | tf_op jit(solution)/shard_map/ppermute | solution.py:68
  88.5 16.5 %collective-permute-start.45 = (f32[2,2,32,512]{3,2,1,0:T(8,128)S(1)}, f32[2,2,32,512]{3,2,1,0:T(8,128)S(1)}, u32[]{:S(2)}, u32[]{:S(2)}) collective-permute-start(f32[2,2,32,512]{3,2,1,0:T(8,128)S(1)} %get-tuple-element.176), channel_id=1, source_target_pairs={{0,6},{1,7},{2,4},{3,5},{4,2},{5,3},{6,0},{7,1},{8,14},{9,15},{10,... | collective-permute-start | bytes 786440 | tf_op jit(solution)/shard_map/ppermute | solution.py:68
  90.3 14.8 %collective-permute-start.46 = (f32[2,2,32,512]{3,2,1,0:T(8,128)S(1)}, f32[2,2,32,512]{3,2,1,0:T(8,128)S(1)}, u32[]{:S(2)}, u32[]{:S(2)}) collective-permute-start(f32[2,2,32,512]{3,2,1,0:T(8,128)S(1)} %get-tuple-element.177), channel_id=1, source_target_pairs={{0,4},{1,5},{2,6},{3,7},{4,0},{5,1},{6,2},{7,3},{8,12},{9,13},{10,... | collective-permute-start | bytes 786440 | tf_op jit(solution)/shard_map/ppermute | solution.py:68
  91.2 13.8 %collective-permute-start.47 = (f32[2,2,32,512]{3,2,1,0:T(8,128)S(1)}, f32[2,2,32,512]{3,2,1,0:T(8,128)S(1)}, u32[]{:S(2)}, u32[]{:S(2)}) collective-permute-start(f32[2,2,32,512]{3,2,1,0:T(8,128)S(1)} %get-tuple-element.179), channel_id=1, source_target_pairs={{0,2},{1,3},{2,0},{3,1},{4,6},{5,7},{6,4},{7,5},{8,10},{9,11},{10,... | collective-permute-start | bytes 786440 | tf_op jit(solution)/shard_map/ppermute | solution.py:68
  (24 other events, 88.1 us)
